TPU v7x, 32 devices: a whole 2x2x4 slice. The times are simulated.
32 devices in a mesh: bucket: 4 (over x, core), ctx: 8 (over z, y).
Axes of the slice: x: 2, y: 2, z: 4, core: 2. Of those that a mesh axis runs over, the one named last changes fastest.
Arguments:
- hidden_in: bfloat16 [4, 1, 1024, 1024], P('bucket', None, 'ctx'), may hold values from -6 to 6
- lengths: int32 [4, 1, 8], P('bucket'), may hold values from 0 to 1024, as said below
- w_query: bfloat16 [1024, 1024], P(('bucket', 'ctx')), may hold values from -0.1875 to 0.1875
- w_key: bfloat16 [1024, 1024], P(('bucket', 'ctx')), may hold values from -0.1875 to 0.1875
- w_value: bfloat16 [1024, 1024], P(('bucket', 'ctx')), may hold values from -0.1875 to 0.1875
- b_query: bfloat16 [1024], P(('bucket', 'ctx')), may hold values from -3 to 3
- b_value: bfloat16 [1024], P(('bucket', 'ctx')), may hold values from -0.119628906 to 0.119628906
- w_out: bfloat16 [1024, 1024], P(('bucket', 'ctx')), may hold values from -2 to 2
- b_out: bfloat16 [1024], P(('bucket', 'ctx')), may hold values from -3 to 3
- first_gain: bfloat16 [1024], P(('bucket', 'ctx')), may hold values from 0.5 to 1.5
- first_shift: bfloat16 [1024], P(('bucket', 'ctx')), may hold values from -3 to 3
- w_up: bfloat16 [1024, 4096], P(('bucket', 'ctx')), may hold values from -0.1875 to 0.1875
- b_up: bfloat16 [4096], P(('bucket', 'ctx')), may hold values from -3 to 3
- w_down: bfloat16 [4096, 1024], P(('bucket', 'ctx')), may hold values from -0.09375 to 0.09375
- b_down: bfloat16 [1024], P(('bucket', 'ctx')), may hold values from -3 to 3
- second_gain: bfloat16 [1024], P(('bucket', 'ctx')), may hold values from 0.5 to 1.5
- second_shift: bfloat16 [1024], P(('bucket', 'ctx')), may hold values from -3 to 3
- cotangent: bfloat16 [4, 1, 1024, 1024], P('bucket', None, 'ctx'), may hold values from -6 to 6
Outputs:
- hidden_out: bfloat16 [4, 1, 1024, 1024], P('bucket', None, 'ctx')
- grad_in: float32 [4, 1, 1024, 1024], P('bucket', None, 'ctx')
- grad_w_query: float32 [1024, 1024], P(('bucket', 'ctx'))
- grad_w_key: float32 [1024, 1024], P(('bucket', 'ctx'))
- grad_w_value: float32 [1024, 1024], P(('bucket', 'ctx'))
- grad_b_query: float32 [1024], P(('bucket', 'ctx'))
- grad_b_value: float32 [1024], P(('bucket', 'ctx'))
- grad_w_out: float32 [1024, 1024], P(('bucket', 'ctx'))
- grad_b_out: float32 [1024], P(('bucket', 'ctx'))
- grad_first_gain: float32 [1024], P(('bucket', 'ctx'))
- grad_first_shift: float32 [1024], P(('bucket', 'ctx'))
- grad_w_up: float32 [1024, 4096], P(('bucket', 'ctx'))
- grad_b_up: float32 [4096], P(('bucket', 'ctx'))
- grad_w_down: float32 [4096, 1024], P(('bucket', 'ctx'))
- grad_b_down: float32 [1024], P(('bucket', 'ctx'))
- grad_second_gain: float32 [1024], P(('bucket', 'ctx'))
- grad_second_shift: float32 [1024], P(('bucket', 'ctx'))
Inputs may be any that keep to these rules, and one draw needn't show every extreme that they name: `lengths`: in length group b (counting from 0) with slot = 1024 // (8 >> b), entries 0 to (8 >> b) - 1 of each pack lie from slot - slot // 4 to slot, and one of them in each pack is exactly slot; the later entries are 0. The single sequence of the last group fills all 1024 slots.
All inputs are finite; a program needn't handle non-finite values.
Results may differ from a plain program's by a relative error of at most 0.018.
Values may be sent and summed in bfloat16 or wider, within the bound.
A program may use at most 192 MiB of HBM per device.

v0:
```python
import math

import jax
import jax.numpy as jnp
from jax import lax
from jax.sharding import PartitionSpec as P

HEAD_DIM = 64


EPSILON = 1e-05
NEG_FILL = -1e30


def matmul(left, right):
    return jnp.dot(left, right, preferred_element_type=jnp.float32)


def row_inner(left, right):
    return lax.dot_general(
        left, right, (((0,), (0,)), ((), ())), preferred_element_type=jnp.float32
    )


def right_inner(left, right):
    return lax.dot_general(
        left, right, (((1,), (1,)), ((), ())), preferred_element_type=jnp.float32
    )


def rounded(values):
    return values.astype(jnp.bfloat16)


def widened(values):
    return values.astype(jnp.float32)


def norm_forward(summed, gain_vec, shift_vec):
    average = jnp.mean(summed, axis=-1, keepdims=True)
    centred = summed - average
    variance = jnp.mean(centred * centred, axis=-1, keepdims=True)
    inv_std = lax.rsqrt(variance + EPSILON)
    normed = centred * inv_std
    return (normed * gain_vec + shift_vec, normed, inv_std)


def norm_backward(incoming, normed, inv_std, gain_vec):
    scaled = incoming * gain_vec
    inner = (
        scaled
        - jnp.mean(scaled, axis=-1, keepdims=True)
        - normed * jnp.mean(scaled * normed, axis=-1, keepdims=True)
    )
    return (inv_std * inner, jnp.sum(incoming * normed, axis=0), jnp.sum(incoming, axis=0))


def gelu_value(values):
    return 0.5 * values * (1.0 + jax.scipy.special.erf(values * 0.7071067811865476))


def gelu_slope(values):
    return (
        0.5 * (1.0 + jax.scipy.special.erf(values * 0.7071067811865476))
        + values * jnp.exp(-0.5 * values * values) * 0.3989422804014327
    )


def split_heads(values):
    return values.reshape(values.shape[0], values.shape[1], values.shape[2] // HEAD_DIM, HEAD_DIM)


def seq_mask(seq_info, query_pos, key_pos):
    seq_lens, slot_len = seq_info
    query_seq = query_pos // slot_len
    key_seq = key_pos // slot_len
    seq_ids = jnp.arange(seq_lens.shape[1], dtype=jnp.int32)
    picked = (key_seq[:, None] == seq_ids[None, :]).astype(jnp.int32)
    key_limit = jnp.sum(picked[None, :, :] * seq_lens[:, None, :], axis=-1)
    key_valid = (key_pos - key_seq * slot_len)[None, :] < key_limit
    same_seq = query_seq[:, None] == key_seq[None, :]
    return (same_seq[None, :, :] & key_valid[:, None, :])[:, None, :, :]


def score_block(query4, key4, query_start, key_start, seq_info):
    raw = jnp.einsum(
        "sqhd,skhd->shqk", query4, key4, preferred_element_type=jnp.float32
    ) * HEAD_DIM ** (-0.5)
    query_pos = query_start + jnp.arange(query4.shape[1], dtype=jnp.int32)
    key_pos = key_start + jnp.arange(key4.shape[1], dtype=jnp.int32)
    allowed = seq_mask(seq_info, query_pos, key_pos)
    return (jnp.where(allowed, raw, NEG_FILL), allowed)


def over_blocks(block_step, running, pieces):
    length_here = pieces[0].shape[1]
    block_len = math.gcd(length_here, 512)
    turn_count = length_here // block_len

    def advance(turn_no, current):
        offset = turn_no * block_len
        sliced = tuple(
            (lax.dynamic_slice_in_dim(piece_arr, offset, block_len, 1) for piece_arr in pieces)
        )
        return block_step(current, sliced, offset)

    return lax.fori_loop(0, turn_count, advance, running)


def body(
    hidden_in,
    lengths,
    w_query,
    w_key,
    w_value,
    b_query,
    b_value,
    w_out,
    b_out,
    first_gain,
    first_shift,
    w_up,
    b_up,
    w_down,
    b_down,
    second_gain,
    second_shift,
    cotangent,
):
    shards = (
        w_query,
        w_key,
        w_value,
        b_query,
        b_value,
        w_out,
        b_out,
        first_gain,
        first_shift,
        w_up,
        b_up,
        w_down,
        b_down,
        second_gain,
        second_shift,
    )
    gathered = (
        lax.all_gather(shards[0], ("bucket", "ctx"), axis=0, tiled=True),
        lax.all_gather(shards[1], ("bucket", "ctx"), axis=0, tiled=True),
        lax.all_gather(shards[2], ("bucket", "ctx"), axis=0, tiled=True),
        lax.all_gather(shards[3], ("bucket", "ctx"), axis=0, tiled=True),
        lax.all_gather(shards[4], ("bucket", "ctx"), axis=0, tiled=True),
        lax.all_gather(shards[5], ("bucket", "ctx"), axis=0, tiled=True),
        lax.all_gather(shards[6], ("bucket", "ctx"), axis=0, tiled=True),
        lax.all_gather(shards[7], ("bucket", "ctx"), axis=0, tiled=True),
        lax.all_gather(shards[8], ("bucket", "ctx"), axis=0, tiled=True),
        lax.all_gather(shards[9], ("bucket", "ctx"), axis=0, tiled=True),
        lax.all_gather(shards[10], ("bucket", "ctx"), axis=0, tiled=True),
        lax.all_gather(shards[11], ("bucket", "ctx"), axis=0, tiled=True),
        lax.all_gather(shards[12], ("bucket", "ctx"), axis=0, tiled=True),
        lax.all_gather(shards[13], ("bucket", "ctx"), axis=0, tiled=True),
        lax.all_gather(shards[14], ("bucket", "ctx"), axis=0, tiled=True),
    )
    (
        query_mat,
        key_mat,
        value_mat,
        query_bias,
        value_bias,
        out_mat,
        out_bias,
        gain_one,
        shift_one,
        up_mat,
        up_bias,
        down_mat,
        down_bias,
        gain_two,
        shift_two,
    ) = gathered
    seq_count = hidden_in.shape[1]
    local_rows = hidden_in.shape[2]
    model_width = hidden_in.shape[3]
    head_count = model_width // HEAD_DIM
    total_rows = seq_count * local_rows
    block_shape = (seq_count, local_rows, model_width)
    score_scale = HEAD_DIM ** (-0.5)
    seq_total = local_rows * lax.axis_size("ctx")
    group_index = lax.axis_index("bucket")
    seq_slots = jnp.right_shift(jnp.int32(lengths.shape[2]), group_index)
    slot_len = jnp.int32(seq_total) // seq_slots
    seq_info = (lengths[0], slot_len)
    own_start = lax.axis_index("ctx") * local_rows
    tokens = hidden_in.reshape(total_rows, model_width)
    query_low = rounded(matmul(tokens, query_mat) + widened(query_bias))
    key_low = rounded(matmul(tokens, key_mat))
    value_low = rounded(matmul(tokens, value_mat) + widened(value_bias))
    query_heads = split_heads(query_low.reshape(block_shape))
    key_rows = key_low.reshape(block_shape)
    value_rows = value_low.reshape(block_shape)

    def stats_step(running, sliced, anchor):
        scores, allowed = score_block(
            query_heads, split_heads(sliced[0]), own_start, anchor, seq_info
        )
        run_max, run_total = running
        new_max = jnp.maximum(run_max, jnp.max(scores, axis=-1))
        raised = jnp.where(allowed, jnp.exp(scores - new_max[..., None]), 0.0)
        return (new_max, run_total * jnp.exp(run_max - new_max) + jnp.sum(raised, axis=-1))

    stat_shape = (seq_count, head_count, local_rows)
    stats_start = (jnp.full(stat_shape, NEG_FILL, jnp.float32), jnp.zeros(stat_shape, jnp.float32))
    run_max, run_total = over_blocks(
        stats_step, stats_start, (lax.all_gather(key_rows, "ctx", axis=1, tiled=True),)
    )
    log_total = run_max + jnp.log(run_total)

    def output_step(running, sliced, anchor):
        key4 = split_heads(sliced[0])
        value4 = split_heads(sliced[1])
        scores, allowed = score_block(query_heads, key4, own_start, anchor, seq_info)
        probs_low = rounded(jnp.where(allowed, jnp.exp(scores - log_total[..., None]), 0.0))
        return running + jnp.einsum(
            "shqk,skhd->sqhd", probs_low, value4, preferred_element_type=jnp.float32
        )

    attended_f32 = over_blocks(
        output_step,
        jnp.zeros(query_heads.shape, jnp.float32),
        (
            lax.all_gather(key_rows, "ctx", axis=1, tiled=True),
            lax.all_gather(value_rows, "ctx", axis=1, tiled=True),
        ),
    )
    attended_low = rounded(attended_f32.reshape(total_rows, model_width))
    branch = matmul(attended_low, out_mat) + widened(out_bias)
    middle, normed_one, inv_one = norm_forward(
        widened(tokens) + branch, widened(gain_one), widened(shift_one)
    )
    middle_low = rounded(middle)
    pre_act = matmul(middle_low, up_mat) + widened(up_bias)
    activated = rounded(gelu_value(pre_act))
    ffn_out = matmul(activated, down_mat) + widened(down_bias)
    result, normed_two, inv_two = norm_forward(
        middle + ffn_out, widened(gain_two), widened(shift_two)
    )
    hidden_out = rounded(result).reshape(hidden_in.shape)
    gathered = (
        lax.all_gather(shards[0], ("bucket", "ctx"), axis=0, tiled=True),
        lax.all_gather(shards[1], ("bucket", "ctx"), axis=0, tiled=True),
        lax.all_gather(shards[2], ("bucket", "ctx"), axis=0, tiled=True),
        lax.all_gather(shards[3], ("bucket", "ctx"), axis=0, tiled=True),
        lax.all_gather(shards[4], ("bucket", "ctx"), axis=0, tiled=True),
        lax.all_gather(shards[5], ("bucket", "ctx"), axis=0, tiled=True),
        lax.all_gather(shards[6], ("bucket", "ctx"), axis=0, tiled=True),
        lax.all_gather(shards[7], ("bucket", "ctx"), axis=0, tiled=True),
        lax.all_gather(shards[8], ("bucket", "ctx"), axis=0, tiled=True),
        lax.all_gather(shards[9], ("bucket", "ctx"), axis=0, tiled=True),
        lax.all_gather(shards[10], ("bucket", "ctx"), axis=0, tiled=True),
        lax.all_gather(shards[11], ("bucket", "ctx"), axis=0, tiled=True),
        lax.all_gather(shards[12], ("bucket", "ctx"), axis=0, tiled=True),
        lax.all_gather(shards[13], ("bucket", "ctx"), axis=0, tiled=True),
        lax.all_gather(shards[14], ("bucket", "ctx"), axis=0, tiled=True),
    )
    query_mat = gathered[0]
    key_mat = gathered[1]
    value_mat = gathered[2]
    out_mat = gathered[5]
    gain_one = gathered[7]
    up_mat = gathered[9]
    down_mat = gathered[11]
    gain_two = gathered[13]
    incoming = widened(cotangent.reshape(total_rows, model_width))
    grad_two_sum, grad_second_gain, grad_second_shift = norm_backward(
        incoming, normed_two, inv_two, widened(gain_two)
    )
    grad_ffn = rounded(grad_two_sum)
    grad_b_down = jnp.sum(widened(grad_ffn), axis=0)
    grad_w_down = row_inner(activated, grad_ffn)
    grad_act = widened(rounded(right_inner(grad_ffn, down_mat)))
    grad_pre = rounded(grad_act * gelu_slope(pre_act))
    grad_b_up = jnp.sum(widened(grad_pre), axis=0)
    grad_w_up = row_inner(middle_low, grad_pre)
    grad_middle = grad_two_sum + widened(rounded(right_inner(grad_pre, up_mat)))
    grad_one_sum, grad_first_gain, grad_first_shift = norm_backward(
        grad_middle, normed_one, inv_one, widened(gain_one)
    )
    grad_branch = rounded(grad_one_sum)
    grad_b_out = jnp.sum(widened(grad_branch), axis=0)
    grad_w_out = row_inner(attended_low, grad_branch)
    grad_att = rounded(right_inner(grad_branch, out_mat)).reshape(block_shape)
    grad_att_heads = split_heads(grad_att)
    delta = jnp.einsum("sqhd,sqhd->shq", widened(grad_att_heads), attended_f32)

    def grad_terms(query4, key4, value4, att4, row_log, row_delta, query_start, key_start):
        scores, allowed = score_block(query4, key4, query_start, key_start, seq_info)
        probs = jnp.where(allowed, jnp.exp(scores - row_log[..., None]), 0.0)
        slope = jnp.einsum("sqhd,skhd->shqk", att4, value4, preferred_element_type=jnp.float32)
        return (rounded(probs), rounded(probs * (slope - row_delta[..., None])))

    def query_step(running, sliced, anchor):
        key4 = split_heads(sliced[0])
        value4 = split_heads(sliced[1])
        probs_low, score_grad = grad_terms(
            query_heads, key4, value4, grad_att_heads, log_total, delta, own_start, anchor
        )
        return (
            running
            + jnp.einsum("shqk,skhd->sqhd", score_grad, key4, preferred_element_type=jnp.float32)
            * score_scale
        )

    grad_q = over_blocks(
        query_step,
        jnp.zeros(query_heads.shape, jnp.float32),
        (
            lax.all_gather(key_rows, "ctx", axis=1, tiled=True),
            lax.all_gather(value_rows, "ctx", axis=1, tiled=True),
        ),
    )
    log_all, delta_all = (
        lax.all_gather(log_total, "ctx", axis=2, tiled=True),
        lax.all_gather(delta, "ctx", axis=2, tiled=True),
    )
    own_keys = split_heads(key_rows)
    own_values = split_heads(value_rows)

    def owner_step(running, sliced, anchor):
        query4 = split_heads(sliced[0])
        att4 = split_heads(sliced[1])
        count_here = sliced[0].shape[1]
        row_log = lax.dynamic_slice_in_dim(log_all, anchor, count_here, 2)
        row_delta = lax.dynamic_slice_in_dim(delta_all, anchor, count_here, 2)
        probs_low, score_grad = grad_terms(
            query4, own_keys, own_values, att4, row_log, row_delta, anchor, own_start
        )
        grad_k, grad_v = running
        grad_k = (
            grad_k
            + jnp.einsum("shqk,sqhd->skhd", score_grad, query4, preferred_element_type=jnp.float32)
            * score_scale
        )
        grad_v = grad_v + jnp.einsum(
            "shqk,sqhd->skhd", probs_low, att4, preferred_element_type=jnp.float32
        )
        return (grad_k, grad_v)

    owner_start = (jnp.zeros(own_keys.shape, jnp.float32), jnp.zeros(own_keys.shape, jnp.float32))
    grad_k_own, grad_v_own = over_blocks(
        owner_step,
        owner_start,
        (
            lax.all_gather(query_low.reshape(block_shape), "ctx", axis=1, tiled=True),
            lax.all_gather(grad_att, "ctx", axis=1, tiled=True),
        ),
    )
    grad_q_low = rounded(grad_q.reshape(total_rows, model_width))
    grad_k_low = rounded(grad_k_own.reshape(total_rows, model_width))
    grad_v_low = rounded(grad_v_own.reshape(total_rows, model_width))
    grad_w_query = row_inner(tokens, grad_q_low)
    grad_b_query = jnp.sum(widened(grad_q_low), axis=0)
    grad_w_key = row_inner(tokens, grad_k_low)
    grad_w_value = row_inner(tokens, grad_v_low)
    grad_b_value = jnp.sum(widened(grad_v_low), axis=0)
    grad_in = (
        grad_one_sum
        + right_inner(grad_q_low, query_mat)
        + right_inner(grad_k_low, key_mat)
        + right_inner(grad_v_low, value_mat)
    )
    owned = (
        lax.psum_scatter(grad_w_query, ("bucket", "ctx"), scatter_dimension=0, tiled=True),
        lax.psum_scatter(grad_w_key, ("bucket", "ctx"), scatter_dimension=0, tiled=True),
        lax.psum_scatter(grad_w_value, ("bucket", "ctx"), scatter_dimension=0, tiled=True),
        lax.psum_scatter(grad_b_query, ("bucket", "ctx"), scatter_dimension=0, tiled=True),
        lax.psum_scatter(grad_b_value, ("bucket", "ctx"), scatter_dimension=0, tiled=True),
        lax.psum_scatter(grad_w_out, ("bucket", "ctx"), scatter_dimension=0, tiled=True),
        lax.psum_scatter(grad_b_out, ("bucket", "ctx"), scatter_dimension=0, tiled=True),
        lax.psum_scatter(grad_first_gain, ("bucket", "ctx"), scatter_dimension=0, tiled=True),
        lax.psum_scatter(grad_first_shift, ("bucket", "ctx"), scatter_dimension=0, tiled=True),
        lax.psum_scatter(grad_w_up, ("bucket", "ctx"), scatter_dimension=0, tiled=True),
        lax.psum_scatter(grad_b_up, ("bucket", "ctx"), scatter_dimension=0, tiled=True),
        lax.psum_scatter(grad_w_down, ("bucket", "ctx"), scatter_dimension=0, tiled=True),
        lax.psum_scatter(grad_b_down, ("bucket", "ctx"), scatter_dimension=0, tiled=True),
        lax.psum_scatter(grad_second_gain, ("bucket", "ctx"), scatter_dimension=0, tiled=True),
        lax.psum_scatter(grad_second_shift, ("bucket", "ctx"), scatter_dimension=0, tiled=True),
    )
    return (hidden_out, grad_in.reshape(hidden_in.shape)) + tuple(owned)


def solution(mesh):
    placed = (
        P("bucket", None, "ctx", None),
        P("bucket", None, None),
        P(("bucket", "ctx"), None),
        P(("bucket", "ctx"), None),
        P(("bucket", "ctx"), None),
        P(("bucket", "ctx")),
        P(("bucket", "ctx")),
        P(("bucket", "ctx"), None),
        P(("bucket", "ctx")),
        P(("bucket", "ctx")),
        P(("bucket", "ctx")),
        P(("bucket", "ctx"), None),
        P(("bucket", "ctx")),
        P(("bucket", "ctx"), None),
        P(("bucket", "ctx")),
        P(("bucket", "ctx")),
        P(("bucket", "ctx")),
        P("bucket", None, "ctx", None),
    )
    return jax.shard_map(
        body,
        mesh=mesh,
        in_specs=placed,
        out_specs=(
            P("bucket", None, "ctx", None),
            P("bucket", None, "ctx", None),
            P(("bucket", "ctx"), None),
            P(("bucket", "ctx"), None),
            P(("bucket", "ctx"), None),
            P(("bucket", "ctx")),
            P(("bucket", "ctx")),
            P(("bucket", "ctx"), None),
            P(("bucket", "ctx")),
            P(("bucket", "ctx")),
            P(("bucket", "ctx")),
            P(("bucket", "ctx"), None),
            P(("bucket", "ctx")),
            P(("bucket", "ctx"), None),
            P(("bucket", "ctx")),
            P(("bucket", "ctx")),
            P(("bucket", "ctx")),
        ),
        check_vma=False,
    )
```

profile of v0, /device:TPU:0, one launch (start us, length us, event | category | flops | bytes accessed | tf_op | source)
XLA Modules:
  0.0 1908.4 jit_solution(7328134293722810519)
XLA Ops:
  16.2 42.3 %all-reduce.18 = (bf16[1024]{0:T(1024)(128)(2,1)S(1)}, bf16[1024]{0:T(1024)(128)(2,1)S(1)}, bf16[1024]{0:T(1024)(128)(2,1)S(1)}, bf16[1024]{0:T(1024)(128)(2,1)S...) all-reduce(bf16[1024]{0:T(1024)(128)(2,1)S(1)} %dynamic-update-slic, ...), channel_id=1, replica_groups=mesh['bucket'=4,'ctx'=8] {'bucket','ctx'}, use_global_device_ids=true, to_apply=%add | all-reduce | flops 8192 | bytes 32768
  58.5 11.8 all-gather.17.cloned.1.call-done
  70.3 2.9 fusion.70
  73.2 55.6 %all-gather.19.cloned.1.call-done = bf16[1024,1024]{1,0:T(8,128)(2,1)} async-done(((bf16[32,1024]{1,0:T(8,128)(2,1)}), bf16[1024,1024]{1,0:T(8,128)(2,1)}) %all-gather.19.cloned.1.call-update) | async-done | bytes 2097168 | tf_op jit(solution)/shard_map/all_gather | solution.py:149
  128.9 2.9 convolution_convert_fusion.3
  134.0 65.9 %all-gather.5 = bf16[32,1,128]{2,1,0:T(2,128)(2,1)S(1)} all-gather(bf16[1,1,128]{2,1,0:T(2,128)(2,1)S(1)} %bitcast.355), channel_id=1, replica_groups=mesh['bucket'=4,'ctx'=8] {'bucket','ctx'}, dimensions={0}, use_global_device_ids=true | all-gather | bytes 8448 | tf_op jit(solution)/shard_map/all_gather | solution.py:158
  200.0 2.0 fusion.71
  203.3 34.1 %all-gather.29.cloned.1.call-done = bf16[1024,1024]{1,0:T(8,128)(2,1)} async-done(((bf16[128,1024]{1,0:T(8,128)(2,1)}), bf16[1024,1024]{1,0:T(8,128)(2,1)}) %all-gather.29.cloned.1.call-update) | async-done | bytes 2097168 | tf_op jit(solution)/shard_map/all_gather | solution.py:232
  237.4 4.0 copy.85
  241.4 45.8 %all-gather.31.cloned.1.call-done = bf16[1024,1024]{1,0:T(8,128)(2,1)} async-done(((bf16[128,1024]{1,0:T(8,128)(2,1)}), bf16[1024,1024]{1,0:T(8,128)(2,1)}) %all-gather.31.cloned.1.call-update) | async-done | bytes 2097168 | tf_op jit(solution)/shard_map/all_gather | solution.py:231
  287.2 2.9 copy.86
  290.1 13.9 while.72
  290.9 2.9 fusion.158
  293.8 3.2 select_reduce_fusion.11
  297.8 2.9 fusion.158
  300.8 3.2 select_reduce_fusion.11
  304.0 13.8 while.73
  304.0 2.4 constant_dynamic-slice_fusion.12
  307.1 3.7 fusion.162
  310.8 2.4 constant_dynamic-slice_fusion.12
  313.9 3.9 fusion.162
  318.8 26.2 %all-gather.23.cloned.1.call-done = bf16[1024,1024]{1,0:T(8,128)(2,1)} async-done(((bf16[32,1024]{1,0:T(8,128)(2,1)}), bf16[1024,1024]{1,0:T(8,128)(2,1)}) %all-gather.23.cloned.1.call-update) | async-done | bytes 2097168 | tf_op jit(solution)/shard_map/all_gather | solution.py:153
  345.1 2.1 fusion.100
  347.5 76.9 %all-gather.25.cloned.1.call-done = bf16[1024,4096]{1,0:T(8,128)(2,1)} async-done(((bf16[32,4096]{1,0:T(8,128)(2,1)}), bf16[1024,4096]{1,0:T(8,128)(2,1)}) %all-gather.25.cloned.1.call-update) | async-done | bytes 8388624 | tf_op jit(solution)/shard_map/all_gather | solution.py:157
  424.4 6.0 convolution_add_fusion
  430.4 73.0 %all-gather.27.cloned.1.call-done = bf16[4096,1024]{1,0:T(8,128)(2,1)} async-done(((bf16[128,1024]{1,0:T(8,128)(2,1)}), bf16[4096,1024]{1,0:T(8,128)(2,1)}) %all-gather.27.cloned.1.call-update) | async-done | bytes 8388624 | tf_op jit(solution)/shard_map/all_gather | solution.py:159
  503.4 5.7 fusion.101
  511.6 3.9 convert_reduce_fusion
  515.5 3.6 multiply_reduce_fusion
  522.9 22.8 %while.74 = (s32[]{:T(128)}, f32[1,128,16,64]{1,3,2,0:T(8,128)}, bf16[1,1024,1024]{1,2,0:T(8,128)(2,1)S(1)}, s32[]{:T(128)}, s32[]{:T(128)}, /*index=5*/s32[]{:T...) while((s32[]{:T(128)}, f32[1,128,16,64]{1,3,2,0:T(8,128)}, ...), condition=%wide.region_18.19_spmd.clone, body=%wide.region_16.18_spmd.clone.sunk | while | flops 410541184 | bytes 17461532 | solution.py:107
  522.9 2.4 constant_dynamic-slice_fusion.13
  525.3 2.7 fusion.168
  528.7 5.6 fusion.169
  534.3 2.4 constant_dynamic-slice_fusion.13
  536.8 2.7 fusion.168
  540.2 5.5 fusion.169
  545.7 1.8 convert_reduce_fusion.5
  548.2 3.6 convolution_bitcast_fusion.2
  551.8 5.4 copy.108
  558.3 2.7 fusion.90
  562.7 30.8 %all_gather.92 = f32[1,16,1024]{2,1,0:T(8,128)S(1)} all-gather(f32[1,16,128]{2,1,0:T(8,128)S(1)} %get-tuple-element.2193), channel_id=1, replica_groups=mesh['bucket'=4,'ctx'=8] {'ctx'}, dimensions={2}, use_global_device_ids=true | all-gather | bytes 73728 | tf_op jit(solution)/shard_map/all_gather | solution.py:322
  593.5 30.6 %all-gather.4 = f32[16,1024]{1,0:T(8,128)S(1)} all-gather(f32[16,128]{1,0:T(8,128)S(1)} %bitcast.352), channel_id=6, replica_groups=mesh['bucket'=4,'ctx'=8] {'ctx'}, dimensions={1}, use_global_device_ids=true | all-gather | bytes 73728 | tf_op jit(solution)/shard_map/all_gather | solution.py:323
  624.1 35.1 %while.75 = (s32[]{:T(128)}, f32[1,128,16,64]{1,3,2,0:T(8,128)}, f32[1,128,16,64]{1,3,2,0:T(8,128)}, bf16[1,1024,1024]{2,1,0:T(8,128)(2,1)}, s32[]{:T(128)}, /*i...) while((s32[]{:T(128)}, f32[1,128,16,64]{1,3,2,0:T(8,128)}, ...), condition=%wide.region_21.22_spmd.clone, body=%wide.region_19.21_spmd.clone.sunk | while | flops 550250496 | bytes 32414816 | solution.py:107
  624.3 1.7 constant_dynamic-slice_fusion.14
  626.6 3.7 fusion.177
  631.5 6.2 fusion.178
  637.7 3.2 fusion.179
  644.0 3.7 fusion.177
  648.9 6.3 fusion.178
  655.2 3.2 fusion.179
  661.0 2.6 convolution_bitcast_fusion.1
  663.6 5.4 copy.110
  671.0 2.6 convolution_bitcast_fusion
  673.6 5.4 copy.112
  680.4 8.2 fusion.96
  690.2 8.1 fusion.93
  699.6 3.2 convolution_add_fusion.3
  702.9 40.6 %all-reduce.17 = (f32[1024]{0:T(1024)S(1)}, f32[1024]{0:T(1024)S(1)}, f32[1024]{0:T(1024)S(1)}, f32[1024]{0:T(1024)S(1)}, f32[1024]{0:T(1024)S(1)}, /*index=5*/f...) all-reduce(f32[1024]{0:T(1024)S(1)} %reduce_sum.223, ...), channel_id=10, replica_groups=mesh['bucket'=4,'ctx'=8] {'bucket','ctx'}, use_global_device_ids=true, to_apply=%region_26.27.clone | all-reduce | flops 12288 | bytes 98304
  748.7 2.5 convolution_add_fusion.2
  752.9 141.6 %reduce-scatter.13.cloned.1.call-done = f32[32,1024]{1,0:T(8,128)} async-done(((f32[1024,1024]{1,0:T(8,128)}), f32[32,1024]{1,0:T(8,128)}) %reduce-scatter.13.cloned.1.call-update) | async-done | bytes 131088 | tf_op jit(solution)/shard_map/reduce_scatter | solution.py:377
  894.5 144.5 %reduce-scatter.21.cloned.1.call-done = f32[32,1024]{1,0:T(8,128)} async-done(((f32[1024,1024]{1,0:T(8,128)}), f32[32,1024]{1,0:T(8,128)}) %reduce-scatter.21.cloned.1.call-update) | async-done | bytes 131088
  1039.0 144.3 %reduce-scatter.23.cloned.1.call-done = f32[32,1024]{1,0:T(8,128)} async-done(((f32[1024,1024]{1,0:T(8,128)}), f32[32,1024]{1,0:T(8,128)}) %reduce-scatter.23.cloned.1.call-update) | async-done | bytes 131088
  1183.2 358.3 %reduce-scatter.15.cloned.1.call-done = f32[32,4096]{1,0:T(8,128)} async-done(((f32[1024,4096]{1,0:T(8,128)}), f32[32,4096]{1,0:T(8,128)}) %reduce-scatter.15.cloned.1.call-update) | async-done | bytes 524304 | tf_op jit(solution)/shard_map/reduce_scatter | solution.py:381
  1541.5 360.1 %reduce-scatter.17.cloned.1.call-done = f32[128,1024]{1,0:T(8,128)} async-done(((f32[4096,1024]{1,0:T(8,128)}), f32[128,1024]{1,0:T(8,128)}) %reduce-scatter.17.cloned.1.call-update) | async-done | bytes 524304 | tf_op jit(solution)/shard_map/reduce_scatter | solution.py:383
  (258 shorter events, 49.4 us)
Async XLA Ops:
  7.2 192.8 %copy-start.5 = (bf16[1,1,128,1024]{3,2,1,0:T(8,128)(2,1)S(1)}, bf16[1,1,128,1024]{3,2,1,0:T(8,128)(2,1)}, u32[]{:S(2)}) copy-start(bf16[1,1,128,1024]{3,2,1,0:T(8,128)(2,1)} %param.26) | copy-start | bytes 786436
  7.2 126.8 %copy-start.45 = (bf16[128]{0:T(256)(128)(2,1)S(1)}, bf16[128]{0:T(256)(128)(2,1)}, u32[]{:S(2)}) copy-start(bf16[128]{0:T(256)(128)(2,1)} %param.38) | copy-start | bytes 772
  7.2 63.1 %all-gather.17.cloned.1.call-start = ((), (), s32[]{:S(2)}) async-start(), calls=%async_computation.6 | async-start | bytes 2162688 | tf_op jit(solution)/shard_map/all_gather | solution.py:150
  7.9 120.9 %all-gather.19.cloned.1.call-start = ((), (), s32[]{:S(2)}) async-start(), calls=%async_computation.7 | async-start | bytes 2162688 | tf_op jit(solution)/shard_map/all_gather | solution.py:149
  8.7 191.3 %all-gather.21.cloned.1.call-start = ((), (), s32[]{:S(2)}) async-start(), calls=%async_computation.8 | async-start | bytes 2162688 | tf_op jit(solution)/shard_map/all_gather | solution.py:148
  9.4 228.0 %all-gather.29.cloned.1.call-start = ((), (), s32[]{:S(2)}) async-start(), calls=%async_computation.15 | async-start | bytes 2359296 | tf_op jit(solution)/shard_map/all_gather | solution.py:232
  73.2 214.0 %all-gather.31.cloned.1.call-start = ((), (), s32[]{:S(2)}) async-start(), calls=%async_computation.16 | async-start | bytes 2359296 | tf_op jit(solution)/shard_map/all_gather | solution.py:231
  131.8 213.3 %all-gather.23.cloned.1.call-start = ((), (), s32[]{:S(2)}) async-start(), calls=%async_computation.9 | async-start | bytes 2162688 | tf_op jit(solution)/shard_map/all_gather | solution.py:153
  132.3 292.0 %all-gather.25.cloned.1.call-start = ((), (), s32[]{:S(2)}) async-start(), calls=%async_computation.10 | async-start | bytes 8650752 | tf_op jit(solution)/shard_map/all_gather | solution.py:157
  133.1 370.3 %all-gather.27.cloned.1.call-start = ((), (), s32[]{:S(2)}) async-start(), calls=%async_computation.11 | async-start | bytes 8650752 | tf_op jit(solution)/shard_map/all_gather | solution.py:159
  133.8 490.3 %all-gather.33.cloned.1.call-start = ((), (), s32[]{:S(2)}) async-start(), calls=%async_computation.17 | async-start | bytes 2359296 | tf_op jit(solution)/shard_map/all_gather | solution.py:353
  202.8 421.4 %all-gather.35.cloned.1.call-start = ((), (), s32[]{:S(2)}) async-start(), calls=%async_computation.18 | async-start | bytes 2359296 | tf_op jit(solution)/shard_map/all_gather | solution.py:354
  237.4 52.6 %copy-start.33 = (s32[1,1,8]{2,1,0:T(1,128)S(1)}, s32[1,1,8]{2,1,0:T(1,128)}, u32[]{:S(2)}) copy-start(s32[1,1,8]{2,1,0:T(1,128)} %param.27) | copy-start | bytes 100
  318.8 111.6 %copy-start.23 = (bf16[1,128,16,64]{1,3,2,0:T(8,128)(2,1)}, bf16[1,128,16,64]{1,3,2,0:T(8,128)(2,1)S(1)}, u32[]{:S(2)}) copy-start(bf16[1,128,16,64]{1,3,2,0:T(8,128)(2,1)S(1)} %convert_element_type.197) | copy-start | bytes 786436
  347.2 171.9 %copy-start.3 = (f32[128,1024]{1,0:T(8,128)}, f32[128,1024]{1,0:T(8,128)S(1)}, u32[]{:S(2)}) copy-start(f32[128,1024]{1,0:T(8,128)S(1)} %get-tuple-element.1649) | copy-start | bytes 1572868
  347.5 171.7 %copy-start.37 = (f32[128]{0:T(128)}, f32[128]{0:T(128)S(1)}, u32[]{:S(2)}) copy-start(f32[128]{0:T(128)S(1)} %add_rsqrt_fusion.1) | copy-start | bytes 1540
  503.4 5.9 copy-start.16
  503.4 8.3 copy-start
  503.4 8.3 copy-start.2
  510.1 5.4 slice-start
  511.6 3.9 copy-start.12
  511.6 3.9 slice-start.1
  515.5 3.6 copy-start.14
  515.5 4.4 copy-start.8
  519.9 3.0 copy-start.9
  520.8 2.0 copy-start.29
  522.8 230.1 %reduce-scatter.19.cloned.1.call-start = ((), (), s32[]{:S(2)}) async-start(), calls=%async_computation.19 | async-start | bytes 4325376
  545.7 11.5 copy-start.34
  547.5 0.7 copy-start.21
  557.2 1.0 copy-start.10
  557.2 1.1 copy-start.24
  557.2 3.9 copy-start.19
  557.2 4.7 copy-start.18
  557.2 36.3 %copy-start.35 = (f32[1,16,128]{2,1,0:T(8,128)S(1)}, f32[1,16,128]{2,1,0:T(8,128)}, u32[]{:S(2)}) copy-start(f32[1,16,128]{2,1,0:T(8,128)} %copy-done.34) | copy-start | bytes 24580
  557.2 337.2 %reduce-scatter.13.cloned.1.call-start = ((), (), s32[]{:S(2)}) async-start(), calls=%async_computation.12 | async-start | bytes 4325376 | tf_op jit(solution)/shard_map/reduce_scatter | solution.py:377
  561.0 478.0 %reduce-scatter.21.cloned.1.call-start = ((), (), s32[]{:S(2)}) async-start(), calls=%async_computation.20 | async-start | bytes 4325376
  624.1 36.9 %copy-start.6 = (bf16[1,1,128,1024]{3,2,1,0:T(8,128)(2,1)S(1)}, bf16[1,1,128,1024]{3,2,1,0:T(8,128)(2,1)}, u32[]{:S(2)}) copy-start(bf16[1,1,128,1024]{3,2,1,0:T(8,128)(2,1)} %param.26) | copy-start | bytes 786436
  631.5 6.2 copy-start.30
  640.9 0.8 copy-start.31
  648.8 6.3 copy-start.30
  658.4 0.8 copy-start.31
  669.0 1.0 copy-start.32
  669.0 514.2 %reduce-scatter.23.cloned.1.call-start = ((), (), s32[]{:S(2)}) async-start(), calls=%async_computation.21 | async-start | bytes 4325376
  670.3 0.7 copy-start.27
  679.0 1.0 copy-start.4
  679.0 1.4 copy-start.15
  679.0 1.4 copy-start.38
  679.0 862.5 %reduce-scatter.15.cloned.1.call-start = ((), (), s32[]{:S(2)}) async-start(), calls=%async_computation.13 | async-start | bytes 17301504 | tf_op jit(solution)/shard_map/reduce_scatter | solution.py:381
  688.6 1.6 copy-start.1
  688.6 1.7 copy-start.13
  688.6 1213.1 %reduce-scatter.17.cloned.1.call-start = ((), (), s32[]{:S(2)}) async-start(), calls=%async_computation.14 | async-start | bytes 17301504 | tf_op jit(solution)/shard_map/reduce_scatter | solution.py:383
  698.4 0.9 copy-start.17
  698.4 1.0 copy-start.36
  698.4 1.1 copy-start.11
  698.4 1.2 copy-start.22
  698.4 4.5 copy-start.39
  698.4 4.5 copy-start.40
  698.4 4.5 copy-start.41
  698.4 4.5 copy-start.42
  698.4 4.5 copy-start.43
  698.4 4.5 copy-start.44
  698.4 50.3 %copy-start.26 = (bf16[1,128,16,64]{1,3,2,0:T(8,128)(2,1)S(1)}, bf16[1,128,16,64]{1,3,2,0:T(8,128)(2,1)}, u32[]{:S(2)}) copy-start(bf16[1,128,16,64]{1,3,2,0:T(8,128)(2,1)} %copy-done.25) | copy-start | bytes 786436
  698.5 52.8 %copy-start.7 = (bf16[1024,1024]{1,0:T(8,128)(2,1)S(1)}, bf16[1024,1024]{1,0:T(8,128)(2,1)}, u32[]{:S(2)}) copy-start(bf16[1024,1024]{1,0:T(8,128)(2,1)} %all-gather.17.cloned.1.call-done) | copy-start | bytes 6291460
  699.4 51.9 %copy-start.28 = (bf16[1,128,16,64]{1,3,2,0:T(8,128)(2,1)S(1)}, bf16[1,128,16,64]{1,3,2,0:T(8,128)(2,1)}, u32[]{:S(2)}) copy-start(bf16[1,128,16,64]{1,3,2,0:T(8,128)(2,1)} %copy-done.27) | copy-start | bytes 786436
  (2 other events, 1.4 us)
Sparse Core Ops, SparseCore 0:
  11.0 59.2 all-gather.16
  73.3 55.5 all-gather.18
  131.8 55.3 all-gather.20
  189.3 48.1 all-gather.28
  239.4 47.7 all-gather.30
  290.0 55.0 all-gather.22
  348.1 76.2 all-gather.24
  427.3 75.9 all-gather.26
  505.5 48.0 all-gather.32
  555.5 48.4 all-gather.34
  606.9 142.9 reduce-scatter.18
  752.7 141.7 reduce-scatter.12
  897.3 141.6 reduce-scatter.20
  1041.7 141.5 reduce-scatter.22
  1186.0 355.5 reduce-scatter.14
  1544.2 357.3 reduce-scatter.16
where the time goes:
time: 1910 us
  waiting for transfers between devices  1480 us (77%)
  blocking collectives  210 us (11%)
  matrix products  121 us (6%)
  local copies, waits for them, and re-layouts  63.1 us (3%)
  other arithmetic  20.7 us (1%)
    reduce_scatter x1, waiting for transfers between devices, body(): lax.psum_scatter(grad_w_down, ('bucket', 'ctx'), scatter_dimension=0, til...  360 us
    reduce_scatter x1, waiting for transfers between devices, body(): lax.psum_scatter(grad_w_up, ('bucket', 'ctx'), scatter_dimension=0, tiled...  358 us
    unnamed x19, waiting for transfers between devices  293 us
    reduce_scatter x1, waiting for transfers between devices, body(): lax.psum_scatter(grad_w_out, ('bucket', 'ctx'), scatter_dimension=0, tile...  142 us
    unnamed x2, blocking collectives  82.9 us
    all_gather x1, waiting for transfers between devices, body(): lax.all_gather(shards[9], ('bucket', 'ctx'), axis=0, tiled=True)  76.9 us
    all_gather x1, waiting for transfers between devices, body(): lax.all_gather(shards[11], ('bucket', 'ctx'), axis=0, tiled=True)  73 us
    all_gather x1, blocking collectives, body(): lax.all_gather(shards[10], ('bucket', 'ctx'), axis=0, tiled=True)  65.9 us
  transfers between devices with their start and end apart: 16, of which 12 were waited for; matrix products, arithmetic and copies ran while one was open for 10% of the time, Pallas kernels for 0%

commit v1 on v0

--- a/solution.py
+++ b/solution.py
@@ -1,15 +1,832 @@
+import functools
 import math
 
 import jax
 import jax.numpy as jnp
 from jax import lax
+from jax.experimental import pallas as pl
+from jax.experimental.pallas import tpu as pltpu
 from jax.sharding import PartitionSpec as P
 
 HEAD_DIM = 64
-
-
 EPSILON = 1e-05
 NEG_FILL = -1e30
+MESH_ID = pl.DeviceIdType.MESH
+F32, BF16 = jnp.float32, jnp.bfloat16
+ROWS = 32
+PIECES = 12
+VMEM_LIMIT = 62 * 2**20
+
+
+def when(condition):
+    return pl.when(condition)
+
+
+def place():
+    bucket, ctx = lax.axis_index("bucket"), lax.axis_index("ctx")
+    return bucket // 2, ctx % 2, ctx // 2, bucket % 2
+
+
+def device(x, y, z, core):
+    return (x * 2 + core, z * 2 + y)
+
+
+def owner(x, y, z, core):
+    return (x * 2 + core) * 8 + z * 2 + y
+
+
+def remote(src, dst, send_sem, recv_sem, target):
+    return pltpu.make_async_remote_copy(
+        src_ref=src, dst_ref=dst, send_sem=send_sem, recv_sem=recv_sem,
+        device_id=target, device_id_type=MESH_ID,
+    )
+
+
+def bytes_of(ref, sem):
+    return pltpu.make_async_copy(ref, ref, sem)
+
+
+class Route:
+    def __init__(self):
+        self.x, self.y, self.z, self.core = x, y, z, core = place()
+        self.ax, self.ay = jnp.where(core == 0, 1 - x, x), jnp.where(core == 0, y, 1 - y)
+        self.bx, self.by = jnp.where(core == 1, 1 - x, x), jnp.where(core == 1, y, 1 - y)
+        self.a = device(self.ax, self.ay, z, core)
+        self.b = device(self.bx, self.by, z, core)
+        self.sibling = device(x, y, z, 1 - core)
+        self.up = device(x, y, jnp.minimum(z + 1, 3), core)
+        self.down = device(x, y, jnp.maximum(z - 1, 0), core)
+
+    def greet(self):
+        z = self.z
+        barrier = pltpu.get_barrier_semaphore()
+        for target in (self.a, self.b, self.sibling):
+            pl.semaphore_signal(barrier, inc=1, device_id=target, device_id_type=MESH_ID)
+
+        @when(z < 3)
+        def _():
+            pl.semaphore_signal(barrier, inc=1, device_id=self.up, device_id_type=MESH_ID)
+
+        @when(z > 0)
+        def _():
+            pl.semaphore_signal(barrier, inc=1, device_id=self.down, device_id_type=MESH_ID)
+
+        pl.semaphore_wait(barrier, 3 + (z < 3).astype(jnp.int32) + (z > 0).astype(jnp.int32))
+
+
+class Gatherer:
+    stages = 7
+
+    def __init__(self, route, count, own, block, span, sems):
+        self.rt, self.count, self.own, self.block, self.span = route, count, own, block, span
+        (self.zs, self.zr, self.ps, self.ar, self.br, self.dr, self.ls) = sems
+
+    def spread(self, c, src, j, jz, to_a, to_b, z_dirs):
+        rt, dst = self.rt, self.block(c, j)
+        if "up" in z_dirs:
+
+            @when(rt.z < 3)
+            def _():
+                remote(src, dst, self.zs.at[0, c, jz], self.zr.at[c, jz], rt.up).start()
+
+        if "down" in z_dirs:
+
+            @when(rt.z > 0)
+            def _():
+                remote(src, dst, self.zs.at[1, c, jz], self.zr.at[c, jz], rt.down).start()
+
+        if to_a:
+            remote(src, dst, self.ps, self.ar.at[c, jz], rt.a).start()
+        if to_b is not None:
+            remote(src, dst, self.ps, self.br.at[c, to_b * 4 + jz], rt.b).start()
+        remote(src, dst, self.ps, self.dr.at[c], rt.sibling).start()
+
+    def near(self, k, action):
+        for sign in (0,) if k == 0 else (-1, 1):
+            zz = self.rt.z + sign * k
+
+            @when((zz >= 0) & (zz <= 3))
+            def _():
+                action(zz, "up" if sign < 0 else "down")
+
+    def own_stage(self, c):
+        rt = self.rt
+        j = owner(rt.x, rt.y, rt.z, rt.core)
+        pltpu.make_async_copy(self.own(c), self.block(c, j), self.ls).start()
+        self.spread(c, self.own(c), j, rt.z, True, 0, ("up", "down"))
+
+    def z_stage(self, c, k):
+        rt = self.rt
+
+        def action(zz, direction):
+            j = owner(rt.x, rt.y, zz, rt.core)
+            bytes_of(self.block(c, j), self.zr.at[c, zz]).wait()
+            self.spread(c, self.block(c, j), j, zz, True, 0, (direction,))
+
+        self.near(k, action)
+
+    def a_stage(self, c, k):
+        rt = self.rt
+
+        def action(zz, _):
+            j = owner(rt.ax, rt.ay, zz, rt.core)
+            bytes_of(self.block(c, j), self.ar.at[c, zz]).wait()
+            self.spread(c, self.block(c, j), j, zz, False, 1, ())
+
+        self.near(k, action)
+
+    def b_stage(self, c, k):
+        rt = self.rt
+
+        def action(zz, _):
+            for which, (xx, yy) in enumerate(((rt.bx, rt.by), (1 - rt.x, 1 - rt.y))):
+                j = owner(xx, yy, zz, rt.core)
+                bytes_of(self.block(c, j), self.br.at[c, which * 4 + zz]).wait()
+                self.spread(c, self.block(c, j), j, zz, False, None, ())
+
+        self.near(k, action)
+
+    def stage(self, s, c):
+        if s == 0:
+            self.own_stage(c)
+        if 1 <= s <= 3:
+            self.z_stage(c, s)
+        if 2 <= s <= 5:
+            self.a_stage(c, s - 2)
+        if 3 <= s <= 6:
+            self.b_stage(c, s - 3)
+
+    def arrived(self, c):
+        bytes_of(self.span(16), self.dr.at[c]).wait()
+
+    def finish(self):
+        bytes_of(self.span(28 * self.count), self.ps).wait()
+        bytes_of(self.span(self.count), self.ls).wait()
+
+    def finish_z(self, c):
+        rt = self.rt
+        for zz in range(4):
+
+            @when((rt.z < 3) & (rt.z >= zz))
+            def _():
+                bytes_of(self.span(1), self.zs.at[0, c, zz]).wait()
+
+            @when((rt.z > 0) & (rt.z <= zz))
+            def _():
+                bytes_of(self.span(1), self.zs.at[1, c, zz]).wait()
+
+
+def gather_sems(count):
+    dma = pltpu.SemaphoreType.DMA
+    return [dma((2, count, 4)), dma((count, 4)), dma(()), dma((count, 4)), dma((count, 8)), dma((count,)), dma(())]
+
+
+def piece_row(c, j):
+    return pl.multiple_of(jnp.where(c < 8, c * 1024 + ROWS * j, 8192 + 128 * j + ROWS * (c - 8)), ROWS)
+
+
+def gather_kernel(x_ref, v_ref, w_ref, t_ref, *sems):
+    rt = Route()
+    main = Gatherer(
+        rt, PIECES,
+        lambda c: x_ref.at[pl.ds(pl.multiple_of(c * ROWS, ROWS), ROWS)],
+        lambda c, j: w_ref.at[pl.ds(piece_row(c, j), ROWS)],
+        lambda n: w_ref.at[pl.ds(0, n * ROWS)],
+        sems[:7],
+    )
+    small = Gatherer(rt, 1, lambda c: v_ref, lambda c, j: t_ref.at[j], lambda n: t_ref.at[pl.ds(0, n)], sems[7:])
+    rt.greet()
+
+    def step(t, _):
+        for s in range(Gatherer.stages):
+            c = t - s
+
+            @when(c == 0)
+            def _():
+                small.stage(s, 0)
+
+            @when((c >= 0) & (c < PIECES))
+            def _():
+                main.stage(s, c)
+
+        return 0
+
+    lax.fori_loop(0, PIECES + Gatherer.stages - 1, step, 0)
+    small.arrived(0)
+    small.finish()
+    small.finish_z(0)
+
+    def last(c, _):
+        main.arrived(c)
+        main.finish_z(c)
+        return 0
+
+    lax.fori_loop(0, PIECES, last, 0)
+    main.finish()
+
+
+def gather_weights(shards, small):
+    vmem, anywhere = pl.BlockSpec(memory_space=pltpu.VMEM), pl.BlockSpec(memory_space=pl.ANY)
+    return pl.pallas_call(
+        gather_kernel,
+        out_shape=(
+            jax.ShapeDtypeStruct((PIECES * 1024, 1024), BF16),
+            jax.ShapeDtypeStruct((32, 16, 128), BF16),
+        ),
+        in_specs=[vmem, vmem],
+        out_specs=(anywhere, vmem),
+        scratch_shapes=gather_sems(PIECES) + gather_sems(1),
+        compiler_params=pltpu.CompilerParams(collective_id=0, has_side_effects=True, vmem_limit_bytes=VMEM_LIMIT),
+    )(shards, small)
+
+
+def add_f32(left, right):
+    return left.astype(F32) + right.astype(F32)
+
+
+class Reducer:
+    stages = 7
+
+    def __init__(self, route, bufs, sems):
+        self.rt = route
+        (self.own, self.sib, self.rd, self.rb, self.ra, self.ru, self.rn, self.out) = bufs
+        (self.sd_s, self.sd_r, self.sb_s, self.sb_r, self.sa_s, self.sa_r, self.sz_s, self.su_r, self.sn_r) = sems
+
+    @staticmethod
+    def slot(xx, yy, zz):
+        return xx * 8 + zz * 2 + yy
+
+    def add(self, c, k, other):
+        self.own[c, k] = add_f32(self.own[c, k], other).astype(self.own.dtype)
+
+    def to_sibling(self, c):
+        remote(self.sib.at[c], self.rd.at[c], self.sd_s.at[c], self.sd_r.at[c], self.rt.sibling).start()
+
+    def to_b(self, c):
+        rt = self.rt
+        bytes_of(self.rd.at[c], self.sd_r.at[c]).wait()
+        for same_a in (0, 1):
+            for zz in range(4):
+                xx, yy = (rt.bx, rt.by) if same_a else (1 - rt.x, 1 - rt.y)
+                k = self.slot(xx, yy, zz)
+                self.add(c, k, self.rd[c, k])
+                remote(self.own.at[c, k], self.rb.at[c, same_a * 4 + zz], self.sb_s.at[c], self.sb_r.at[c], rt.b).start()
+        for same_a in (0, 1):
+            for zz in range(4):
+                xx, yy = (rt.x, rt.y) if same_a else (rt.ax, rt.ay)
+                k = self.slot(xx, yy, zz)
+                self.add(c, k, self.rd[c, k])
+
+    def to_a(self, c):
+        rt = self.rt
+        bytes_of(self.rb.at[c], self.sb_r.at[c]).wait()
+        for zz in range(4):
+            k = self.slot(rt.ax, rt.ay, zz)
+            self.add(c, k, self.rb[c, zz])
+            remote(self.own.at[c, k], self.ra.at[c, zz], self.sa_s.at[c], self.sa_r.at[c], rt.a).start()
+        for zz in range(4):
+            self.add(c, self.slot(rt.x, rt.y, zz), self.rb[c, 4 + zz])
+
+    def from_a(self, c):
+        rt = self.rt
+        bytes_of(self.ra.at[c], self.sa_r.at[c]).wait()
+        for zz in range(4):
+            self.add(c, self.slot(rt.x, rt.y, zz), self.ra[c, zz])
+
+    def along_z(self, c, hop):
+        rt = self.rt
+        x, y = rt.x, rt.y
+
+        @when(rt.z == hop)
+        def _():
+            for d in range(3, hop, -1):
+                k = self.slot(x, y, d)
+                if hop > 0:
+                    bytes_of(self.ru.at[c, d - 1], self.su_r.at[c, d - 1]).wait()
+                    self.add(c, k, self.ru[c, d - 1])
+                remote(self.own.at[c, k], self.ru.at[c, d - 1], self.sz_s.at[c, d], self.su_r.at[c, d - 1], rt.up).start()
+            if hop > 0:
+                bytes_of(self.ru.at[c, hop - 1], self.su_r.at[c, hop - 1]).wait()
+
+        at = 3 - hop
+
+        @when(rt.z == at)
+        def _():
+            for d in range(at):
+                k = self.slot(x, y, d)
+                if at < 3:
+                    bytes_of(self.rn.at[c, d], self.sn_r.at[c, d]).wait()
+                    self.add(c, k, self.rn[c, d])
+                remote(self.own.at[c, k], self.rn.at[c, d], self.sz_s.at[c, d], self.sn_r.at[c, d], rt.down).start()
+            if at < 3:
+                bytes_of(self.rn.at[c, at], self.sn_r.at[c, at]).wait()
+
+    def total(self, c):
+        rt = self.rt
+        k = self.slot(rt.x, rt.y, rt.z)
+
+        @when(rt.z == 0)
+        def _():
+            self.out[c] = add_f32(self.own[c, k], self.rn[c, 0])
+
+        @when(rt.z == 3)
+        def _():
+            self.out[c] = add_f32(self.own[c, k], self.ru[c, 2])
+
+        for at in (1, 2):
+
+            @when(rt.z == at)
+            def _():
+                self.out[c] = add_f32(self.own[c, k], self.ru[c, at - 1]) + self.rn[c, at].astype(F32)
+
+    def stage(self, s, c):
+        if s == 0:
+            self.to_sibling(c)
+        if s == 1:
+            self.to_b(c)
+        if s == 2:
+            self.to_a(c)
+        if s == 3:
+            self.from_a(c)
+        if s >= 3:
+            self.along_z(c, s - 3)
+        if s == 6:
+            self.total(c)
+
+    def finish(self, c):
+        rt = self.rt
+        bytes_of(self.sib.at[c], self.sd_s.at[c]).wait()
+        bytes_of(self.rb.at[c], self.sb_s.at[c]).wait()
+        bytes_of(self.ra.at[c], self.sa_s.at[c]).wait()
+        for d in range(4):
+
+            @when(rt.z != d)
+            def _():
+                bytes_of(self.ra.at[c, 0], self.sz_s.at[c, d]).wait()
+
+
+def reducer_bufs(count, block, dtype):
+    sizes = (16, 16, 16, 8, 4, 3, 3)
+    return [pltpu.VMEM((count, n) + block, dtype) for n in sizes] + [pltpu.VMEM((count,) + block, F32)]
+
+
+def reducer_sems(count):
+    dma = pltpu.SemaphoreType.DMA
+    return [dma((count,))] * 6 + [dma((count, 4)), dma((count, 3)), dma((count, 3))]
+
+
+def outer(left, right):
+    return lax.dot_general(left, right, (((0,), (0,)), ((), ())), preferred_element_type=F32)
+
+
+def inner(left, right):
+    return lax.dot_general(left, right, (((1,), (1,)), ((), ())), preferred_element_type=F32)
+
+
+def dense(left, right):
+    return jnp.dot(left, right, preferred_element_type=F32)
+
+
+def reduce_kernel(jobs, *refs):
+    n_in = 2 * len(jobs) + 2
+    ins, outs, rest = refs[:n_in], refs[n_in:n_in + 2], refs[n_in + 2:]
+    count = sum(n for _, n in jobs)
+    m_bufs, m_sems, v_bufs, v_sems = rest[:8], rest[8:17], rest[17:25], rest[25:34]
+    rt = Route()
+    main, small = Reducer(rt, m_bufs, m_sems), Reducer(rt, v_bufs, v_sems)
+    own, sib = m_bufs[0], m_bufs[1]
+    halves = ((sib, 1 - rt.core), (own, rt.core))
+
+    def tall(left, right, first):
+        def one(i, _):
+            for buf, core in halves:
+                j = (i // 8) * 16 + core * 8 + i % 8
+                part = left[:, pl.ds(pl.multiple_of(j * 128, 128), 128)]
+                grad = outer(part, right[...]).astype(BF16)
+                for q in range(4):
+                    buf[first + q, i] = grad[q * ROWS:(q + 1) * ROWS]
+            return 0
+
+        lax.fori_loop(0, 16, one, 0)
+
+    def square(left, right, c):
+        for buf, core in halves:
+            for xx in range(2):
+                part = left[:, pl.ds(pl.multiple_of((xx * 2 + core) * 256, 256), 256)]
+                buf[c, xx * 8:xx * 8 + 8] = outer(part, right).astype(BF16).reshape(8, ROWS, 1024)
+
+    def compute(c):
+        first = 0
+        for i, (kind, n) in enumerate(jobs):
+            left, right = ins[2 * i], ins[2 * i + 1]
+            if kind == "tall":
+
+                @when(c == first)
+                def _():
+                    tall(left, right, first)
+
+            else:
+
+                @when((c >= first) & (c < first + n))
+                def _():
+                    square(left, right[:, pl.ds(pl.multiple_of((c - first) * 1024, 1024), 1024)], c)
+
+            first += n
+
+    def compute_small():
+        rows8, up8 = ins[-2], ins[-1]
+
+        def one(i, _):
+            for buf, core in ((v_bufs[1], 1 - rt.core), (v_bufs[0], rt.core)):
+                j = (i // 8) * 16 + core * 8 + i % 8
+                buf[0, i, 0:8] = rows8[:, pl.ds(pl.multiple_of((j // 4) * 128, 128), 128)]
+                buf[0, i, 8:16] = up8[:, pl.ds(pl.multiple_of(j * 128, 128), 128)]
+            return 0
+
+        lax.fori_loop(0, 16, one, 0)
+
+    rt.greet()
+
+    def step(t, _):
+        for s in range(Reducer.stages):
+            c = t - s
+
+            @when((c >= 0) & (c < count))
+            def _():
+                if s == 0:
+                    compute(c)
+                main.stage(s, c)
+
+            @when(c == count)
+            def _():
+                if s == 0:
+                    compute_small()
+                small.stage(s, 0)
+
+        return 0
+
+    lax.fori_loop(0, count + Reducer.stages, step, 0)
+
+    def last(c, _):
+        main.finish(c)
+        return 0
+
+    lax.fori_loop(0, count, last, 0)
+    small.finish(0)
+    outs[0][...] = m_bufs[7][...]
+    mine = v_bufs[7][0]
+    quarter = owner(rt.x, rt.y, rt.z, rt.core) % 4
+    picked = jnp.zeros((16, 32), F32)
+    for q in range(4):
+        picked = jnp.where(quarter == q, mine[:, q * 32:(q + 1) * 32], picked)
+    outs[1][:, 0:128] = mine
+    outs[1][:, 128:160] = picked
+
+
+def reduce_gradients(jobs, ins, rows8, up8):
+    count = sum(n for _, n in jobs)
+    vmem = pl.BlockSpec(memory_space=pltpu.VMEM)
+    return pl.pallas_call(
+        functools.partial(reduce_kernel, jobs),
+        out_shape=(jax.ShapeDtypeStruct((count, ROWS, 1024), F32), jax.ShapeDtypeStruct((16, 256), F32)),
+        in_specs=[vmem] * (len(ins) + 2),
+        out_specs=(vmem, vmem),
+        scratch_shapes=reducer_bufs(count, (ROWS, 1024), BF16) + reducer_sems(count)
+        + reducer_bufs(1, (16, 128), F32) + reducer_sems(1),
+        compiler_params=pltpu.CompilerParams(collective_id=1, has_side_effects=True, vmem_limit_bytes=VMEM_LIMIT),
+    )(*ins, rows8, up8)
+
+
+def head_mask(shape, head):
+    lane = lax.broadcasted_iota(jnp.int32, shape, len(shape) - 1)
+    return (lane // HEAD_DIM) == head
+
+
+def only_head(values, head):
+    return jnp.where(head_mask(values.shape, head), values, jnp.zeros_like(values))
+
+
+def key_sequences(len_ref, shift, keys):
+    pos = lax.broadcasted_iota(jnp.int32, (keys, 128), 0)
+    seq = lax.shift_right_logical(pos, shift)
+    at = pos - lax.shift_left(seq, shift)
+    limit = jnp.zeros((keys, 128), jnp.int32)
+    for s in range(8):
+        limit = jnp.where(seq == s, len_ref[s], limit)
+    return jnp.where(at < limit, seq, -1)
+
+
+def key_bias(kseq, shift, start, width):
+    keys = kseq.shape[0]
+    qseq = lax.shift_right_logical(start + lax.broadcasted_iota(jnp.int32, (1, 128), 1), shift)
+    parts = []
+    for w in range(width // 128):
+        qs = lax.shift_right_logical(start + w * 128 + lax.broadcasted_iota(jnp.int32, (1, 128), 1), shift)
+        parts.append(jnp.where(kseq == qs, 0.0, NEG_FILL))
+    return jnp.concatenate(parts, axis=1)
+
+
+class Swap:
+    def __init__(self):
+        self.bucket, self.me = lax.axis_index("bucket"), lax.axis_index("ctx")
+
+    def greet(self):
+        barrier = pltpu.get_barrier_semaphore()
+        for off in range(1, 8):
+            target = (self.bucket, (self.me + off) % 8)
+            pl.semaphore_signal(barrier, inc=1, device_id=target, device_id_type=MESH_ID)
+        pl.semaphore_wait(barrier, 7)
+
+    def heads_out(self, tokens, heads, send_sem, recv_sem, local_sem):
+        rows = pl.ds(pl.multiple_of(self.me * 128, 128), 128)
+        for off in (4, 3, 5, 2, 6, 1, 7):
+            d = (self.me + off) % 8
+            remote(tokens.at[:, pl.ds(pl.multiple_of(d * 128, 128), 128)], heads.at[rows], send_sem, recv_sem, (self.bucket, d)).start()
+        pltpu.make_async_copy(tokens.at[:, pl.ds(pl.multiple_of(self.me * 128, 128), 128)], heads.at[rows], local_sem).start()
+
+    def heads_back(self, heads, tokens, send_sem, recv_sem, local_sem):
+        cols = pl.ds(pl.multiple_of(self.me * 128, 128), 128)
+        for off in (4, 3, 5, 2, 6, 1, 7):
+            d = (self.me + off) % 8
+            remote(heads.at[pl.ds(pl.multiple_of(d * 128, 128), 128)], tokens.at[:, cols], send_sem, recv_sem, (self.bucket, d)).start()
+        pltpu.make_async_copy(heads.at[pl.ds(pl.multiple_of(self.me * 128, 128), 128)], tokens.at[:, cols], local_sem).start()
+
+    def wait(self, heads, send_sem, recv_sem, local_sem):
+        seven = heads.at[pl.ds(0, 7 * 128)]
+        bytes_of(seven, recv_sem).wait()
+        bytes_of(seven, send_sem).wait()
+        bytes_of(heads.at[pl.ds(0, 128)], local_sem).wait()
+
+
+Q_BLOCK = 256
+
+
+def attend_block(i, shift, kseq, q, k, v, o_ref, lse_ref):
+    start = i * Q_BLOCK
+    rows = pl.ds(pl.multiple_of(start, Q_BLOCK), Q_BLOCK)
+    bias = key_bias(kseq[...], shift, start, Q_BLOCK)
+    scaled = q[rows] * jnp.asarray(HEAD_DIM ** (-0.5), BF16)
+    result = []
+    for h in range(2):
+        s = inner(k[...], only_head(scaled, h)) + bias
+        m = jnp.max(s, axis=0, keepdims=True)
+        e = jnp.exp(s - m)
+        total = jnp.sum(e, axis=0, keepdims=True)
+        w = (e * (1.0 / total)).astype(BF16)
+        lse_ref[h:h + 1, rows] = m + jnp.log(total)
+        o = outer(v[...], w)
+        result.append(o[h * HEAD_DIM:(h + 1) * HEAD_DIM])
+    o_ref[rows] = jnp.concatenate(result, axis=0).T.astype(BF16)
+
+
+def attend_kernel(x_ref, w_ref, t_ref, len_ref, att_ref, qh, kh, vh, lse, qkv, oh, kseq, wbuf, wsem, sems):
+    swap = Swap()
+    shift = 7 + swap.bucket
+    copies = [pltpu.make_async_copy(w_ref.at[pl.ds(i * 1024, 1024)], wbuf.at[i], wsem.at[i]) for i in range(3)]
+    for c in copies:
+        c.start()
+    swap.greet()
+    x = x_ref[...]
+    table = table_of(t_ref)
+    for i, (dst, row) in enumerate(((qh, 0), (kh, None), (vh, 1))):
+        copies[i].wait()
+        val = dense(x, wbuf[i])
+        if row is not None:
+            val = val + table[row:row + 1]
+        qkv[i] = val.astype(BF16)
+        swap.heads_out(qkv.at[i], dst, sems.at[3 * i], sems.at[3 * i + 1], sems.at[3 * i + 2])
+    kseq[...] = key_sequences(len_ref, shift, kseq.shape[0])
+    for i, dst in enumerate((qh, kh, vh)):
+        swap.wait(dst, sems.at[3 * i], sems.at[3 * i + 1], sems.at[3 * i + 2])
+
+    def block(i, _):
+        attend_block(i, shift, kseq, qh, kh, vh, oh, lse)
+        return 0
+
+    lax.fori_loop(0, qh.shape[0] // Q_BLOCK, block, 0)
+    swap.heads_back(oh, att_ref, sems.at[9], sems.at[10], sems.at[11])
+    swap.wait(oh, sems.at[9], sems.at[10], sems.at[11])
+
+
+def table_of(t_ref):
+    groups = []
+    for g in range(8):
+        groups.append(sum(t_ref[4 * g + i].astype(F32) for i in range(4)))
+    return jnp.concatenate(groups, axis=1)
+
+
+def attend(tokens, weights, table, lens):
+    vmem, anywhere = pl.BlockSpec(memory_space=pltpu.VMEM), pl.BlockSpec(memory_space=pl.ANY)
+    hs = jax.ShapeDtypeStruct((1024, 128), BF16)
+    return pl.pallas_call(
+        attend_kernel,
+        out_shape=(jax.ShapeDtypeStruct((128, 1024), BF16), hs, hs, hs, jax.ShapeDtypeStruct((2, 1024), F32)),
+        in_specs=[vmem, anywhere, vmem, pl.BlockSpec(memory_space=pltpu.SMEM)],
+        out_specs=(vmem,) * 5,
+        scratch_shapes=[
+            pltpu.VMEM((3, 128, 1024), BF16), pltpu.VMEM((1024, 128), BF16), pltpu.VMEM((1024, 128), jnp.int32),
+            pltpu.VMEM((3, 1024, 1024), BF16), pltpu.SemaphoreType.DMA((3,)), pltpu.SemaphoreType.DMA((12,)),
+        ],
+        compiler_params=pltpu.CompilerParams(collective_id=2, has_side_effects=True, vmem_limit_bytes=VMEM_LIMIT),
+    )(tokens, weights, table, lens)
+
+
+def attend_back_block(i, shift, kseq, q, k, v, do, lse, dq, dk, dv):
+    start = i * Q_BLOCK
+    rows = pl.ds(pl.multiple_of(start, Q_BLOCK), Q_BLOCK)
+    bias = key_bias(kseq[...], shift, start, Q_BLOCK)
+    scaled = q[rows] * jnp.asarray(HEAD_DIM ** (-0.5), BF16)
+    back = do[rows]
+    result = []
+    for h in range(2):
+        qm, dm = only_head(scaled, h), only_head(back, h)
+        p = jnp.exp(inner(k[...], qm) + bias - lse[h:h + 1, rows])
+        slope = inner(v[...], dm)
+        product = p * slope
+        delta = jnp.sum(product, axis=0, keepdims=True)
+        ds = (product - p * delta).astype(BF16)
+        dv[...] += dense(p.astype(BF16), dm)
+        dk[...] += dense(ds, qm)
+        g = outer(k[...], ds) * (HEAD_DIM ** (-0.5))
+        result.append(g[h * HEAD_DIM:(h + 1) * HEAD_DIM])
+    dq[rows] = jnp.concatenate(result, axis=0).T.astype(BF16)
+
+
+def attend_back_kernel(g_ref, qh, kh, vh, lse, len_ref, dq_t, dk_t, dv_t, doh, dqh, dk, dv, dkh, dvh, kseq, sems):
+    swap = Swap()
+    shift = 7 + swap.bucket
+    swap.greet()
+    swap.heads_out(g_ref, doh, sems.at[0], sems.at[1], sems.at[2])
+    kseq[...] = key_sequences(len_ref, shift, kseq.shape[0])
+    dk[...] = jnp.zeros_like(dk)
+    dv[...] = jnp.zeros_like(dv)
+    swap.wait(doh, sems.at[0], sems.at[1], sems.at[2])
+
+    def block(i, _):
+        attend_back_block(i, shift, kseq, qh, kh, vh, doh, lse, dqh, dk, dv)
+        return 0
+
+    lax.fori_loop(0, qh.shape[0] // Q_BLOCK, block, 0)
+    dkh[...] = dk[...].astype(BF16)
+    dvh[...] = dv[...].astype(BF16)
+    trio = ((dqh, dq_t), (dkh, dk_t), (dvh, dv_t))
+    for i, (src, dst) in enumerate(trio):
+        swap.heads_back(src, dst, sems.at[3 * i + 3], sems.at[3 * i + 4], sems.at[3 * i + 5])
+    for i, (src, dst) in enumerate(trio):
+        swap.wait(src, sems.at[3 * i + 3], sems.at[3 * i + 4], sems.at[3 * i + 5])
+
+
+def attend_back(grad_att, qh, kh, vh, lse, lens):
+    vmem = pl.BlockSpec(memory_space=pltpu.VMEM)
+    ts = jax.ShapeDtypeStruct((128, 1024), BF16)
+    half, full = pltpu.VMEM((1024, 128), BF16), pltpu.VMEM((1024, 128), F32)
+    return pl.pallas_call(
+        attend_back_kernel,
+        out_shape=(ts, ts, ts),
+        in_specs=[vmem] * 5 + [pl.BlockSpec(memory_space=pltpu.SMEM)],
+        out_specs=(vmem,) * 3,
+        scratch_shapes=[half, half, full, full, half, half, pltpu.VMEM((1024, 128), jnp.int32), pltpu.SemaphoreType.DMA((12,))],
+        compiler_params=pltpu.CompilerParams(collective_id=3, has_side_effects=True, vmem_limit_bytes=VMEM_LIMIT),
+    )(grad_att, qh, kh, vh, lse, lens)
+
+
+def gelu_value(values):
+    return 0.5 * values * (1.0 + lax.erf(values * 0.7071067811865476))
+
+
+def gelu_slope(values):
+    return 0.5 * (1.0 + lax.erf(values * 0.7071067811865476)) + values * jnp.exp(-0.5 * values * values) * 0.3989422804014327
+
+
+def row_mean(values):
+    return jnp.mean(values, axis=-1, keepdims=True)
+
+
+def column_sum(values):
+    return jnp.sum(values, axis=0, keepdims=True)
+
+
+def norm_parts(summed):
+    centred = summed - row_mean(summed)
+    inv_std = lax.rsqrt(row_mean(centred * centred) + EPSILON)
+    return centred * inv_std, inv_std
+
+
+def norm_back(incoming, normed, inv_std, gain):
+    scaled = incoming * gain
+    return inv_std * (scaled - row_mean(scaled) - normed * row_mean(scaled * normed))
+
+
+V_QUERY, V_VALUE, V_OUT, V_GAIN1, V_SHIFT1, V_DOWN, V_GAIN2, V_SHIFT2 = range(8)
+
+
+def middle_kernel(x_ref, att_ref, w_ref, t_ref, cot_ref,
+                  hid_ref, act_ref, gffn_ref, mid_ref, gpre_ref, gbr_ref, gone_ref, gatt_ref, rows_ref, up_ref,
+                  wbuf, pre, wsem):
+    order = [3, 4, 8, 5, 9, 6, 10, 7, 11]
+    copies = {i: pltpu.make_async_copy(w_ref.at[pl.ds(i * 1024, 1024)], wbuf.at[i - 3], wsem.at[i - 3]) for i in order}
+    for i in order:
+        copies[i].start()
+    table = table_of(t_ref)
+
+    def vec(row):
+        return table[row:row + 1]
+
+    x = x_ref[...].astype(F32)
+    copies[3].wait()
+    normed1, inv1 = norm_parts(x + (dense(att_ref[...], wbuf[0]) + vec(V_OUT)))
+    middle = normed1 * vec(V_GAIN1) + vec(V_SHIFT1)
+    mid_ref[...] = middle.astype(BF16)
+    ffn = jnp.zeros(x.shape, F32)
+    for i in range(4):
+        copies[4 + i].wait()
+        b_up = jnp.concatenate([t_ref[8 * i + j][8:9].astype(F32) for j in range(8)], axis=1)
+        value = dense(mid_ref[...], wbuf[1 + i]) + b_up
+        pre[i] = value
+        act = gelu_value(value).astype(BF16)
+        act_ref[:, i * 1024:(i + 1) * 1024] = act
+        copies[8 + i].wait()
+        ffn = ffn + dense(act, wbuf[5 + i])
+    normed2, inv2 = norm_parts(middle + (ffn + vec(V_DOWN)))
+    hid_ref[...] = (normed2 * vec(V_GAIN2) + vec(V_SHIFT2)).astype(BF16)
+    g = cot_ref[...].astype(F32)
+    rows_ref[...] = jnp.zeros_like(rows_ref)
+    rows_ref[V_GAIN2:V_GAIN2 + 1] = column_sum(g * normed2)
+    rows_ref[V_SHIFT2:V_SHIFT2 + 1] = column_sum(g)
+    gtwo = norm_back(g, normed2, inv2, vec(V_GAIN2))
+    gffn = gtwo.astype(BF16)
+    gffn_ref[...] = gffn
+    rows_ref[V_DOWN:V_DOWN + 1] = column_sum(gffn.astype(F32))
+    back = jnp.zeros(x.shape, F32)
+    up_ref[...] = jnp.zeros_like(up_ref)
+    for i in range(4):
+        gact = inner(gffn_ref[...], wbuf[5 + i]).astype(BF16).astype(F32)
+        gpre = (gact * gelu_slope(pre[i])).astype(BF16)
+        gpre_ref[:, i * 1024:(i + 1) * 1024] = gpre
+        up_ref[0:1, i * 1024:(i + 1) * 1024] = column_sum(gpre.astype(F32))
+        back = back + inner(gpre, wbuf[1 + i])
+    gmid = gtwo + back.astype(BF16).astype(F32)
+    rows_ref[V_GAIN1:V_GAIN1 + 1] = column_sum(gmid * normed1)
+    rows_ref[V_SHIFT1:V_SHIFT1 + 1] = column_sum(gmid)
+    gone = norm_back(gmid, normed1, inv1, vec(V_GAIN1))
+    gone_ref[...] = gone
+    gbr = gone.astype(BF16)
+    gbr_ref[...] = gbr
+    rows_ref[V_OUT:V_OUT + 1] = column_sum(gbr.astype(F32))
+    gatt_ref[...] = inner(gbr, wbuf[0]).astype(BF16)
+
+
+def middle_layer(tokens, attended, weights, table, cotangent):
+    vmem, anywhere = pl.BlockSpec(memory_space=pltpu.VMEM), pl.BlockSpec(memory_space=pl.ANY)
+
+    def s(shape, dtype):
+        return jax.ShapeDtypeStruct(shape, dtype)
+
+    narrow, wide = (128, 1024), (128, 4096)
+    return pl.pallas_call(
+        middle_kernel,
+        out_shape=(
+            s(narrow, BF16), s(wide, BF16), s(narrow, BF16), s(narrow, BF16), s(wide, BF16),
+            s(narrow, BF16), s(narrow, F32), s(narrow, BF16), s((8, 1024), F32), s((8, 4096), F32),
+        ),
+        in_specs=[vmem, vmem, anywhere, vmem, vmem],
+        out_specs=(vmem,) * 10,
+        scratch_shapes=[pltpu.VMEM((9, 1024, 1024), BF16), pltpu.VMEM((4, 128, 1024), F32), pltpu.SemaphoreType.DMA((9,))],
+        compiler_params=pltpu.CompilerParams(vmem_limit_bytes=VMEM_LIMIT),
+    )(tokens, attended, weights, table, cotangent)
+
+
+def fast_body(hidden_in, lengths, w_query, w_key, w_value, b_query, b_value, w_out, b_out, first_gain, first_shift,
+              w_up, b_up, w_down, b_down, second_gain, second_shift, cotangent):
+    tokens = hidden_in.reshape(128, 1024)
+    shards = jnp.concatenate(
+        [w_query, w_key, w_value, w_out] + [w_up[:, i * 1024:(i + 1) * 1024] for i in range(4)] + [w_down], axis=0
+    )
+    me = lax.axis_index("bucket") * 8 + lax.axis_index("ctx")
+    rows = jnp.stack([b_query, b_value, b_out, first_gain, first_shift, b_down, second_gain, second_shift])
+    spread = jnp.concatenate([jnp.where(me % 4 == q, rows, jnp.zeros_like(rows)) for q in range(4)], axis=1)
+    small = jnp.concatenate([spread, b_up[None], jnp.zeros((7, 128), BF16)], axis=0)
+    weights, table = gather_weights(shards, small)
+    lens = lengths.reshape(8)
+    attended, qh, kh, vh, lse = attend(tokens, weights, table, lens)
+    (hidden_out, act, gffn, mid, gpre, gbr, gone, gatt, rows8, up8) = middle_layer(
+        tokens, attended, weights, table, cotangent.reshape(128, 1024)
+    )
+    dq, dk, dv = attend_back(gatt, qh, kh, vh, lse, lens)
+    grad_in = gone + inner(dq, weights[0:1024]) + inner(dk, weights[1024:2048]) + inner(dv, weights[2048:3072])
+    more = jnp.stack([jnp.sum(dq.astype(F32), axis=0), jnp.sum(dv.astype(F32), axis=0)])
+    rows8 = jnp.concatenate([more, rows8[2:]], axis=0)
+    jobs = (("tall", 4), ("square", 4), ("square", 1), ("square", 1), ("square", 1), ("square", 1))
+    sums, small_sums = reduce_gradients(
+        jobs, (act, gffn, mid, gpre, attended, gbr, tokens, dq, tokens, dk, tokens, dv), rows8, up8
+    )
+    g_down = sums[:4].reshape(128, 1024)
+    g_up = jnp.concatenate([sums[4 + i] for i in range(4)], axis=1)
+    row = lambda r: small_sums[r, 128:160]
+    return (
+        hidden_out.reshape(hidden_in.shape), grad_in.reshape(hidden_in.shape), sums[9], sums[10], sums[11],
+        row(0), row(1), sums[8], row(2), row(3), row(4), g_up, small_sums[8, 0:128], g_down, row(5), row(6), row(7),
+    )
 
 
 def matmul(left, right):
@@ -55,11 +872,11 @@
     return (inv_std * inner, jnp.sum(incoming * normed, axis=0), jnp.sum(incoming, axis=0))
 
 
-def gelu_value(values):
+def plain_gelu_value(values):
     return 0.5 * values * (1.0 + jax.scipy.special.erf(values * 0.7071067811865476))
 
 
-def gelu_slope(values):
+def plain_gelu_slope(values):
     return (
         0.5 * (1.0 + jax.scipy.special.erf(values * 0.7071067811865476))
         + values * jnp.exp(-0.5 * values * values) * 0.3989422804014327
@@ -107,7 +924,7 @@
     return lax.fori_loop(0, turn_count, advance, running)
 
 
-def body(
+def general_body(
     hidden_in,
     lengths,
     w_query,
@@ -239,7 +1056,7 @@
     )
     middle_low = rounded(middle)
     pre_act = matmul(middle_low, up_mat) + widened(up_bias)
-    activated = rounded(gelu_value(pre_act))
+    activated = rounded(plain_gelu_value(pre_act))
     ffn_out = matmul(activated, down_mat) + widened(down_bias)
     result, normed_two, inv_two = norm_forward(
         middle + ffn_out, widened(gain_two), widened(shift_two)
@@ -278,7 +1095,7 @@
     grad_b_down = jnp.sum(widened(grad_ffn), axis=0)
     grad_w_down = row_inner(activated, grad_ffn)
     grad_act = widened(rounded(right_inner(grad_ffn, down_mat)))
-    grad_pre = rounded(grad_act * gelu_slope(pre_act))
+    grad_pre = rounded(grad_act * plain_gelu_slope(pre_act))
     grad_b_up = jnp.sum(widened(grad_pre), axis=0)
     grad_w_up = row_inner(middle_low, grad_pre)
     grad_middle = grad_two_sum + widened(rounded(right_inner(grad_pre, up_mat)))
@@ -409,6 +1226,11 @@
         P(("bucket", "ctx")),
         P("bucket", None, "ctx", None),
     )
+    def body(*arguments):
+        here = dict(mesh.shape) == {"bucket": 4, "ctx": 8}
+        shapes = arguments[0].shape == (1, 1, 128, 1024) and arguments[11].shape == (32, 4096)
+        return (fast_body if here and shapes else general_body)(*arguments)
+
     return jax.shard_map(
         body,
         mesh=mesh,

time: 1910 us -> 364 us (0.19)
  waiting for transfers between devices: 1480 us -> 0 us
  Pallas kernels: 0 us -> 336 us
  blocking collectives: 210 us -> 0 us
  matrix products: 121 us -> 8.31 us
  local copies, waits for them, and re-layouts: 63.1 us -> 15.6 us
    reduce_scatter x3 -> x0, waiting for transfers between devices: 860 us -> none  [the longest x1 360 us: body(): lax.psum_scatter(grad_w_down, ('bucket', 'ctx'), scatter_dimension=0, til...]
    pallas_call x0 -> x5, Pallas kernels: none -> 336 us  [the longest x1 132 us: reduce_gradients(): pl.pallas_call(functools.partial(reduce_kernel, jobs), out_shape=(jax.Sha...]
    all_gather x10 -> x0, waiting for transfers between devices: 323 us -> none  [the longest x1 76.9 us: body(): lax.all_gather(shards[9], ('bucket', 'ctx'), axis=0, tiled=True)]
    unnamed x19 -> x0, waiting for transfers between devices: 293 us -> none
    all_gather x3 -> x0, blocking collectives: 127 us -> none  [the longest x1 65.9 us: body(): lax.all_gather(shards[10], ('bucket', 'ctx'), axis=0, tiled=True)]
    dot_general x32 -> x3, matrix products: 121 us -> 8.31 us  [inner(): lax.dot_general(left, right, (((1,), (1,)), ((), ())), preferred_element_...]
    unnamed x2 -> x0, blocking collectives: 82.9 us -> none
    unnamed x122 -> x20, local copies, waits for them, and re-layouts: 43.2 us -> 6.78 us
  transfers between devices with their start and end apart: 16 -> 0, of which waited for: 12 -> 0; matrix products, arithmetic and copies ran while one was open for 10% -> 0% of each run, Pallas kernels for 0% -> 0%
where the time goes in v1:
time: 364 us; the launch traced here: 363 us
  Pallas kernels  336 us (92%)
  local copies, waits for them, and re-layouts  15.6 us (4%)
  matrix products  8.31 us (2%)
    pallas_call x1, Pallas kernels, reduce_gradients(): pl.pallas_call(functools.partial(reduce_kernel, jobs), out_shape=(jax.Sha...  132 us
    pallas_call x1, Pallas kernels, gather_weights(): pl.pallas_call(gather_kernel, out_shape=(jax.ShapeDtypeStruct((PIECES * 1...  114 us
    pallas_call x1, Pallas kernels, attend(): pl.pallas_call(attend_kernel, out_shape=(jax.ShapeDtypeStruct((128, 1024)...  39.3 us
    pallas_call x1, Pallas kernels, attend_back(): pl.pallas_call(attend_back_kernel, out_shape=(ts, ts, ts), in_specs=[vmem...  34.2 us
    pallas_call x1, Pallas kernels, middle_layer(): pl.pallas_call(middle_kernel, out_shape=(s(narrow, BF16), s(wide, BF16),...  15.9 us
    dot_general x3, matrix products, inner(): lax.dot_general(left, right, (((1,), (1,)), ((), ())), preferred_element_...  8.31 us

profile of v1, /device:TPU:0, one launch (start us, length us, event | category | flops | bytes accessed | tf_op | source)
XLA Modules:
  0.0 363.5 jit_solution(328050208021767974)
XLA Ops:
  0.7 0.8 constant_dynamic-update-slice_fusion.4
  1.5 0.8 constant_dynamic-update-slice_fusion.3
  2.3 0.8 constant_dynamic-update-slice_fusion.2
  3.2 0.8 constant_dynamic-update-slice_fusion.1
  4.0 0.8 slice_dynamic-update-slice_fusion.3
  4.9 0.8 slice_dynamic-update-slice_fusion.2
  5.7 0.8 slice_dynamic-update-slice_fusion.1
  6.6 0.8 slice_dynamic-update-slice_fusion
  7.4 1.0 constant_dynamic-update-slice_fusion.x_ref
  8.4 0.0 copy-start.2
  8.4 1.1 stack.41
  9.5 0.1 pad.12.clone
  9.6 1.3 maximum_maximum_fusion.v_ref
  10.9 0.0 copy-done.2
  10.9 114.2 %shard_map.305 = (bf16[12288,1024]{1,0:T(8,128)(2,1)}, bf16[32,16,128]{2,1,0:T(8,128)(2,1)}) custom-call(bf16[384,1024]{1,0:T(8,128)(2,1)} %copy-done.2, bf16[16,128]{1,0:T(8,128)(2,1)} %maximum_maximum_fusion.v_ref), custom_call_target="tpu_custom_call" | custom-call | tf_op jit(solution)/shard_map/pallas_call | solution.py:230
  125.2 39.3 %shard_map.306 = (bf16[128,1024]{1,0:T(8,128)(2,1)}, bf16[1024,128]{1,0:T(8,128)(2,1)}, bf16[1024,128]{1,0:T(8,128)(2,1)}, bf16[1024,128]{1,0:T(8,128)(2,1)}, f32[2,1024]{1,0:T(2,128)}) custom-call(bf16[128,1024]{1,0:T(8,128)(2,1)} %bitcast.55, bf16[12288,1024]{1,0:T(8,128)(2,1)} %get-tuple-element.39.w_ref, bf16[32,16,128]{2,1,0:T(8,128)(2,1)} %get-tuple-element.40.t_ref, ...), custom_call_target="tpu_custom_call" | custom-call | tf_op jit(solution)/shard_map/pallas_call | solution.py:621
  164.5 15.9 %shard_map.307 = (bf16[128,1024]{1,0:T(8,128)(2,1)}, bf16[128,4096]{1,0:T(8,128)(2,1)}, bf16[128,1024]{1,0:T(8,128)(2,1)}, bf16[128,1024]{1,0:T(8,128)(2,1)}, bf...) custom-call(bf16[128,1024]{1,0:T(8,128)(2,1)} %bitcast.56, ...), custom_call_target="tpu_custom_call" | custom-call | tf_op jit(solution)/shard_map/pallas_call | solution.py:786
  180.4 34.2 %shard_map.308 = (bf16[128,1024]{1,0:T(8,128)(2,1)}, bf16[128,1024]{1,0:T(8,128)(2,1)}, bf16[128,1024]{1,0:T(8,128)(2,1)}) custom-call(bf16[128,1024]{1,0:T(8,128)(2,1)} %get-tuple-element.44.g_ref, bf16[1024,128]{1,0:T(8,128)(2,1)} %get-tuple-element.45.qh, bf16[1024,128]{1,0:T(8,128)(2,1)} %get-tuple-element.46.kh, ...), custom_call_target="tpu_custom_call" | custom-call | tf_op jit(solution)/shard_map/pallas_call | solution.py:683
  214.6 0.0 copy-start.4
  214.6 2.6 fusion
  217.2 0.0 copy-start
  217.2 0.0 copy-start.3
  217.2 0.0 copy-done.4
  217.2 2.5 fusion.2
  219.7 0.0 copy-done
  219.7 0.0 copy-done.3
  219.7 0.0 copy-start.5
  219.8 0.0 copy-start.1
  219.8 3.3 fusion.15
  223.1 0.0 copy-done.5
  223.1 0.0 copy-done.1
  223.1 0.1 convert_reduce_fusion
  223.2 0.6 pad_maximum_fusion.1.refs_12_
  223.8 132.1 %shard_map.309 = (f32[12,32,1024]{2,1,0:T(8,128)}, f32[16,256]{1,0:T(8,128)}) custom-call(bf16[128,4096]{1,0:T(8,128)(2,1)} %get-tuple-element.52.refs_0_, bf16[128,1024]{1,0:T(8,128)(2,1)} %get-tuple-element.53.refs_1_, bf16[128,1024]{1,0:T(8,128)(2,1)} %get-tuple-element.54.refs_2_, bf16[128,4096]{1,0:T(8,128)(2,1)} %get-tuple-element.55.refs_3_, ...), custom_call_target="tpu_custom_call" | custom-call | tf_op jit(solution)/shard_map/pallas_call | solution.py:489
  355.9 2.1 slice_bitcast_fusion.3
  358.1 1.5 slice_bitcast_fusion.8
  359.6 0.8 pad_maximum_fusion
  360.4 1.2 slice_bitcast_fusion.11
  361.6 1.9 slice.100
  (3 shorter events, 0.0 us)
Async XLA Ops:
  8.4 2.5 copy-start.2
  214.6 2.6 copy-start.4
  217.2 2.5 copy-start
  217.2 2.5 copy-start.3
  219.7 3.3 copy-start.5
  219.8 3.3 copy-start.1

commit v2 on v0

--- a/solution.py
+++ b/solution.py
@@ -3,13 +3,897 @@
 import jax
 import jax.numpy as jnp
 from jax import lax
+from jax.experimental import pallas as pl
+from jax.experimental.pallas import tpu as pltpu
 from jax.sharding import PartitionSpec as P
 
 HEAD_DIM = 64
-
-
 EPSILON = 1e-05
 NEG_FILL = -1e30
+MESH_ID = pl.DeviceIdType.MESH
+F32, BF16 = jnp.float32, jnp.bfloat16
+ROWS = 32
+PIECES = 12
+VMEM_LIMIT = 62 * 2**20
+
+
+def when(condition):
+    return pl.when(condition)
+
+
+def place():
+    bucket, ctx = lax.axis_index("bucket"), lax.axis_index("ctx")
+    return bucket // 2, ctx % 2, ctx // 2, bucket % 2
+
+
+def device(x, y, z, core):
+    return (x * 2 + core, z * 2 + y)
+
+
+def owner(x, y, z, core):
+    return (x * 2 + core) * 8 + z * 2 + y
+
+
+def remote(src, dst, send_sem, recv_sem, target):
+    return pltpu.make_async_remote_copy(
+        src_ref=src, dst_ref=dst, send_sem=send_sem, recv_sem=recv_sem,
+        device_id=target, device_id_type=MESH_ID,
+    )
+
+
+def bytes_of(ref, sem):
+    return pltpu.make_async_copy(ref, ref, sem)
+
+
+class Route:
+    def __init__(self):
+        self.x, self.y, self.z, self.core = x, y, z, core = place()
+        self.ax, self.ay = jnp.where(core == 0, 1 - x, x), jnp.where(core == 0, y, 1 - y)
+        self.bx, self.by = jnp.where(core == 1, 1 - x, x), jnp.where(core == 1, y, 1 - y)
+        self.a = device(self.ax, self.ay, z, core)
+        self.b = device(self.bx, self.by, z, core)
+        self.sibling = device(x, y, z, 1 - core)
+        self.up = device(x, y, jnp.minimum(z + 1, 3), core)
+        self.down = device(x, y, jnp.maximum(z - 1, 0), core)
+
+    def greet(self):
+        z = self.z
+        bucket, ctx = lax.axis_index("bucket"), lax.axis_index("ctx")
+        barrier = pltpu.get_barrier_semaphore()
+        pack = [(bucket, (ctx + off) % 8) for off in range(1, 8)]
+        for target in [self.a, self.b, self.sibling] + pack:
+            pl.semaphore_signal(barrier, inc=1, device_id=target, device_id_type=MESH_ID)
+
+        @when(z < 3)
+        def _():
+            pl.semaphore_signal(barrier, inc=1, device_id=self.up, device_id_type=MESH_ID)
+
+        @when(z > 0)
+        def _():
+            pl.semaphore_signal(barrier, inc=1, device_id=self.down, device_id_type=MESH_ID)
+
+        pl.semaphore_wait(barrier, 10 + (z < 3).astype(jnp.int32) + (z > 0).astype(jnp.int32))
+
+
+class Gatherer:
+    stages = 7
+
+    def __init__(self, route, count, own, block, span, sems):
+        self.rt, self.count, self.own, self.block, self.span = route, count, own, block, span
+        (self.zs, self.zr, self.ps, self.ar, self.br, self.dr, self.ls) = sems
+
+    def spread(self, c, src, j, jz, to_a, to_b, z_dirs):
+        rt, dst = self.rt, self.block(c, j)
+        if "up" in z_dirs:
+
+            @when(rt.z < 3)
+            def _():
+                remote(src, dst, self.zs.at[0, c, jz], self.zr.at[c, jz], rt.up).start()
+
+        if "down" in z_dirs:
+
+            @when(rt.z > 0)
+            def _():
+                remote(src, dst, self.zs.at[1, c, jz], self.zr.at[c, jz], rt.down).start()
+
+        if to_a:
+            remote(src, dst, self.ps, self.ar.at[c, jz], rt.a).start()
+        if to_b is not None:
+            remote(src, dst, self.ps, self.br.at[c, to_b * 4 + jz], rt.b).start()
+        remote(src, dst, self.ps, self.dr.at[c], rt.sibling).start()
+
+    def near(self, k, action):
+        for sign in (0,) if k == 0 else (-1, 1):
+            zz = self.rt.z + sign * k
+
+            @when((zz >= 0) & (zz <= 3))
+            def _():
+                action(zz, "up" if sign < 0 else "down")
+
+    def own_stage(self, c):
+        rt = self.rt
+        j = owner(rt.x, rt.y, rt.z, rt.core)
+        pltpu.make_async_copy(self.own(c), self.block(c, j), self.ls.at[c]).start()
+        self.spread(c, self.own(c), j, rt.z, True, 0, ("up", "down"))
+
+    def z_stage(self, c, k):
+        rt = self.rt
+
+        def action(zz, direction):
+            j = owner(rt.x, rt.y, zz, rt.core)
+            bytes_of(self.block(c, j), self.zr.at[c, zz]).wait()
+            self.spread(c, self.block(c, j), j, zz, True, 0, (direction,))
+
+        self.near(k, action)
+
+    def a_stage(self, c, k):
+        rt = self.rt
+
+        def action(zz, _):
+            j = owner(rt.ax, rt.ay, zz, rt.core)
+            bytes_of(self.block(c, j), self.ar.at[c, zz]).wait()
+            self.spread(c, self.block(c, j), j, zz, False, 1, ())
+
+        self.near(k, action)
+
+    def b_stage(self, c, k):
+        rt = self.rt
+
+        def action(zz, _):
+            for which, (xx, yy) in enumerate(((rt.bx, rt.by), (1 - rt.x, 1 - rt.y))):
+                j = owner(xx, yy, zz, rt.core)
+                bytes_of(self.block(c, j), self.br.at[c, which * 4 + zz]).wait()
+                self.spread(c, self.block(c, j), j, zz, False, None, ())
+
+        self.near(k, action)
+
+    def stage(self, s, c):
+        if s == 0:
+            self.own_stage(c)
+        if 1 <= s <= 3:
+            self.z_stage(c, s)
+        if 2 <= s <= 5:
+            self.a_stage(c, s - 2)
+        if 3 <= s <= 6:
+            self.b_stage(c, s - 3)
+
+    def arrived(self, c):
+        bytes_of(self.span(16), self.dr.at[c]).wait()
+        bytes_of(self.span(1), self.ls.at[c]).wait()
+
+    def finish(self):
+        bytes_of(self.span(28 * self.count), self.ps).wait()
+
+    def finish_z(self, c):
+        rt = self.rt
+        for zz in range(4):
+
+            @when((rt.z < 3) & (rt.z >= zz))
+            def _():
+                bytes_of(self.span(1), self.zs.at[0, c, zz]).wait()
+
+            @when((rt.z > 0) & (rt.z <= zz))
+            def _():
+                bytes_of(self.span(1), self.zs.at[1, c, zz]).wait()
+
+
+def gather_sems(count):
+    dma = pltpu.SemaphoreType.DMA
+    return [dma((2, count, 4)), dma((count, 4)), dma(()), dma((count, 4)), dma((count, 8)), dma((count,)), dma((count,))]
+
+
+def outer(left, right):
+    return lax.dot_general(left, right, (((0,), (0,)), ((), ())), preferred_element_type=F32)
+
+
+def inner(left, right):
+    return lax.dot_general(left, right, (((1,), (1,)), ((), ())), preferred_element_type=F32)
+
+
+def dense(left, right):
+    return jnp.dot(left, right, preferred_element_type=F32)
+
+
+def head_mask(shape, head):
+    lane = lax.broadcasted_iota(jnp.int32, shape, len(shape) - 1)
+    return (lane // HEAD_DIM) == head
+
+
+def only_head(values, head):
+    return jnp.where(head_mask(values.shape, head), values, jnp.zeros_like(values))
+
+
+def key_sequences(len_ref, shift, keys):
+    pos = lax.broadcasted_iota(jnp.int32, (keys, 128), 0)
+    seq = lax.shift_right_logical(pos, shift)
+    at = pos - lax.shift_left(seq, shift)
+    limit = jnp.zeros((keys, 128), jnp.int32)
+    for s in range(8):
+        limit = jnp.where(seq == s, len_ref[s], limit)
+    return jnp.where(at < limit, seq, -1)
+
+
+def key_bias(kseq, shift, start, width):
+    keys = kseq.shape[0]
+    qseq = lax.shift_right_logical(start + lax.broadcasted_iota(jnp.int32, (1, 128), 1), shift)
+    parts = []
+    for w in range(width // 128):
+        qs = lax.shift_right_logical(start + w * 128 + lax.broadcasted_iota(jnp.int32, (1, 128), 1), shift)
+        parts.append(jnp.where(kseq == qs, 0.0, NEG_FILL))
+    return jnp.concatenate(parts, axis=1)
+
+
+class Swap:
+    def __init__(self):
+        self.bucket, self.me = lax.axis_index("bucket"), lax.axis_index("ctx")
+
+    def heads_out(self, tokens, heads, send_sem, recv_sem, local_sem):
+        rows = pl.ds(pl.multiple_of(self.me * 128, 128), 128)
+        for off in (4, 3, 5, 2, 6, 1, 7):
+            d = (self.me + off) % 8
+            remote(tokens.at[:, pl.ds(pl.multiple_of(d * 128, 128), 128)], heads.at[rows], send_sem, recv_sem, (self.bucket, d)).start()
+        pltpu.make_async_copy(tokens.at[:, pl.ds(pl.multiple_of(self.me * 128, 128), 128)], heads.at[rows], local_sem).start()
+
+    def heads_back(self, heads, tokens, send_sem, recv_sem, local_sem):
+        cols = pl.ds(pl.multiple_of(self.me * 128, 128), 128)
+        for off in (4, 3, 5, 2, 6, 1, 7):
+            d = (self.me + off) % 8
+            remote(heads.at[pl.ds(pl.multiple_of(d * 128, 128), 128)], tokens.at[:, cols], send_sem, recv_sem, (self.bucket, d)).start()
+        pltpu.make_async_copy(heads.at[pl.ds(pl.multiple_of(self.me * 128, 128), 128)], tokens.at[:, cols], local_sem).start()
+
+    def wait(self, heads, send_sem, recv_sem, local_sem):
+        seven = heads.at[pl.ds(0, 7 * 128)]
+        bytes_of(seven, recv_sem).wait()
+        bytes_of(seven, send_sem).wait()
+        bytes_of(heads.at[pl.ds(0, 128)], local_sem).wait()
+
+
+Q_BLOCK = 256
+
+
+def attend_block(i, shift, kseq, q, k, v, o_ref, lse_ref):
+    start = i * Q_BLOCK
+    rows = pl.ds(pl.multiple_of(start, Q_BLOCK), Q_BLOCK)
+    bias = key_bias(kseq[...], shift, start, Q_BLOCK)
+    scaled = q[rows] * jnp.asarray(HEAD_DIM ** (-0.5), BF16)
+    result = []
+    for h in range(2):
+        s = inner(k[...], only_head(scaled, h)) + bias
+        m = jnp.max(s, axis=0, keepdims=True)
+        e = jnp.exp(s - m)
+        total = jnp.sum(e, axis=0, keepdims=True)
+        w = (e * (1.0 / total)).astype(BF16)
+        lse_ref[h:h + 1, rows] = m + jnp.log(total)
+        o = outer(v[...], w)
+        result.append(o[h * HEAD_DIM:(h + 1) * HEAD_DIM])
+    o_ref[rows] = jnp.concatenate(result, axis=0).T.astype(BF16)
+
+
+def attend_back_block(i, shift, kseq, q, k, v, do, lse, dq, dk, dv):
+    start = i * Q_BLOCK
+    rows = pl.ds(pl.multiple_of(start, Q_BLOCK), Q_BLOCK)
+    bias = key_bias(kseq[...], shift, start, Q_BLOCK)
+    scaled = q[rows] * jnp.asarray(HEAD_DIM ** (-0.5), BF16)
+    back = do[rows]
+    result = []
+    for h in range(2):
+        qm, dm = only_head(scaled, h), only_head(back, h)
+        p = jnp.exp(inner(k[...], qm) + bias - lse[h:h + 1, rows])
+        slope = inner(v[...], dm)
+        product = p * slope
+        delta = jnp.sum(product, axis=0, keepdims=True)
+        ds = (product - p * delta).astype(BF16)
+        dv[...] += dense(p.astype(BF16), dm)
+        dk[...] += dense(ds, qm)
+        g = outer(k[...], ds) * (HEAD_DIM ** (-0.5))
+        result.append(g[h * HEAD_DIM:(h + 1) * HEAD_DIM])
+    dq[rows] = jnp.concatenate(result, axis=0).T.astype(BF16)
+
+
+def table_of(t_ref):
+    groups = []
+    for g in range(8):
+        groups.append(sum(t_ref[4 * g + i].astype(F32) for i in range(4)))
+    return jnp.concatenate(groups, axis=1)
+
+
+def gelu_value(values):
+    return 0.5 * values * (1.0 + lax.erf(values * 0.7071067811865476))
+
+
+def gelu_slope(values):
+    return 0.5 * (1.0 + lax.erf(values * 0.7071067811865476)) + values * jnp.exp(-0.5 * values * values) * 0.3989422804014327
+
+
+def row_mean(values):
+    return jnp.mean(values, axis=-1, keepdims=True)
+
+
+def column_sum(values):
+    return jnp.sum(values, axis=0, keepdims=True)
+
+
+def norm_parts(summed):
+    centred = summed - row_mean(summed)
+    inv_std = lax.rsqrt(row_mean(centred * centred) + EPSILON)
+    return centred * inv_std, inv_std
+
+
+def norm_back(incoming, normed, inv_std, gain):
+    scaled = incoming * gain
+    return inv_std * (scaled - row_mean(scaled) - normed * row_mean(scaled * normed))
+
+
+V_QUERY, V_VALUE, V_OUT, V_GAIN1, V_SHIFT1, V_DOWN, V_GAIN2, V_SHIFT2 = range(8)
+V_UP = 8
+W_DOWN, W_UP = 4096, 8192
+
+
+def piece_row(c, j):
+    tall = (c >= 4) & (c < 8)
+    return pl.multiple_of(jnp.where(tall, W_DOWN + 128 * j + ROWS * (c - 4), c * 1024 + ROWS * j), ROWS)
+
+
+def forward_kernel(x_ref, cot_ref, v_ref, len_ref, wq, wk, wv, wo, wu, wd,
+                   w_out, att, qh, kh, vh, lse, hid, act, pre, mid, nor1, inv1, gtwo, gffn, rows, table,
+                   w, own, tiles, qkv, oh, kseq, own_sems, out_sems, swap_sems, *sems):
+    rt, swap = Route(), Swap()
+    shift = 7 + swap.bucket
+    loads = [pltpu.make_async_copy(ref, own.at[pl.ds(i * ROWS, ROWS)], own_sems.at[i]) for i, ref in enumerate((wq, wk, wv, wo))]
+    loads.append(pltpu.make_async_copy(wd, own.at[pl.ds(4 * ROWS, 4 * ROWS)], own_sems.at[4]))
+    for i in range(4):
+        loads.append(pltpu.make_async_copy(wu.at[:, pl.ds(i * 1024, 1024)], own.at[pl.ds((8 + i) * ROWS, ROWS)], own_sems.at[5 + i]))
+    for load in loads:
+        load.start()
+    main = Gatherer(
+        rt, PIECES,
+        lambda c: own.at[pl.ds(pl.multiple_of(c * ROWS, ROWS), ROWS)],
+        lambda c, j: w.at[pl.ds(piece_row(c, j), ROWS)],
+        lambda n: w.at[pl.ds(0, n * ROWS)],
+        sems[:7],
+    )
+    small = Gatherer(rt, 1, lambda c: v_ref, lambda c, j: tiles.at[j], lambda n: tiles.at[pl.ds(0, n)], sems[7:])
+    for load in loads:
+        load.wait()
+    rt.greet()
+
+    def vec(row):
+        return table[row:row + 1]
+
+    def project(i):
+        value = dense(x_ref[...], w[i * 1024:(i + 1) * 1024])
+        if i != 1:
+            value = value + vec(V_QUERY if i == 0 else V_VALUE)
+        qkv[i] = value.astype(BF16)
+        swap.heads_out(qkv.at[i], (qh, kh, vh)[i], *(swap_sems.at[3 * i + n] for n in range(3)))
+
+    def start():
+        small.arrived(0)
+        table[0:16] = table_of(tiles)
+        for i in range(4):
+            table[V_UP + i:V_UP + i + 1] = jnp.concatenate([tiles[8 * i + j][8:9].astype(F32) for j in range(8)], axis=1)
+        kseq[...] = key_sequences(len_ref, shift, kseq.shape[0])
+        project(0)
+
+    def score(first):
+        if first == 0:
+            for i, ref in enumerate((qh, kh, vh)):
+                swap.wait(ref, *(swap_sems.at[3 * i + n] for n in range(3)))
+
+        def block(i, _):
+            attend_block(i, shift, kseq, qh, kh, vh, oh, lse)
+            return 0
+
+        lax.fori_loop(first, first + 2, block, 0)
+        if first == 2:
+            swap.heads_back(oh, att, *(swap_sems.at[9 + n] for n in range(3)))
+
+    def first_norm():
+        swap.wait(oh, *(swap_sems.at[9 + n] for n in range(3)))
+        normed, inv = norm_parts(x_ref[...].astype(F32) + (dense(att[...], w[3072:4096]) + vec(V_OUT)))
+        nor1[...] = normed
+        inv1[...] = inv
+        mid[...] = (normed * vec(V_GAIN1) + vec(V_SHIFT1)).astype(BF16)
+        gtwo[...] = jnp.zeros_like(gtwo)
+
+    def up(i):
+        value = dense(mid[...], w[W_UP + i * 1024:W_UP + (i + 1) * 1024]) + vec(V_UP + i)
+        pre[i] = value
+        now = gelu_value(value).astype(BF16)
+        act[:, i * 1024:(i + 1) * 1024] = now
+        gtwo[...] += dense(now, w[W_DOWN + i * 1024:W_DOWN + (i + 1) * 1024])
+
+    items = {
+        7: start, 8: lambda: project(1), 9: lambda: project(2), 10: lambda: score(0), 11: lambda: score(2), 13: first_norm,
+        15: lambda: up(0), 16: lambda: up(1), 17: lambda: up(2), 18: lambda: up(3),
+    }
+
+    def save(i):
+        rows_of = pl.ds(pl.multiple_of(i * 1024, 1024), 1024)
+        return pltpu.make_async_copy(w.at[rows_of], w_out.at[rows_of], out_sems.at[i])
+
+    def step(t, _):
+        for s in range(Gatherer.stages):
+            c = t - s
+
+            @when(c == 0)
+            def _():
+                small.stage(s, 0)
+
+            @when((c >= 0) & (c < PIECES))
+            def _():
+                main.stage(s, c)
+
+        c = t - Gatherer.stages
+
+        @when(c >= 0)
+        def _():
+            main.arrived(c)
+
+            @when((c < 4) | (c >= 8))
+            def _():
+                save(c).start()
+
+            @when(c == 7)
+            def _():
+                for i in range(4, 8):
+                    save(i).start()
+
+        for k, item in items.items():
+
+            @when(t == k)
+            def _():
+                item()
+
+        return 0
+
+    lax.fori_loop(0, PIECES + Gatherer.stages, step, 0)
+    middle = nor1[...] * vec(V_GAIN1) + vec(V_SHIFT1)
+    normed2, inv2 = norm_parts(middle + (gtwo[...] + vec(V_DOWN)))
+    hid[...] = (normed2 * vec(V_GAIN2) + vec(V_SHIFT2)).astype(BF16)
+    g = cot_ref[...].astype(F32)
+    rows[...] = jnp.zeros_like(rows)
+    rows[V_GAIN2:V_GAIN2 + 1] = column_sum(g * normed2)
+    rows[V_SHIFT2:V_SHIFT2 + 1] = column_sum(g)
+    back = norm_back(g, normed2, inv2, vec(V_GAIN2))
+    gtwo[...] = back
+    low = back.astype(BF16)
+    gffn[...] = low
+    rows[V_DOWN:V_DOWN + 1] = column_sum(low.astype(F32))
+    small.finish()
+    small.finish_z(0)
+
+    def last(c, _):
+        main.finish_z(c)
+        save(c).wait()
+        return 0
+
+    lax.fori_loop(0, PIECES, last, 0)
+    main.finish()
+
+
+def shaped(shape, dtype):
+    return jax.ShapeDtypeStruct(shape, dtype)
+
+
+def forward(tokens, cotangent, small, lens, weights):
+    vmem, anywhere = pl.BlockSpec(memory_space=pltpu.VMEM), pl.BlockSpec(memory_space=pl.ANY)
+    dma = pltpu.SemaphoreType.DMA
+    narrow, wide, heads = (128, 1024), (128, 4096), (1024, 128)
+    return pl.pallas_call(
+        forward_kernel,
+        out_shape=(
+            shaped((PIECES * 1024, 1024), BF16), shaped(narrow, BF16), shaped(heads, BF16), shaped(heads, BF16),
+            shaped(heads, BF16), shaped((2, 1024), F32), shaped(narrow, BF16), shaped(wide, BF16),
+            shaped((4,) + narrow, F32), shaped(narrow, BF16), shaped(narrow, F32), shaped((128, 1), F32),
+            shaped(narrow, F32), shaped(narrow, BF16), shaped((16, 1024), F32), shaped((16, 1024), F32),
+        ),
+        in_specs=[vmem, vmem, vmem, pl.BlockSpec(memory_space=pltpu.SMEM)] + [anywhere] * 6,
+        out_specs=(anywhere,) + (vmem,) * 15,
+        scratch_shapes=[
+            pltpu.VMEM((PIECES * 1024, 1024), BF16), pltpu.VMEM((PIECES * ROWS, 1024), BF16), pltpu.VMEM((32, 16, 128), BF16),
+            pltpu.VMEM((3, 128, 1024), BF16), pltpu.VMEM(heads, BF16), pltpu.VMEM(heads, jnp.int32),
+            dma((9,)), dma((PIECES,)), dma((12,)),
+        ] + gather_sems(PIECES) + gather_sems(1),
+        compiler_params=pltpu.CompilerParams(collective_id=0, has_side_effects=True, vmem_limit_bytes=VMEM_LIMIT),
+    )(tokens, cotangent, small, lens, *weights)
+
+
+def add_f32(left, right):
+    return left.astype(F32) + right.astype(F32)
+
+
+class Reducer:
+    stages = 7
+
+    def __init__(self, route, bufs, sems):
+        self.rt = route
+        (self.own, self.rb, self.ra, self.ru, self.rn, self.out) = bufs
+        (self.sb_s, self.sb_r, self.sa_s, self.sa_r, self.sz_s, self.su_r, self.sn_r) = sems
+
+    @staticmethod
+    def slot(xx, yy, zz):
+        return xx * 8 + zz * 2 + yy
+
+    def add(self, c, k, other):
+        self.own[c, k] = add_f32(self.own[c, k], other).astype(self.own.dtype)
+
+    def to_b(self, c):
+        rt = self.rt
+        for same_a in (0, 1):
+            for zz in range(4):
+                xx, yy = (rt.bx, rt.by) if same_a else (1 - rt.x, 1 - rt.y)
+                k = self.slot(xx, yy, zz)
+                remote(self.own.at[c, k], self.rb.at[c, same_a * 4 + zz], self.sb_s.at[c], self.sb_r.at[c], rt.b).start()
+
+    def to_a(self, c):
+        rt = self.rt
+        bytes_of(self.rb.at[c], self.sb_r.at[c]).wait()
+        for zz in range(4):
+            k = self.slot(rt.ax, rt.ay, zz)
+            self.add(c, k, self.rb[c, zz])
+            remote(self.own.at[c, k], self.ra.at[c, zz], self.sa_s.at[c], self.sa_r.at[c], rt.a).start()
+        for zz in range(4):
+            self.add(c, self.slot(rt.x, rt.y, zz), self.rb[c, 4 + zz])
+
+    def from_a(self, c):
+        rt = self.rt
+        bytes_of(self.ra.at[c], self.sa_r.at[c]).wait()
+        for zz in range(4):
+            self.add(c, self.slot(rt.x, rt.y, zz), self.ra[c, zz])
+
+    def along_z(self, c, hop):
+        rt = self.rt
+        x, y = rt.x, rt.y
+
+        @when(rt.z == hop)
+        def _():
+            for d in range(3, hop, -1):
+                k = self.slot(x, y, d)
+                if hop > 0:
+                    bytes_of(self.ru.at[c, d - 1], self.su_r.at[c, d - 1]).wait()
+                    self.add(c, k, self.ru[c, d - 1])
+                remote(self.own.at[c, k], self.ru.at[c, d - 1], self.sz_s.at[c, d], self.su_r.at[c, d - 1], rt.up).start()
+            if hop > 0:
+                bytes_of(self.ru.at[c, hop - 1], self.su_r.at[c, hop - 1]).wait()
+
+        at = 3 - hop
+
+        @when(rt.z == at)
+        def _():
+            for d in range(at):
+                k = self.slot(x, y, d)
+                if at < 3:
+                    bytes_of(self.rn.at[c, d], self.sn_r.at[c, d]).wait()
+                    self.add(c, k, self.rn[c, d])
+                remote(self.own.at[c, k], self.rn.at[c, d], self.sz_s.at[c, d], self.sn_r.at[c, d], rt.down).start()
+            if at < 3:
+                bytes_of(self.rn.at[c, at], self.sn_r.at[c, at]).wait()
+
+    def total(self, c):
+        rt = self.rt
+        k = self.slot(rt.x, rt.y, rt.z)
+
+        @when(rt.z == 0)
+        def _():
+            self.out[c] = add_f32(self.own[c, k], self.rn[c, 0])
+
+        @when(rt.z == 3)
+        def _():
+            self.out[c] = add_f32(self.own[c, k], self.ru[c, 2])
+
+        for at in (1, 2):
+
+            @when(rt.z == at)
+            def _():
+                self.out[c] = add_f32(self.own[c, k], self.ru[c, at - 1]) + self.rn[c, at].astype(F32)
+
+    def stage(self, s, c):
+        if s == 0:
+            self.to_b(c)
+        if s == 2:
+            self.to_a(c)
+        if s == 3:
+            self.from_a(c)
+        if s >= 3:
+            self.along_z(c, s - 3)
+        if s == 6:
+            self.total(c)
+
+    def finish(self, c):
+        rt = self.rt
+        bytes_of(self.rb.at[c], self.sb_s.at[c]).wait()
+        bytes_of(self.ra.at[c], self.sa_s.at[c]).wait()
+        for d in range(4):
+
+            @when(rt.z != d)
+            def _():
+                bytes_of(self.ra.at[c, 0], self.sz_s.at[c, d]).wait()
+
+
+def reducer_bufs(count, block, dtype):
+    return [pltpu.VMEM((count, n) + block, dtype) for n in (16, 8, 4, 3, 3)] + [pltpu.VMEM((count,) + block, F32)]
+
+
+def reducer_sems(count):
+    dma = pltpu.SemaphoreType.DMA
+    return [dma((count,))] * 4 + [dma((count, 4)), dma((count, 3)), dma((count, 3))]
+
+
+class Shared:
+    def __init__(self, route, ref, sems, at):
+        self.rt, self.ref, self.send, self.recv = route, ref, sems.at[2 * at], sems.at[2 * at + 1]
+
+    def give(self):
+        remote(self.ref.at[pl.ds(0, 128)], self.ref.at[pl.ds(128, 128)], self.send, self.recv, self.rt.sibling).start()
+
+    def wait(self):
+        bytes_of(self.ref.at[pl.ds(0, 128)], self.recv).wait()
+
+    def sent(self):
+        bytes_of(self.ref.at[pl.ds(0, 128)], self.send).wait()
+
+
+def backward_kernel(x_ref, att, qh, kh, vh, lse, act, pre, mid, nor1, inv1, gtwo, gffn, rows_in, table, len_ref, w,
+                    gin, sums, small_out,
+                    x2, att2, mid2, act2, gffn2, gpre2, gbr2, dq2, dk2, dv2, rows2, wbuf, gatt, doh, dqh, dk, dv, dkh, dvh,
+                    kseq, acc, w_sems, swap_sems, shared_sems, *rest):
+    rt, swap = Route(), Swap()
+    shift = 7 + swap.bucket
+    m_bufs, m_sems, v_bufs, v_sems = rest[:6], rest[6:13], rest[13:19], rest[19:26]
+    main, small = Reducer(rt, m_bufs, m_sems), Reducer(rt, v_bufs, v_sems)
+    own = m_bufs[0]
+    pairs = (x2, att2, mid2, act2, gffn2, gpre2, gbr2, dq2, dk2, dv2)
+    sx, satt, smid, sact, sgffn, sgpre, sgbr, sdq, sdk, sdv = (Shared(rt, ref, shared_sems, i) for i, ref in enumerate(pairs))
+
+    order = [4, 8, 5, 9, 6, 10, 7, 11, 3, 0, 1, 2]
+    slots = wbuf.shape[0]
+
+    def load(n):
+        return pltpu.make_async_copy(w.at[pl.ds(order[n] * 1024, 1024)], wbuf.at[n % slots], w_sems.at[n])
+
+    for n in range(slots):
+        load(n).start()
+    for ref, value in ((x2, x_ref), (att2, att), (mid2, mid), (act2, act), (gffn2, gffn)):
+        ref[0:128] = value[...]
+    rt.greet()
+    for one in (sgffn, sact, smid, satt, sx):
+        one.give()
+
+    def used(n):
+        if n + slots < PIECES:
+            load(n + slots).start()
+
+    def tall(left, right, first):
+        def one(i, _):
+            j = (i // 8) * 16 + rt.core * 8 + i % 8
+            part = left[:, pl.ds(pl.multiple_of(j * 128, 128), 128)]
+            grad = outer(part, right[...]).astype(BF16)
+            for q in range(4):
+                own[first + q, i] = grad[q * ROWS:(q + 1) * ROWS]
+            return 0
+
+        lax.fori_loop(0, 16, one, 0)
+
+    def square(left, right, c):
+        for xx in range(2):
+            part = left[:, pl.ds(pl.multiple_of((xx * 2 + rt.core) * 256, 256), 256)]
+            own[c, xx * 8:xx * 8 + 8] = outer(part, right).astype(BF16).reshape(8, ROWS, 1024)
+
+    def compute(c):
+        @when(c == 0)
+        def _():
+            sgffn.wait()
+            sact.wait()
+            tall(act2, gffn2, 0)
+
+        @when(c == 4)
+        def _():
+            sgpre.wait()
+            smid.wait()
+
+        @when((c >= 4) & (c < 8))
+        def _():
+            square(mid2, gpre2[:, pl.ds(pl.multiple_of((c - 4) * 1024, 1024), 1024)], c)
+
+        for k, (left, right, lw, rw) in enumerate(
+            ((att2, gbr2, satt, sgbr), (x2, dq2, sx, sdq), (x2, dk2, None, sdk), (x2, dv2, None, sdv))
+        ):
+
+            @when(c == 8 + k)
+            def _():
+                if lw is not None:
+                    lw.wait()
+                rw.wait()
+                square(left, right[...], c)
+
+    def compute_small():
+        bytes_of(rows2.at[1], shared_sems.at[21]).wait()
+        both = rows2[0] + rows2[1]
+        rows2[0] = both
+
+        def one(i, _):
+            j = (i // 8) * 16 + rt.core * 8 + i % 8
+            v_bufs[0][0, i, 0:8] = rows2[0, 0:8, pl.ds(pl.multiple_of((j // 4) * 128, 128), 128)]
+            ups = rows2[0, 8:16, pl.ds(pl.multiple_of((j % 8) * 128, 128), 128)]
+            row = lax.broadcasted_iota(jnp.int32, (8, 128), 0)
+            v_bufs[0][0, i, 8:16] = jnp.where(row == j // 8, ups, 0.0)
+            return 0
+
+        lax.fori_loop(0, 16, one, 0)
+
+    rows2[0] = rows_in[...]
+
+    def ffn_back(i):
+        load(2 * i).wait()
+        gact = inner(gffn2[0:128], wbuf[(2 * i) % slots]).astype(BF16).astype(F32)
+        used(2 * i)
+        gpre = (gact * gelu_slope(pre[i])).astype(BF16)
+        gpre2[0:128, i * 1024:(i + 1) * 1024] = gpre
+        rows2[0, V_UP + i:V_UP + i + 1] = column_sum(gpre.astype(F32))
+        load(2 * i + 1).wait()
+        part = inner(gpre, wbuf[(2 * i + 1) % slots])
+        used(2 * i + 1)
+        if i == 0:
+            acc[...] = part
+        else:
+            acc[...] += part
+
+    def ffn_end():
+        sgpre.give()
+        gmid = gtwo[...] + acc[...].astype(BF16).astype(F32)
+        normed1 = nor1[...]
+        rows2[0, V_GAIN1:V_GAIN1 + 1] = column_sum(gmid * normed1)
+        rows2[0, V_SHIFT1:V_SHIFT1 + 1] = column_sum(gmid)
+        gone = norm_back(gmid, normed1, inv1[...], table[V_GAIN1:V_GAIN1 + 1])
+        acc[...] = gone
+        gbr = gone.astype(BF16)
+        gbr2[0:128] = gbr
+        sgbr.give()
+        rows2[0, V_OUT:V_OUT + 1] = column_sum(gbr.astype(F32))
+        load(8).wait()
+        gatt[...] = inner(gbr, wbuf[8 % slots]).astype(BF16)
+        used(8)
+        swap.heads_out(gatt, doh, *(swap_sems.at[n] for n in range(3)))
+        kseq[...] = key_sequences(len_ref, shift, kseq.shape[0])
+        dk[...] = jnp.zeros_like(dk)
+        dv[...] = jnp.zeros_like(dv)
+
+    def score_back(first, count):
+        if first == 0:
+            swap.wait(doh, *(swap_sems.at[n] for n in range(3)))
+
+        def block(i, _):
+            attend_back_block(i, shift, kseq, qh, kh, vh, doh, lse, dqh, dk, dv)
+            return 0
+
+        lax.fori_loop(first, first + count, block, 0)
+
+    trio = ((dqh, dq2, sdq), (dkh, dk2, sdk), (dvh, dv2, sdv))
+
+    def score_end():
+        dkh[...] = dk[...].astype(BF16)
+        dvh[...] = dv[...].astype(BF16)
+        for i, (src, dst, _) in enumerate(trio):
+            swap.heads_back(src, dst.at[pl.ds(0, 128)], *(swap_sems.at[3 * i + 3 + n] for n in range(3)))
+
+    def exchange():
+        for i, (src, dst, shared) in enumerate(trio):
+            swap.wait(src, *(swap_sems.at[3 * i + 3 + n] for n in range(3)))
+            shared.give()
+        rows2[0, V_QUERY:V_QUERY + 1] = column_sum(dq2[0:128].astype(F32))
+        rows2[0, V_VALUE:V_VALUE + 1] = column_sum(dv2[0:128].astype(F32))
+        remote(rows2.at[0], rows2.at[1], shared_sems.at[20], shared_sems.at[21], rt.sibling).start()
+
+    def input_grad():
+        total = acc[...]
+        for i, ref in enumerate((dq2, dk2, dv2)):
+            load(9 + i).wait()
+            total = total + inner(ref[0:128], wbuf[(9 + i) % slots])
+        gin[...] = total
+        bytes_of(rows2.at[0], shared_sems.at[20]).wait()
+
+    items = {
+        0: (lambda: ffn_back(0), lambda: ffn_back(1)),
+        1: (lambda: ffn_back(2), lambda: ffn_back(3), ffn_end),
+        2: (lambda: score_back(0, 1),), 3: (lambda: score_back(1, 1),), 4: (lambda: score_back(2, 1),),
+        5: (lambda: score_back(3, 1), score_end),
+        7: (exchange,), 8: (input_grad,),
+    }
+
+    def step(t, _):
+        @when(t < PIECES)
+        def _():
+            compute(t)
+            main.stage(0, t)
+
+        @when(t == PIECES)
+        def _():
+            compute_small()
+            small.stage(0, 0)
+
+        for s in range(Reducer.stages - 1, 0, -1):
+            c = t - s
+
+            @when((c >= 0) & (c < PIECES))
+            def _():
+                main.stage(s, c)
+
+            @when(c == PIECES)
+            def _():
+                small.stage(s, 0)
+
+        for k, parts in items.items():
+
+            @when(t == k)
+            def _():
+                for part in parts:
+                    part()
+
+        return 0
+
+    lax.fori_loop(0, PIECES + Reducer.stages, step, 0)
+
+    def last(c, _):
+        main.finish(c)
+        return 0
+
+    lax.fori_loop(0, PIECES, last, 0)
+    small.finish(0)
+    for one in (sx, satt, smid, sact, sgffn, sgpre, sgbr, sdq, sdk, sdv):
+        one.sent()
+    sums[...] = m_bufs[5][...]
+    mine = v_bufs[5][0]
+    quarter = owner(rt.x, rt.y, rt.z, rt.core) % 4
+    picked = jnp.zeros((16, 32), F32)
+    for q in range(4):
+        picked = jnp.where(quarter == q, mine[:, q * 32:(q + 1) * 32], picked)
+    small_out[:, 0:128] = jnp.broadcast_to(column_sum(mine[8:16]), (16, 128))
+    small_out[:, 128:160] = picked
+
+
+def backward(tokens, kept, lens, weights):
+    vmem, anywhere = pl.BlockSpec(memory_space=pltpu.VMEM), pl.BlockSpec(memory_space=pl.ANY)
+    dma = pltpu.SemaphoreType.DMA
+    narrow, heads = (128, 1024), (1024, 128)
+    pair, wide_pair = pltpu.VMEM((256, 1024), BF16), pltpu.VMEM((256, 4096), BF16)
+    half, full = pltpu.VMEM(heads, BF16), pltpu.VMEM(heads, F32)
+    return pl.pallas_call(
+        backward_kernel,
+        out_shape=(shaped(narrow, F32), shaped((PIECES, ROWS, 1024), F32), shaped((16, 256), F32)),
+        in_specs=[vmem] * (1 + len(kept)) + [pl.BlockSpec(memory_space=pltpu.SMEM), anywhere],
+        out_specs=(vmem,) * 3,
+        scratch_shapes=[
+            pair, pair, pair, wide_pair, pair, wide_pair, pair, pair, pair, pair, pltpu.VMEM((2, 16, 1024), F32),
+            pltpu.VMEM((4, 1024, 1024), BF16), pltpu.VMEM(narrow, BF16), half, half, full, full, half, half,
+            pltpu.VMEM(heads, jnp.int32), pltpu.VMEM(narrow, F32), dma((PIECES,)), dma((12,)), dma((22,)),
+        ] + reducer_bufs(PIECES, (ROWS, 1024), BF16) + reducer_sems(PIECES)
+        + reducer_bufs(1, (16, 128), F32) + reducer_sems(1),
+        compiler_params=pltpu.CompilerParams(collective_id=1, has_side_effects=True, vmem_limit_bytes=VMEM_LIMIT),
+    )(tokens, *kept, lens, weights)
+
+
+def fast_body(hidden_in, lengths, w_query, w_key, w_value, b_query, b_value, w_out, b_out, first_gain, first_shift,
+              w_up, b_up, w_down, b_down, second_gain, second_shift, cotangent):
+    tokens = hidden_in.reshape(128, 1024)
+    me = lax.axis_index("bucket") * 8 + lax.axis_index("ctx")
+    rows = jnp.stack([b_query, b_value, b_out, first_gain, first_shift, b_down, second_gain, second_shift])
+    spread = jnp.concatenate([jnp.where(me % 4 == q, rows, jnp.zeros_like(rows)) for q in range(4)], axis=1)
+    small = jnp.concatenate([spread, b_up[None], jnp.zeros((7, 128), BF16)], axis=0)
+    lens = lengths.reshape(8)
+    (weights, att, qh, kh, vh, lse, hidden_out, act, pre, mid, nor1, inv1, gtwo, gffn, rows16, table) = forward(
+        tokens, cotangent.reshape(128, 1024), small, lens, (w_query, w_key, w_value, w_out, w_up, w_down)
+    )
+    grad_in, sums, small_sums = backward(
+        tokens, (att, qh, kh, vh, lse, act, pre, mid, nor1, inv1, gtwo, gffn, rows16, table), lens, weights
+    )
+    g_down = sums[:4].reshape(128, 1024)
+    g_up = jnp.concatenate([sums[4 + i] for i in range(4)], axis=1)
+    row = lambda r: small_sums[r, 128:160]
+    return (
+        hidden_out.reshape(hidden_in.shape), grad_in.reshape(hidden_in.shape), sums[9], sums[10], sums[11],
+        row(0), row(1), sums[8], row(2), row(3), row(4), g_up, small_sums[8, 0:128], g_down, row(5), row(6), row(7),
+    )
 
 
 def matmul(left, right):
@@ -55,11 +939,11 @@
     return (inv_std * inner, jnp.sum(incoming * normed, axis=0), jnp.sum(incoming, axis=0))
 
 
-def gelu_value(values):
+def plain_gelu_value(values):
     return 0.5 * values * (1.0 + jax.scipy.special.erf(values * 0.7071067811865476))
 
 
-def gelu_slope(values):
+def plain_gelu_slope(values):
     return (
         0.5 * (1.0 + jax.scipy.special.erf(values * 0.7071067811865476))
         + values * jnp.exp(-0.5 * values * values) * 0.3989422804014327
@@ -107,7 +991,7 @@
     return lax.fori_loop(0, turn_count, advance, running)
 
 
-def body(
+def general_body(
     hidden_in,
     lengths,
     w_query,
@@ -239,7 +1123,7 @@
     )
     middle_low = rounded(middle)
     pre_act = matmul(middle_low, up_mat) + widened(up_bias)
-    activated = rounded(gelu_value(pre_act))
+    activated = rounded(plain_gelu_value(pre_act))
     ffn_out = matmul(activated, down_mat) + widened(down_bias)
     result, normed_two, inv_two = norm_forward(
         middle + ffn_out, widened(gain_two), widened(shift_two)
@@ -278,7 +1162,7 @@
     grad_b_down = jnp.sum(widened(grad_ffn), axis=0)
     grad_w_down = row_inner(activated, grad_ffn)
     grad_act = widened(rounded(right_inner(grad_ffn, down_mat)))
-    grad_pre = rounded(grad_act * gelu_slope(pre_act))
+    grad_pre = rounded(grad_act * plain_gelu_slope(pre_act))
     grad_b_up = jnp.sum(widened(grad_pre), axis=0)
     grad_w_up = row_inner(middle_low, grad_pre)
     grad_middle = grad_two_sum + widened(rounded(right_inner(grad_pre, up_mat)))
@@ -409,6 +1293,11 @@
         P(("bucket", "ctx")),
         P("bucket", None, "ctx", None),
     )
+    def body(*arguments):
+        here = dict(mesh.shape) == {"bucket": 4, "ctx": 8}
+        shapes = arguments[0].shape == (1, 1, 128, 1024) and arguments[11].shape == (32, 4096)
+        return (fast_body if here and shapes else general_body)(*arguments)
+
     return jax.shard_map(
         body,
         mesh=mesh,

time: 1910 us -> 296 us (0.15)
  waiting for transfers between devices: 1480 us -> 0 us
  Pallas kernels: 0 us -> 283 us
  blocking collectives: 210 us -> 0 us
  matrix products: 121 us -> 0 us
  local copies, waits for them, and re-layouts: 63.1 us -> 9.2 us
    reduce_scatter x3 -> x0, waiting for transfers between devices: 860 us -> none  [the longest x1 360 us: body(): lax.psum_scatter(grad_w_down, ('bucket', 'ctx'), scatter_dimension=0, til...]
    all_gather x10 -> x0, waiting for transfers between devices: 323 us -> none  [the longest x1 76.9 us: body(): lax.all_gather(shards[9], ('bucket', 'ctx'), axis=0, tiled=True)]
    unnamed x19 -> x0, waiting for transfers between devices: 293 us -> none
    pallas_call x0 -> x2, Pallas kernels: none -> 283 us  [the longest x1 149 us: backward(): pl.pallas_call(backward_kernel, out_shape=(shaped(narrow, F32), shaped((P...]
    all_gather x3 -> x0, blocking collectives: 127 us -> none  [the longest x1 65.9 us: body(): lax.all_gather(shards[10], ('bucket', 'ctx'), axis=0, tiled=True)]
    dot_general x32 -> x0, matrix products: 121 us -> none  [the longest x6 27.8 us: row_inner(): lax.dot_general(left, right, (((0,), (0,)), ((), ())), preferred_element_...]
    unnamed x2 -> x0, blocking collectives: 82.9 us -> none
    unnamed x122 -> x6, local copies, waits for them, and re-layouts: 43.2 us -> 1.5 us
  transfers between devices with their start and end apart: 16 -> 0, of which waited for: 12 -> 0; matrix products, arithmetic and copies ran while one was open for 10% -> 0% of each run, Pallas kernels for 0% -> 0%
where the time goes in v2:
time: 296 us; the launch traced here: 295 us
  Pallas kernels  283 us (96%)
  local copies, waits for them, and re-layouts  9.2 us (3%)
    pallas_call x1, Pallas kernels, backward(): pl.pallas_call(backward_kernel, out_shape=(shaped(narrow, F32), shaped((P...  149 us
    pallas_call x1, Pallas kernels, forward(): pl.pallas_call(forward_kernel, out_shape=(shaped((PIECES * 1024, 1024), B...  134 us

profile of v2, /device:TPU:0, one launch (start us, length us, event | category | flops | bytes accessed | tf_op | source)
XLA Modules:
  0.0 295.3 jit_solution(8326045273782033735)
XLA Ops:
  0.7 0.1 pad.9.clone
  0.8 0.8 stack.35
  1.6 1.3 maximum_maximum_fusion.v_ref
  2.9 134.1 %shard_map.305 = (bf16[12288,1024]{1,0:T(8,128)(2,1)}, bf16[128,1024]{1,0:T(8,128)(2,1)}, bf16[1024,128]{1,0:T(8,128)(2,1)}, bf16[1024,128]{1,0:T(8,128)(2,1)}, ...) custom-call(bf16[128,1024]{1,0:T(8,128)(2,1)} %bitcast.49, ...), custom_call_target="tpu_custom_call" | custom-call | tf_op jit(solution)/shard_map/pallas_call | solution.py:483
  137.0 149.2 %shard_map.306 = (f32[128,1024]{1,0:T(8,128)}, f32[12,32,1024]{2,1,0:T(8,128)}, f32[16,256]{1,0:T(8,128)}) custom-call(bf16[128,1024]{1,0:T(8,128)(2,1)} %bitcast.50, bf16[128,1024]{1,0:T(8,128)(2,1)} %get-tuple-element.37.att, bf16[1024,128]{1,0:T(8,128)(2,1)} %get-tuple-element.38.qh, bf16[1024,128]{1,0:T(8,128)(2,1)} %get-tuple-element.39.kh, ...), custom_call_target="tpu_custom_call" | custom-call | tf_op jit(solution)/shard_map/pallas_call | solution.py:861
  286.2 1.2 slice_bitcast_fusion.11
  287.3 1.5 slice_bitcast_fusion.8
  288.9 0.0 copy-start.1
  288.9 1.9 slice.68
  290.8 0.0 copy-start
  290.8 2.2 slice_bitcast_fusion.3
  293.0 0.8 pad_maximum_fusion
  293.8 0.0 copy-done.1
  293.8 0.7 copy.37
  294.5 0.0 copy-done
  294.5 0.8 copy.38
  (2 shorter events, 0.0 us)
Async XLA Ops:
  288.9 5.0 %copy-start.1 = (bf16[128,1024]{1,0:T(8,128)(2,1)S(1)}, bf16[128,1024]{1,0:T(8,128)(2,1)}, u32[]{:S(2)}) copy-start(bf16[128,1024]{1,0:T(8,128)(2,1)} %get-tuple-element.36) | copy-start | bytes 786436
  290.8 3.7 %copy-start = (f32[128,1024]{1,0:T(8,128)S(1)}, f32[128,1024]{1,0:T(8,128)}, u32[]{:S(2)}) copy-start(f32[128,1024]{1,0:T(8,128)} %get-tuple-element.52) | copy-start | bytes 1572868

commit v3 on v2

--- a/solution.py
+++ b/solution.py
@@ -14,7 +14,7 @@
 F32, BF16 = jnp.float32, jnp.bfloat16
 ROWS = 32
 PIECES = 12
-VMEM_LIMIT = 62 * 2**20
+VMEM_LIMIT = 63 * 2**20
 
 
 def when(condition):
@@ -45,23 +45,32 @@
     return pltpu.make_async_copy(ref, ref, sem)
 
 
+class Roles:
+    def __init__(self, route, b_along_x):
+        x, y, z, core = route.x, route.y, route.z, route.core
+        self.ax, self.ay = jnp.where(b_along_x, x, 1 - x), jnp.where(b_along_x, 1 - y, y)
+        self.bx, self.by = jnp.where(b_along_x, 1 - x, x), jnp.where(b_along_x, y, 1 - y)
+        self.a = device(self.ax, self.ay, z, core)
+        self.b = device(self.bx, self.by, z, core)
+
+
 class Route:
     def __init__(self):
         self.x, self.y, self.z, self.core = x, y, z, core = place()
-        self.ax, self.ay = jnp.where(core == 0, 1 - x, x), jnp.where(core == 0, y, 1 - y)
-        self.bx, self.by = jnp.where(core == 1, 1 - x, x), jnp.where(core == 1, y, 1 - y)
-        self.a = device(self.ax, self.ay, z, core)
-        self.b = device(self.bx, self.by, z, core)
+        self.across = (device(1 - x, y, z, core), device(x, 1 - y, z, core))
         self.sibling = device(x, y, z, 1 - core)
         self.up = device(x, y, jnp.minimum(z + 1, 3), core)
         self.down = device(x, y, jnp.maximum(z - 1, 0), core)
+
+    def roles(self, turned):
+        return Roles(self, (self.core == 1) | turned)
 
     def greet(self):
         z = self.z
         bucket, ctx = lax.axis_index("bucket"), lax.axis_index("ctx")
         barrier = pltpu.get_barrier_semaphore()
         pack = [(bucket, (ctx + off) % 8) for off in range(1, 8)]
-        for target in [self.a, self.b, self.sibling] + pack:
+        for target in [*self.across, self.sibling] + pack:
             pl.semaphore_signal(barrier, inc=1, device_id=target, device_id_type=MESH_ID)
 
         @when(z < 3)
@@ -75,31 +84,54 @@
         pl.semaphore_wait(barrier, 10 + (z < 3).astype(jnp.int32) + (z > 0).astype(jnp.int32))
 
 
+class Plan:
+    def __init__(self, count, mixed, turned):
+        self.count, self.which_mixed, self.which_turned = count, mixed, turned
+
+    def mixed(self, c):
+        return self.member(c, self.which_mixed)
+
+    def turned(self, c):
+        return self.member(c, self.which_turned)
+
+    @staticmethod
+    def member(c, items):
+        hit = jnp.bool_(False)
+        for item in items:
+            hit = hit | (c == item)
+        return hit
+
+
 class Gatherer:
     stages = 7
 
-    def __init__(self, route, count, own, block, span, sems):
-        self.rt, self.count, self.own, self.block, self.span = route, count, own, block, span
+    def __init__(self, route, plan, own, block, span, sems):
+        self.rt, self.plan, self.own, self.block, self.span = route, plan, own, block, span
         (self.zs, self.zr, self.ps, self.ar, self.br, self.dr, self.ls) = sems
 
-    def spread(self, c, src, j, jz, to_a, to_b, z_dirs):
+    def spread(self, c, src, j, jz, ro, to_a, to_b, z_dirs):
         rt, dst = self.rt, self.block(c, j)
-        if "up" in z_dirs:
+        which, directions = z_dirs
+        if "up" in directions:
 
             @when(rt.z < 3)
             def _():
-                remote(src, dst, self.zs.at[0, c, jz], self.zr.at[c, jz], rt.up).start()
-
-        if "down" in z_dirs:
+                remote(src, dst, self.zs.at[0, c, which, jz], self.zr.at[c, which, jz], rt.up).start()
+
+        if "down" in directions:
 
             @when(rt.z > 0)
             def _():
-                remote(src, dst, self.zs.at[1, c, jz], self.zr.at[c, jz], rt.down).start()
-
-        if to_a:
-            remote(src, dst, self.ps, self.ar.at[c, jz], rt.a).start()
+                remote(src, dst, self.zs.at[1, c, which, jz], self.zr.at[c, which, jz], rt.down).start()
+
         if to_b is not None:
-            remote(src, dst, self.ps, self.br.at[c, to_b * 4 + jz], rt.b).start()
+            remote(src, dst, self.ps, self.br.at[c, to_b * 4 + jz], ro.b).start()
+        if to_a is not None:
+
+            @when(to_a)
+            def _():
+                remote(src, dst, self.ps, self.ar.at[c, jz], ro.a).start()
+
         remote(src, dst, self.ps, self.dr.at[c], rt.sibling).start()
 
     def near(self, k, action):
@@ -111,49 +143,78 @@
                 action(zz, "up" if sign < 0 else "down")
 
     def own_stage(self, c):
-        rt = self.rt
+        rt, ro = self.rt, self.rt.roles(self.plan.turned(c))
         j = owner(rt.x, rt.y, rt.z, rt.core)
         pltpu.make_async_copy(self.own(c), self.block(c, j), self.ls.at[c]).start()
-        self.spread(c, self.own(c), j, rt.z, True, 0, ("up", "down"))
+        self.spread(c, self.own(c), j, rt.z, ro, jnp.bool_(True), 0, (0, ("up", "down")))
 
     def z_stage(self, c, k):
-        rt = self.rt
+        rt, ro = self.rt, self.rt.roles(self.plan.turned(c))
 
         def action(zz, direction):
             j = owner(rt.x, rt.y, zz, rt.core)
-            bytes_of(self.block(c, j), self.zr.at[c, zz]).wait()
-            self.spread(c, self.block(c, j), j, zz, True, 0, (direction,))
+            bytes_of(self.block(c, j), self.zr.at[c, 0, zz]).wait()
+            self.spread(c, self.block(c, j), j, zz, ro, ~self.plan.mixed(c), 0, (0, (direction,)))
 
         self.near(k, action)
 
-    def a_stage(self, c, k):
-        rt = self.rt
+    def z_stage_of_a(self, c, k):
+        rt, ro = self.rt, self.rt.roles(self.plan.turned(c))
+
+        def action(zz, direction):
+            j = owner(ro.ax, ro.ay, zz, rt.core)
+            bytes_of(self.block(c, j), self.zr.at[c, 1, zz]).wait()
+            self.spread(c, self.block(c, j), j, zz, ro, None, 1, (1, (direction,)))
+
+        self.near(k, action)
+
+    def a_stage(self, c, k, directions=()):
+        rt, ro = self.rt, self.rt.roles(self.plan.turned(c))
 
         def action(zz, _):
-            j = owner(rt.ax, rt.ay, zz, rt.core)
+            j = owner(ro.ax, ro.ay, zz, rt.core)
             bytes_of(self.block(c, j), self.ar.at[c, zz]).wait()
-            self.spread(c, self.block(c, j), j, zz, False, 1, ())
+            self.spread(c, self.block(c, j), j, zz, ro, None, 1, (1, directions))
 
         self.near(k, action)
 
     def b_stage(self, c, k):
-        rt = self.rt
+        rt, ro = self.rt, self.rt.roles(self.plan.turned(c))
 
         def action(zz, _):
-            for which, (xx, yy) in enumerate(((rt.bx, rt.by), (1 - rt.x, 1 - rt.y))):
+            for which, (xx, yy) in enumerate(((ro.bx, ro.by), (1 - rt.x, 1 - rt.y))):
                 j = owner(xx, yy, zz, rt.core)
                 bytes_of(self.block(c, j), self.br.at[c, which * 4 + zz]).wait()
-                self.spread(c, self.block(c, j), j, zz, False, None, ())
+                self.spread(c, self.block(c, j), j, zz, ro, None, None, (0, ()))
 
         self.near(k, action)
 
     def stage(self, s, c):
+        mixed = self.plan.mixed(c)
         if s == 0:
             self.own_stage(c)
         if 1 <= s <= 3:
             self.z_stage(c, s)
-        if 2 <= s <= 5:
-            self.a_stage(c, s - 2)
+        if s == 1:
+
+            @when(mixed)
+            def _():
+                self.a_stage(c, 0, ("up", "down"))
+
+            @when(~mixed)
+            def _():
+                self.a_stage(c, 0)
+
+        if 2 <= s <= 4:
+
+            @when(mixed)
+            def _():
+                self.z_stage_of_a(c, s - 1)
+
+            @when(~mixed)
+            def _():
+                self.a_stage(c, s - 1)
+
         if 3 <= s <= 6:
             self.b_stage(c, s - 3)
 
@@ -162,24 +223,32 @@
         bytes_of(self.span(1), self.ls.at[c]).wait()
 
     def finish(self):
-        bytes_of(self.span(28 * self.count), self.ps).wait()
+        bytes_of(self.span(28 * self.plan.count - 3 * len(self.plan.which_mixed)), self.ps).wait()
 
     def finish_z(self, c):
         rt = self.rt
-        for zz in range(4):
-
-            @when((rt.z < 3) & (rt.z >= zz))
-            def _():
-                bytes_of(self.span(1), self.zs.at[0, c, zz]).wait()
-
-            @when((rt.z > 0) & (rt.z <= zz))
-            def _():
-                bytes_of(self.span(1), self.zs.at[1, c, zz]).wait()
+
+        def sent(which):
+            for zz in range(4):
+
+                @when((rt.z < 3) & (rt.z >= zz))
+                def _():
+                    bytes_of(self.span(1), self.zs.at[0, c, which, zz]).wait()
+
+                @when((rt.z > 0) & (rt.z <= zz))
+                def _():
+                    bytes_of(self.span(1), self.zs.at[1, c, which, zz]).wait()
+
+        sent(0)
+
+        @when(self.plan.mixed(c))
+        def _():
+            sent(1)
 
 
 def gather_sems(count):
     dma = pltpu.SemaphoreType.DMA
-    return [dma((2, count, 4)), dma((count, 4)), dma(()), dma((count, 4)), dma((count, 8)), dma((count,)), dma((count,))]
+    return [dma((2, count, 2, 4)), dma((count, 2, 4)), dma(()), dma((count, 4)), dma((count, 8)), dma((count,)), dma((count,))]
 
 
 def outer(left, right):
@@ -327,6 +396,9 @@
 V_QUERY, V_VALUE, V_OUT, V_GAIN1, V_SHIFT1, V_DOWN, V_GAIN2, V_SHIFT2 = range(8)
 V_UP = 8
 W_DOWN, W_UP = 4096, 8192
+GATHER = Plan(PIECES, (1, 2, 4, 5, 7, 8, 10, 11), (2,))
+REDUCE = Plan(PIECES, (0, 1, 3, 4, 6, 7, 9, 10), (7,))
+ONE_PIECE = Plan(1, (), ())
 
 
 def piece_row(c, j):
@@ -334,25 +406,269 @@
     return pl.multiple_of(jnp.where(tall, W_DOWN + 128 * j + ROWS * (c - 4), c * 1024 + ROWS * j), ROWS)
 
 
-def forward_kernel(x_ref, cot_ref, v_ref, len_ref, wq, wk, wv, wo, wu, wd,
-                   w_out, att, qh, kh, vh, lse, hid, act, pre, mid, nor1, inv1, gtwo, gffn, rows, table,
-                   w, own, tiles, qkv, oh, kseq, own_sems, out_sems, swap_sems, *sems):
+def add_f32(left, right):
+    return left.astype(F32) + right.astype(F32)
+
+
+class Reducer:
+    stages = 7
+
+    def __init__(self, route, plan, own, rb, ra, ru, rn, out, sems):
+        self.rt, self.plan = route, plan
+        self.own, self.rb, self.ra, self.ru, self.rn, self.out = own, rb, ra, ru, rn, out
+        (self.sb_s, self.sb_r, self.sa_s, self.sa_r, self.sz_s, self.su_r, self.sn_r) = sems
+
+    @staticmethod
+    def slot(xx, yy, zz):
+        return xx * 8 + zz * 2 + yy
+
+    def add(self, c, k, other):
+        at = self.own(c, k)
+        at[...] = add_f32(at[...], other).astype(at.dtype)
+
+    def roles(self, c):
+        return self.rt.roles(self.plan.turned(c))
+
+    def b_blocks(self, c):
+        rt, ro = self.rt, self.roles(c)
+        blocks = []
+        for same_a in (0, 1):
+            for zz in range(4):
+                xx, yy = (ro.bx, ro.by) if same_a else (1 - rt.x, 1 - rt.y)
+                blocks.append((self.slot(xx, yy, zz), same_a * 4 + zz))
+        return blocks
+
+    def send_b(self, c, k, at):
+        remote(self.own(c, k), self.rb.at[c, at], self.sb_s.at[c], self.sb_r.at[c], self.roles(c).b).start()
+
+    def to_b(self, c):
+        for k, at in self.b_blocks(c):
+            self.send_b(c, k, at)
+
+    def from_b(self, c):
+        bytes_of(self.rb.at[c], self.sb_r.at[c]).wait()
+
+    def to_a(self, c):
+        rt, ro = self.rt, self.roles(c)
+        for zz in range(4):
+            k = self.slot(ro.ax, ro.ay, zz)
+            self.add(c, k, self.rb[c, zz])
+            remote(self.own(c, k), self.ra(c, zz), self.sa_s.at[c], self.sa_r.at[c], ro.a).start()
+        for zz in range(4):
+            self.add(c, self.slot(rt.x, rt.y, zz), self.rb[c, 4 + zz])
+
+    def keep_b(self, c):
+        rt, ro = self.rt, self.roles(c)
+        for zz in range(4):
+            self.add(c, self.slot(ro.ax, ro.ay, zz), self.rb[c, zz])
+            self.add(c, self.slot(rt.x, rt.y, zz), self.rb[c, 4 + zz])
+
+    def from_a(self, c):
+        rt = self.rt
+        bytes_of(self.rb.at[c, pl.ds(0, 4)], self.sa_r.at[c]).wait()
+        for zz in range(4):
+            self.add(c, self.slot(rt.x, rt.y, zz), self.ra(c, zz)[...])
+
+    def along_z(self, c, hop, which):
+        rt, ro = self.rt, self.roles(c)
+        x, y = (ro.ax, ro.ay) if which else (rt.x, rt.y)
+
+        @when(rt.z == hop)
+        def _():
+            for d in range(3, hop, -1):
+                k = self.slot(x, y, d)
+                at, sem = self.ru(c, which, d - 1), self.su_r.at[c, which, d - 1]
+                if hop > 0:
+                    bytes_of(at, sem).wait()
+                    self.add(c, k, at[...])
+                remote(self.own(c, k), at, self.sz_s.at[c, which, d], sem, rt.up).start()
+            if hop > 0:
+                bytes_of(self.ru(c, which, hop - 1), self.su_r.at[c, which, hop - 1]).wait()
+
+        end = 3 - hop
+
+        @when(rt.z == end)
+        def _():
+            for d in range(end):
+                k = self.slot(x, y, d)
+                at, sem = self.rn(c, which, d), self.sn_r.at[c, which, d]
+                if end < 3:
+                    bytes_of(at, sem).wait()
+                    self.add(c, k, at[...])
+                remote(self.own(c, k), at, self.sz_s.at[c, which, d], sem, rt.down).start()
+            if end < 3:
+                bytes_of(self.rn(c, which, end), self.sn_r.at[c, which, end]).wait()
+
+    def sum_z(self, c, which, store):
+        rt, ro = self.rt, self.roles(c)
+        k = self.slot(ro.ax, ro.ay, rt.z) if which else self.slot(rt.x, rt.y, rt.z)
+
+        @when(rt.z == 0)
+        def _():
+            store(k, add_f32(self.own(c, k)[...], self.rn(c, which, 0)[...]))
+
+        @when(rt.z == 3)
+        def _():
+            store(k, add_f32(self.own(c, k)[...], self.ru(c, which, 2)[...]))
+
+        for at in (1, 2):
+
+            @when(rt.z == at)
+            def _():
+                store(k, add_f32(self.own(c, k)[...], self.ru(c, which, at - 1)[...]) + self.rn(c, which, at)[...].astype(F32))
+
+    def close_a(self, c):
+        ro = self.roles(c)
+
+        def store(k, value):
+            at = self.own(c, k)
+            at[...] = value.astype(at.dtype)
+
+        self.sum_z(c, 1, store)
+        k = self.slot(ro.ax, ro.ay, self.rt.z)
+        remote(self.own(c, k), self.ra(c, 0), self.sa_s.at[c], self.sa_r.at[c], ro.a).start()
+
+    def total(self, c, from_a):
+        def store(k, value):
+            if from_a:
+                bytes_of(self.ra(c, 0), self.sa_r.at[c]).wait()
+                value = value + self.ra(c, 0)[...].astype(F32)
+            self.out[c] = value
+
+        self.sum_z(c, 0, store)
+
+    def stage(self, s, c):
+        mixed = self.plan.mixed(c)
+        if s == 0:
+            self.to_b(c)
+        if s == 2:
+            self.from_b(c)
+
+        if s >= 2:
+
+            @when(mixed)
+            def _():
+                if s == 2:
+                    self.keep_b(c)
+                if s <= 5:
+                    self.along_z(c, s - 2, 1)
+                    self.along_z(c, s - 2, 0)
+                if s == 5:
+                    self.close_a(c)
+                if s == 6:
+                    self.total(c, True)
+
+            @when(~mixed)
+            def _():
+                if s == 2:
+                    self.to_a(c)
+                if s == 3:
+                    self.from_a(c)
+                if s >= 3:
+                    self.along_z(c, s - 3, 0)
+                if s == 6:
+                    self.total(c, False)
+
+    def finish(self, c):
+        rt = self.rt
+        bytes_of(self.rb.at[c], self.sb_s.at[c]).wait()
+
+        def sent(which):
+            for d in range(4):
+
+                @when(rt.z != d)
+                def _():
+                    bytes_of(self.ra(c, 0), self.sz_s.at[c, which, d]).wait()
+
+        sent(0)
+
+        @when(self.plan.mixed(c))
+        def _():
+            sent(1)
+            bytes_of(self.ra(c, 0), self.sa_s.at[c]).wait()
+
+        @when(~self.plan.mixed(c))
+        def _():
+            bytes_of(self.rb.at[c, pl.ds(0, 4)], self.sa_s.at[c]).wait()
+
+
+def reducer_sems(count):
+    dma = pltpu.SemaphoreType.DMA
+    return [dma((count,))] * 4 + [dma((count, 2, 4)), dma((count, 2, 3)), dma((count, 2, 3))]
+
+
+class Shared:
+    def __init__(self, route, ref, sems, at, start=0):
+        cols = pl.ds(start, 1024)
+        self.rt, self.mine, self.other = route, ref.at[pl.ds(0, 128), cols], ref.at[pl.ds(128, 128), cols]
+        self.send, self.recv = sems.at[0, at], sems.at[1, at]
+
+    def give(self):
+        remote(self.mine, self.other, self.send, self.recv, self.rt.sibling).start()
+
+    def wait(self):
+        bytes_of(self.mine, self.recv).wait()
+
+    def sent(self):
+        bytes_of(self.mine, self.send).wait()
+
+
+OFFSETS = (0, 0, 2, 3, 4, 5, 6)
+
+
+def layer_kernel(x_ref, cot_ref, v_ref, len_ref, wq, wk, wv, wo, wu, wd,
+                 kept, hid, gin, sums, small_out,
+                 w, own, tiles, qkv, oh, kseq, qh, kh, vh, doh, lse, pre, nor1, inv1, gtwo, dk, dv, table, rows2,
+                 x2, att2, mid2, act2, gffn2, gpre2, gbr2, dq2, dk2, dv2,
+                 rb, ra, ru, rn, v_own, v_rb, v_ra, v_ru, v_rn, v_out,
+                 own_sems, kept_sems, swap_sems, shared_sems, row_sems, *sems):
     rt, swap = Route(), Swap()
     shift = 7 + swap.bucket
+    g_sems, gv_sems, r_sems, rv_sems = sems[:7], sems[7:14], sems[14:21], sems[21:28]
     loads = [pltpu.make_async_copy(ref, own.at[pl.ds(i * ROWS, ROWS)], own_sems.at[i]) for i, ref in enumerate((wq, wk, wv, wo))]
     loads.append(pltpu.make_async_copy(wd, own.at[pl.ds(4 * ROWS, 4 * ROWS)], own_sems.at[4]))
     for i in range(4):
         loads.append(pltpu.make_async_copy(wu.at[:, pl.ds(i * 1024, 1024)], own.at[pl.ds((8 + i) * ROWS, ROWS)], own_sems.at[5 + i]))
+    loads.append(pltpu.make_async_copy(x_ref, x2.at[pl.ds(0, 128)], own_sems.at[9]))
     for load in loads:
         load.start()
-    main = Gatherer(
-        rt, PIECES,
+    gather = Gatherer(
+        rt, GATHER,
         lambda c: own.at[pl.ds(pl.multiple_of(c * ROWS, ROWS), ROWS)],
         lambda c, j: w.at[pl.ds(piece_row(c, j), ROWS)],
         lambda n: w.at[pl.ds(0, n * ROWS)],
-        sems[:7],
-    )
-    small = Gatherer(rt, 1, lambda c: v_ref, lambda c, j: tiles.at[j], lambda n: tiles.at[pl.ds(0, n)], sems[7:])
+        g_sems,
+    )
+    gather_small = Gatherer(rt, ONE_PIECE, lambda c: v_ref, lambda c, j: tiles.at[j], lambda n: tiles.at[pl.ds(0, n)], gv_sems)
+
+    def own_block(c, k):
+        first = jnp.where(c < 6, c * 512, W_DOWN + (c - 6) * 512)
+        return w.at[pl.ds(pl.multiple_of(first + k * ROWS, ROWS), ROWS)]
+
+    def third(c):
+        return c // 3, c % 3
+
+    def ra_block(c, i):
+        n, m = third(c)
+        return ra.at[n * 6 + m + i]
+
+    def z_block(ref):
+        def place_of(c, which, d):
+            n, m = third(c)
+            return ref.at[n * 15 + m * 6 + which * 3 + d]
+
+        return place_of
+
+    reduce = Reducer(rt, REDUCE, own_block, rb, ra_block, z_block(ru), z_block(rn), sums, r_sems)
+    reduce_small = Reducer(
+        rt, ONE_PIECE, lambda c, k: v_own.at[k], v_rb, lambda c, i: v_ra.at[i],
+        lambda c, which, d: v_ru.at[d], lambda c, which, d: v_rn.at[d], v_out, rv_sems,
+    )
+    sx, satt, smid, sgffn, sgbr, sdq, sdk, sdv = (
+        Shared(rt, ref, shared_sems, i) for i, ref in enumerate((x2, att2, mid2, gffn2, gbr2, dq2, dk2, dv2))
+    )
+    sact = [Shared(rt, act2, shared_sems, 8 + i, i * 1024) for i in range(4)]
+    sgpre = [Shared(rt, gpre2, shared_sems, 12 + i, i * 1024) for i in range(4)]
     for load in loads:
         load.wait()
     rt.greet()
@@ -360,16 +676,20 @@
     def vec(row):
         return table[row:row + 1]
 
+    def trio(at):
+        return tuple(swap_sems.at[3 * at + n] for n in range(3))
+
     def project(i):
-        value = dense(x_ref[...], w[i * 1024:(i + 1) * 1024])
+        value = dense(x2[0:128], w[i * 1024:(i + 1) * 1024])
         if i != 1:
             value = value + vec(V_QUERY if i == 0 else V_VALUE)
         qkv[i] = value.astype(BF16)
-        swap.heads_out(qkv.at[i], (qh, kh, vh)[i], *(swap_sems.at[3 * i + n] for n in range(3)))
+        swap.heads_out(qkv.at[i], (qh, kh, vh)[i], *trio(i))
 
     def start():
-        small.arrived(0)
-        table[0:16] = table_of(tiles)
+        gather_small.arrived(0)
+        sx.give()
+        table[...] = table_of(tiles)
         for i in range(4):
             table[V_UP + i:V_UP + i + 1] = jnp.concatenate([tiles[8 * i + j][8:9].astype(F32) for j in range(8)], axis=1)
         kseq[...] = key_sequences(len_ref, shift, kseq.shape[0])
@@ -378,7 +698,7 @@
     def score(first):
         if first == 0:
             for i, ref in enumerate((qh, kh, vh)):
-                swap.wait(ref, *(swap_sems.at[3 * i + n] for n in range(3)))
+                swap.wait(ref, *trio(i))
 
         def block(i, _):
             attend_block(i, shift, kseq, qh, kh, vh, oh, lse)
@@ -386,21 +706,24 @@
 
         lax.fori_loop(first, first + 2, block, 0)
         if first == 2:
-            swap.heads_back(oh, att, *(swap_sems.at[9 + n] for n in range(3)))
+            swap.heads_back(oh, att2.at[pl.ds(0, 128)], *trio(3))
 
     def first_norm():
-        swap.wait(oh, *(swap_sems.at[9 + n] for n in range(3)))
-        normed, inv = norm_parts(x_ref[...].astype(F32) + (dense(att[...], w[3072:4096]) + vec(V_OUT)))
+        swap.wait(oh, *trio(3))
+        satt.give()
+        normed, inv = norm_parts(x2[0:128].astype(F32) + (dense(att2[0:128], w[3072:4096]) + vec(V_OUT)))
         nor1[...] = normed
         inv1[...] = inv
-        mid[...] = (normed * vec(V_GAIN1) + vec(V_SHIFT1)).astype(BF16)
+        mid2[0:128] = (normed * vec(V_GAIN1) + vec(V_SHIFT1)).astype(BF16)
+        smid.give()
         gtwo[...] = jnp.zeros_like(gtwo)
 
     def up(i):
-        value = dense(mid[...], w[W_UP + i * 1024:W_UP + (i + 1) * 1024]) + vec(V_UP + i)
+        value = dense(mid2[0:128], w[W_UP + i * 1024:W_UP + (i + 1) * 1024]) + vec(V_UP + i)
         pre[i] = value
         now = gelu_value(value).astype(BF16)
-        act[:, i * 1024:(i + 1) * 1024] = now
+        act2[0:128, i * 1024:(i + 1) * 1024] = now
+        sact[i].give()
         gtwo[...] += dense(now, w[W_DOWN + i * 1024:W_DOWN + (i + 1) * 1024])
 
     items = {
@@ -410,35 +733,30 @@
 
     def save(i):
         rows_of = pl.ds(pl.multiple_of(i * 1024, 1024), 1024)
-        return pltpu.make_async_copy(w.at[rows_of], w_out.at[rows_of], out_sems.at[i])
-
-    def step(t, _):
+        return pltpu.make_async_copy(w.at[rows_of], kept.at[rows_of], kept_sems.at[i])
+
+    def gather_step(t, _):
         for s in range(Gatherer.stages):
             c = t - s
 
             @when(c == 0)
             def _():
-                small.stage(s, 0)
+                gather_small.stage(s, 0)
 
             @when((c >= 0) & (c < PIECES))
             def _():
-                main.stage(s, c)
+                gather.stage(s, c)
 
         c = t - Gatherer.stages
 
         @when(c >= 0)
         def _():
-            main.arrived(c)
-
-            @when((c < 4) | (c >= 8))
+            gather.arrived(c)
+
+            @when(c < 3)
             def _():
                 save(c).start()
 
-            @when(c == 7)
-            def _():
-                for i in range(4, 8):
-                    save(i).start()
-
         for k, item in items.items():
 
             @when(t == k)
@@ -447,250 +765,76 @@
 
         return 0
 
-    lax.fori_loop(0, PIECES + Gatherer.stages, step, 0)
+    lax.fori_loop(0, PIECES + Gatherer.stages, gather_step, 0)
     middle = nor1[...] * vec(V_GAIN1) + vec(V_SHIFT1)
     normed2, inv2 = norm_parts(middle + (gtwo[...] + vec(V_DOWN)))
+    g = cot_ref[...].astype(F32)
+    back = norm_back(g, normed2, inv2, vec(V_GAIN2))
+    low = back.astype(BF16)
+    gffn2[0:128] = low
+    sgffn.give()
+    gtwo[...] = back
     hid[...] = (normed2 * vec(V_GAIN2) + vec(V_SHIFT2)).astype(BF16)
-    g = cot_ref[...].astype(F32)
-    rows[...] = jnp.zeros_like(rows)
-    rows[V_GAIN2:V_GAIN2 + 1] = column_sum(g * normed2)
-    rows[V_SHIFT2:V_SHIFT2 + 1] = column_sum(g)
-    back = norm_back(g, normed2, inv2, vec(V_GAIN2))
-    gtwo[...] = back
-    low = back.astype(BF16)
-    gffn[...] = low
-    rows[V_DOWN:V_DOWN + 1] = column_sum(low.astype(F32))
-    small.finish()
-    small.finish_z(0)
-
-    def last(c, _):
-        main.finish_z(c)
-        save(c).wait()
+    rows2[0] = jnp.zeros(table.shape, F32)
+    rows2[0, V_GAIN2:V_GAIN2 + 1] = column_sum(g * normed2)
+    rows2[0, V_SHIFT2:V_SHIFT2 + 1] = column_sum(g)
+    rows2[0, V_DOWN:V_DOWN + 1] = column_sum(low.astype(F32))
+    gather_small.finish()
+    gather_small.finish_z(0)
+
+    def gathered(c, _):
+        gather.finish_z(c)
         return 0
 
-    lax.fori_loop(0, PIECES, last, 0)
-    main.finish()
-
-
-def shaped(shape, dtype):
-    return jax.ShapeDtypeStruct(shape, dtype)
-
-
-def forward(tokens, cotangent, small, lens, weights):
-    vmem, anywhere = pl.BlockSpec(memory_space=pltpu.VMEM), pl.BlockSpec(memory_space=pl.ANY)
-    dma = pltpu.SemaphoreType.DMA
-    narrow, wide, heads = (128, 1024), (128, 4096), (1024, 128)
-    return pl.pallas_call(
-        forward_kernel,
-        out_shape=(
-            shaped((PIECES * 1024, 1024), BF16), shaped(narrow, BF16), shaped(heads, BF16), shaped(heads, BF16),
-            shaped(heads, BF16), shaped((2, 1024), F32), shaped(narrow, BF16), shaped(wide, BF16),
-            shaped((4,) + narrow, F32), shaped(narrow, BF16), shaped(narrow, F32), shaped((128, 1), F32),
-            shaped(narrow, F32), shaped(narrow, BF16), shaped((16, 1024), F32), shaped((16, 1024), F32),
-        ),
-        in_specs=[vmem, vmem, vmem, pl.BlockSpec(memory_space=pltpu.SMEM)] + [anywhere] * 6,
-        out_specs=(anywhere,) + (vmem,) * 15,
-        scratch_shapes=[
-            pltpu.VMEM((PIECES * 1024, 1024), BF16), pltpu.VMEM((PIECES * ROWS, 1024), BF16), pltpu.VMEM((32, 16, 128), BF16),
-            pltpu.VMEM((3, 128, 1024), BF16), pltpu.VMEM(heads, BF16), pltpu.VMEM(heads, jnp.int32),
-            dma((9,)), dma((PIECES,)), dma((12,)),
-        ] + gather_sems(PIECES) + gather_sems(1),
-        compiler_params=pltpu.CompilerParams(collective_id=0, has_side_effects=True, vmem_limit_bytes=VMEM_LIMIT),
-    )(tokens, cotangent, small, lens, *weights)
-
-
-def add_f32(left, right):
-    return left.astype(F32) + right.astype(F32)
-
-
-class Reducer:
-    stages = 7
-
-    def __init__(self, route, bufs, sems):
-        self.rt = route
-        (self.own, self.rb, self.ra, self.ru, self.rn, self.out) = bufs
-        (self.sb_s, self.sb_r, self.sa_s, self.sa_r, self.sz_s, self.su_r, self.sn_r) = sems
-
-    @staticmethod
-    def slot(xx, yy, zz):
-        return xx * 8 + zz * 2 + yy
-
-    def add(self, c, k, other):
-        self.own[c, k] = add_f32(self.own[c, k], other).astype(self.own.dtype)
-
-    def to_b(self, c):
-        rt = self.rt
+    lax.fori_loop(0, PIECES, gathered, 0)
+    gather.finish()
+    for i in range(3):
+        save(i).wait()
+
+    def tall(first):
+        order = [(k, at) for k, at in reduce.b_blocks(first)]
+        kept_here = []
         for same_a in (0, 1):
             for zz in range(4):
-                xx, yy = (rt.bx, rt.by) if same_a else (1 - rt.x, 1 - rt.y)
-                k = self.slot(xx, yy, zz)
-                remote(self.own.at[c, k], self.rb.at[c, same_a * 4 + zz], self.sb_s.at[c], self.sb_r.at[c], rt.b).start()
-
-    def to_a(self, c):
-        rt = self.rt
-        bytes_of(self.rb.at[c], self.sb_r.at[c]).wait()
-        for zz in range(4):
-            k = self.slot(rt.ax, rt.ay, zz)
-            self.add(c, k, self.rb[c, zz])
-            remote(self.own.at[c, k], self.ra.at[c, zz], self.sa_s.at[c], self.sa_r.at[c], rt.a).start()
-        for zz in range(4):
-            self.add(c, self.slot(rt.x, rt.y, zz), self.rb[c, 4 + zz])
-
-    def from_a(self, c):
-        rt = self.rt
-        bytes_of(self.ra.at[c], self.sa_r.at[c]).wait()
-        for zz in range(4):
-            self.add(c, self.slot(rt.x, rt.y, zz), self.ra[c, zz])
-
-    def along_z(self, c, hop):
-        rt = self.rt
-        x, y = rt.x, rt.y
-
-        @when(rt.z == hop)
-        def _():
-            for d in range(3, hop, -1):
-                k = self.slot(x, y, d)
-                if hop > 0:
-                    bytes_of(self.ru.at[c, d - 1], self.su_r.at[c, d - 1]).wait()
-                    self.add(c, k, self.ru[c, d - 1])
-                remote(self.own.at[c, k], self.ru.at[c, d - 1], self.sz_s.at[c, d], self.su_r.at[c, d - 1], rt.up).start()
-            if hop > 0:
-                bytes_of(self.ru.at[c, hop - 1], self.su_r.at[c, hop - 1]).wait()
-
-        at = 3 - hop
-
-        @when(rt.z == at)
-        def _():
-            for d in range(at):
-                k = self.slot(x, y, d)
-                if at < 3:
-                    bytes_of(self.rn.at[c, d], self.sn_r.at[c, d]).wait()
-                    self.add(c, k, self.rn[c, d])
-                remote(self.own.at[c, k], self.rn.at[c, d], self.sz_s.at[c, d], self.sn_r.at[c, d], rt.down).start()
-            if at < 3:
-                bytes_of(self.rn.at[c, at], self.sn_r.at[c, at]).wait()
-
-    def total(self, c):
-        rt = self.rt
-        k = self.slot(rt.x, rt.y, rt.z)
-
-        @when(rt.z == 0)
-        def _():
-            self.out[c] = add_f32(self.own[c, k], self.rn[c, 0])
-
-        @when(rt.z == 3)
-        def _():
-            self.out[c] = add_f32(self.own[c, k], self.ru[c, 2])
-
-        for at in (1, 2):
-
-            @when(rt.z == at)
-            def _():
-                self.out[c] = add_f32(self.own[c, k], self.ru[c, at - 1]) + self.rn[c, at].astype(F32)
-
-    def stage(self, s, c):
-        if s == 0:
-            self.to_b(c)
-        if s == 2:
-            self.to_a(c)
-        if s == 3:
-            self.from_a(c)
-        if s >= 3:
-            self.along_z(c, s - 3)
-        if s == 6:
-            self.total(c)
-
-    def finish(self, c):
-        rt = self.rt
-        bytes_of(self.rb.at[c], self.sb_s.at[c]).wait()
-        bytes_of(self.ra.at[c], self.sa_s.at[c]).wait()
-        for d in range(4):
-
-            @when(rt.z != d)
-            def _():
-                bytes_of(self.ra.at[c, 0], self.sz_s.at[c, d]).wait()
-
-
-def reducer_bufs(count, block, dtype):
-    return [pltpu.VMEM((count, n) + block, dtype) for n in (16, 8, 4, 3, 3)] + [pltpu.VMEM((count,) + block, F32)]
-
-
-def reducer_sems(count):
-    dma = pltpu.SemaphoreType.DMA
-    return [dma((count,))] * 4 + [dma((count, 4)), dma((count, 3)), dma((count, 3))]
-
-
-class Shared:
-    def __init__(self, route, ref, sems, at):
-        self.rt, self.ref, self.send, self.recv = route, ref, sems.at[2 * at], sems.at[2 * at + 1]
-
-    def give(self):
-        remote(self.ref.at[pl.ds(0, 128)], self.ref.at[pl.ds(128, 128)], self.send, self.recv, self.rt.sibling).start()
-
-    def wait(self):
-        bytes_of(self.ref.at[pl.ds(0, 128)], self.recv).wait()
-
-    def sent(self):
-        bytes_of(self.ref.at[pl.ds(0, 128)], self.send).wait()
-
-
-def backward_kernel(x_ref, att, qh, kh, vh, lse, act, pre, mid, nor1, inv1, gtwo, gffn, rows_in, table, len_ref, w,
-                    gin, sums, small_out,
-                    x2, att2, mid2, act2, gffn2, gpre2, gbr2, dq2, dk2, dv2, rows2, wbuf, gatt, doh, dqh, dk, dv, dkh, dvh,
-                    kseq, acc, w_sems, swap_sems, shared_sems, *rest):
-    rt, swap = Route(), Swap()
-    shift = 7 + swap.bucket
-    m_bufs, m_sems, v_bufs, v_sems = rest[:6], rest[6:13], rest[13:19], rest[19:26]
-    main, small = Reducer(rt, m_bufs, m_sems), Reducer(rt, v_bufs, v_sems)
-    own = m_bufs[0]
-    pairs = (x2, att2, mid2, act2, gffn2, gpre2, gbr2, dq2, dk2, dv2)
-    sx, satt, smid, sact, sgffn, sgpre, sgbr, sdq, sdk, sdv = (Shared(rt, ref, shared_sems, i) for i, ref in enumerate(pairs))
-
-    order = [4, 8, 5, 9, 6, 10, 7, 11, 3, 0, 1, 2]
-    slots = wbuf.shape[0]
-
-    def load(n):
-        return pltpu.make_async_copy(w.at[pl.ds(order[n] * 1024, 1024)], wbuf.at[n % slots], w_sems.at[n])
-
-    for n in range(slots):
-        load(n).start()
-    for ref, value in ((x2, x_ref), (att2, att), (mid2, mid), (act2, act), (gffn2, gffn)):
-        ref[0:128] = value[...]
-    rt.greet()
-    for one in (sgffn, sact, smid, satt, sx):
-        one.give()
-
-    def used(n):
-        if n + slots < PIECES:
-            load(n + slots).start()
-
-    def tall(left, right, first):
-        def one(i, _):
-            j = (i // 8) * 16 + rt.core * 8 + i % 8
-            part = left[:, pl.ds(pl.multiple_of(j * 128, 128), 128)]
-            grad = outer(part, right[...]).astype(BF16)
+                ro = reduce.roles(first)
+                xx, yy = (rt.x, rt.y) if same_a else (ro.ax, ro.ay)
+                kept_here.append(reduce.slot(xx, yy, zz))
+
+        def block(k):
+            j = (k // 8) * 16 + rt.core * 8 + k % 8
+            part = act2[:, pl.ds(pl.multiple_of(j * 128, 128), 128)]
+            grad = outer(part, gffn2[...]).astype(BF16)
             for q in range(4):
-                own[first + q, i] = grad[q * ROWS:(q + 1) * ROWS]
-            return 0
-
-        lax.fori_loop(0, 16, one, 0)
+                own_block(first + q, k)[...] = grad[q * ROWS:(q + 1) * ROWS]
+
+        for k, at in order:
+            block(k)
+            for q in range(4):
+                reduce.send_b(first + q, k, at)
+        for k in kept_here:
+            block(k)
 
     def square(left, right, c):
         for xx in range(2):
             part = left[:, pl.ds(pl.multiple_of((xx * 2 + rt.core) * 256, 256), 256)]
-            own[c, xx * 8:xx * 8 + 8] = outer(part, right).astype(BF16).reshape(8, ROWS, 1024)
+            grad = outer(part, right).astype(BF16)
+            for i in range(8):
+                own_block(c, xx * 8 + i)[...] = grad[i * ROWS:(i + 1) * ROWS]
 
     def compute(c):
         @when(c == 0)
         def _():
-            sgffn.wait()
-            sact.wait()
-            tall(act2, gffn2, 0)
-
-        @when(c == 4)
-        def _():
-            sgpre.wait()
-            smid.wait()
+            for one in sact + [sgffn]:
+                one.wait()
+            tall(0)
+
+        for i in range(4):
+
+            @when(c == 4 + i)
+            def _():
+                if i == 0:
+                    smid.wait()
+                sgpre[i].wait()
 
         @when((c >= 4) & (c < 8))
         def _():
@@ -707,123 +851,125 @@
                 rw.wait()
                 square(left, right[...], c)
 
+        @when(c >= 4)
+        def _():
+            reduce.to_b(c)
+
+    def share_rows():
+        return remote(rows2.at[0], rows2.at[1], row_sems.at[0], row_sems.at[1], rt.sibling)
+
     def compute_small():
-        bytes_of(rows2.at[1], shared_sems.at[21]).wait()
-        both = rows2[0] + rows2[1]
-        rows2[0] = both
+        bytes_of(rows2.at[1], row_sems.at[1]).wait()
+        rows2[0] = rows2[0] + rows2[1]
 
         def one(i, _):
             j = (i // 8) * 16 + rt.core * 8 + i % 8
-            v_bufs[0][0, i, 0:8] = rows2[0, 0:8, pl.ds(pl.multiple_of((j // 4) * 128, 128), 128)]
+            v_own[i, 0:8] = rows2[0, 0:8, pl.ds(pl.multiple_of((j // 4) * 128, 128), 128)]
             ups = rows2[0, 8:16, pl.ds(pl.multiple_of((j % 8) * 128, 128), 128)]
             row = lax.broadcasted_iota(jnp.int32, (8, 128), 0)
-            v_bufs[0][0, i, 8:16] = jnp.where(row == j // 8, ups, 0.0)
+            v_own[i, 8:16] = jnp.where(row == j // 8, ups, 0.0)
             return 0
 
         lax.fori_loop(0, 16, one, 0)
 
-    rows2[0] = rows_in[...]
-
     def ffn_back(i):
-        load(2 * i).wait()
-        gact = inner(gffn2[0:128], wbuf[(2 * i) % slots]).astype(BF16).astype(F32)
-        used(2 * i)
+        gact = inner(gffn2[0:128], w[W_DOWN + i * 1024:W_DOWN + (i + 1) * 1024]).astype(BF16).astype(F32)
         gpre = (gact * gelu_slope(pre[i])).astype(BF16)
         gpre2[0:128, i * 1024:(i + 1) * 1024] = gpre
+        sgpre[i].give()
         rows2[0, V_UP + i:V_UP + i + 1] = column_sum(gpre.astype(F32))
-        load(2 * i + 1).wait()
-        part = inner(gpre, wbuf[(2 * i + 1) % slots])
-        used(2 * i + 1)
+        part = inner(gpre, w[W_UP + i * 1024:W_UP + (i + 1) * 1024])
         if i == 0:
-            acc[...] = part
+            gin[...] = part
         else:
-            acc[...] += part
+            gin[...] += part
+
+    def load(i):
+        return pltpu.make_async_copy(kept.at[pl.ds(i * 1024, 1024)], w.at[pl.ds(W_UP + i * 1024, 1024)], kept_sems.at[i])
 
     def ffn_end():
-        sgpre.give()
-        gmid = gtwo[...] + acc[...].astype(BF16).astype(F32)
+        for i in range(3):
+            load(i).start()
+        gmid = gtwo[...] + gin[...].astype(BF16).astype(F32)
         normed1 = nor1[...]
+        gone = norm_back(gmid, normed1, inv1[...], vec(V_GAIN1))
+        gbr = gone.astype(BF16)
+        gbr2[0:128] = gbr
+        qkv[0] = inner(gbr, w[3072:4096]).astype(BF16)
+        swap.heads_out(qkv.at[0], doh, *trio(4))
+        gin[...] = gone
+        sgbr.give()
         rows2[0, V_GAIN1:V_GAIN1 + 1] = column_sum(gmid * normed1)
         rows2[0, V_SHIFT1:V_SHIFT1 + 1] = column_sum(gmid)
-        gone = norm_back(gmid, normed1, inv1[...], table[V_GAIN1:V_GAIN1 + 1])
-        acc[...] = gone
-        gbr = gone.astype(BF16)
-        gbr2[0:128] = gbr
-        sgbr.give()
         rows2[0, V_OUT:V_OUT + 1] = column_sum(gbr.astype(F32))
-        load(8).wait()
-        gatt[...] = inner(gbr, wbuf[8 % slots]).astype(BF16)
-        used(8)
-        swap.heads_out(gatt, doh, *(swap_sems.at[n] for n in range(3)))
-        kseq[...] = key_sequences(len_ref, shift, kseq.shape[0])
         dk[...] = jnp.zeros_like(dk)
         dv[...] = jnp.zeros_like(dv)
 
     def score_back(first, count):
         if first == 0:
-            swap.wait(doh, *(swap_sems.at[n] for n in range(3)))
+            swap.wait(doh, *trio(4))
 
         def block(i, _):
-            attend_back_block(i, shift, kseq, qh, kh, vh, doh, lse, dqh, dk, dv)
+            attend_back_block(i, shift, kseq, qh, kh, vh, doh, lse, qh, dk, dv)
             return 0
 
         lax.fori_loop(first, first + count, block, 0)
 
-    trio = ((dqh, dq2, sdq), (dkh, dk2, sdk), (dvh, dv2, sdv))
+    back_trio = ((qh, dq2, sdq), (kh, dk2, sdk), (vh, dv2, sdv))
 
     def score_end():
-        dkh[...] = dk[...].astype(BF16)
-        dvh[...] = dv[...].astype(BF16)
-        for i, (src, dst, _) in enumerate(trio):
-            swap.heads_back(src, dst.at[pl.ds(0, 128)], *(swap_sems.at[3 * i + 3 + n] for n in range(3)))
+        kh[...] = dk[...].astype(BF16)
+        vh[...] = dv[...].astype(BF16)
+        for i, (src, dst, _) in enumerate(back_trio):
+            swap.heads_back(src, dst.at[pl.ds(0, 128)], *trio(5 + i))
 
     def exchange():
-        for i, (src, dst, shared) in enumerate(trio):
-            swap.wait(src, *(swap_sems.at[3 * i + 3 + n] for n in range(3)))
+        for i, (src, dst, shared) in enumerate(back_trio):
+            swap.wait(src, *trio(5 + i))
             shared.give()
         rows2[0, V_QUERY:V_QUERY + 1] = column_sum(dq2[0:128].astype(F32))
         rows2[0, V_VALUE:V_VALUE + 1] = column_sum(dv2[0:128].astype(F32))
-        remote(rows2.at[0], rows2.at[1], shared_sems.at[20], shared_sems.at[21], rt.sibling).start()
+        share_rows().start()
 
     def input_grad():
-        total = acc[...]
+        total = gin[...]
         for i, ref in enumerate((dq2, dk2, dv2)):
-            load(9 + i).wait()
-            total = total + inner(ref[0:128], wbuf[(9 + i) % slots])
+            load(i).wait()
+            total = total + inner(ref[0:128], w[W_UP + i * 1024:W_UP + (i + 1) * 1024])
         gin[...] = total
-        bytes_of(rows2.at[0], shared_sems.at[20]).wait()
-
-    items = {
-        0: (lambda: ffn_back(0), lambda: ffn_back(1)),
+        share_rows().wait_send()
+
+    back_items = {
+        0: (lambda: ffn_back(1),),
         1: (lambda: ffn_back(2), lambda: ffn_back(3), ffn_end),
         2: (lambda: score_back(0, 1),), 3: (lambda: score_back(1, 1),), 4: (lambda: score_back(2, 1),),
         5: (lambda: score_back(3, 1), score_end),
         7: (exchange,), 8: (input_grad,),
     }
-
-    def step(t, _):
+    ffn_back(0)
+
+    def reduce_step(t, _):
         @when(t < PIECES)
         def _():
             compute(t)
-            main.stage(0, t)
 
         @when(t == PIECES)
         def _():
             compute_small()
-            small.stage(0, 0)
-
-        for s in range(Reducer.stages - 1, 0, -1):
-            c = t - s
+            reduce_small.to_b(0)
+
+        for s in range(Reducer.stages - 1, 1, -1):
+            c = t - OFFSETS[s]
 
             @when((c >= 0) & (c < PIECES))
             def _():
-                main.stage(s, c)
+                reduce.stage(s, c)
 
             @when(c == PIECES)
             def _():
-                small.stage(s, 0)
-
-        for k, parts in items.items():
+                reduce_small.stage(s, 0)
+
+        for k, parts in back_items.items():
 
             @when(t == k)
             def _():
@@ -832,18 +978,17 @@
 
         return 0
 
-    lax.fori_loop(0, PIECES + Reducer.stages, step, 0)
-
-    def last(c, _):
-        main.finish(c)
+    lax.fori_loop(0, PIECES + 1 + OFFSETS[-1], reduce_step, 0)
+
+    def reduced(c, _):
+        reduce.finish(c)
         return 0
 
-    lax.fori_loop(0, PIECES, last, 0)
-    small.finish(0)
-    for one in (sx, satt, smid, sact, sgffn, sgpre, sgbr, sdq, sdk, sdv):
+    lax.fori_loop(0, PIECES, reduced, 0)
+    reduce_small.finish(0)
+    for one in [sx, satt, smid, sgffn, sgbr, sdq, sdk, sdv] + sact + sgpre:
         one.sent()
-    sums[...] = m_bufs[5][...]
-    mine = v_bufs[5][0]
+    mine = v_out[0]
     quarter = owner(rt.x, rt.y, rt.z, rt.core) % 4
     picked = jnp.zeros((16, 32), F32)
     for q in range(4):
@@ -852,25 +997,72 @@
     small_out[:, 128:160] = picked
 
 
-def backward(tokens, kept, lens, weights):
+def shaped(shape, dtype):
+    return jax.ShapeDtypeStruct(shape, dtype)
+
+
+def layer(tokens, cotangent, small, lens, weights):
     vmem, anywhere = pl.BlockSpec(memory_space=pltpu.VMEM), pl.BlockSpec(memory_space=pl.ANY)
     dma = pltpu.SemaphoreType.DMA
     narrow, heads = (128, 1024), (1024, 128)
-    pair, wide_pair = pltpu.VMEM((256, 1024), BF16), pltpu.VMEM((256, 4096), BF16)
     half, full = pltpu.VMEM(heads, BF16), pltpu.VMEM(heads, F32)
+    pair, wide_pair, tokens_f32 = pltpu.VMEM((256, 1024), BF16), pltpu.VMEM((256, 4096), BF16), pltpu.VMEM(narrow, F32)
+
+    def blocks(*n):
+        return pltpu.VMEM(n + (ROWS, 1024), BF16)
+
+    def tiles(*n):
+        return pltpu.VMEM(n + (16, 128), F32)
+
     return pl.pallas_call(
-        backward_kernel,
-        out_shape=(shaped(narrow, F32), shaped((PIECES, ROWS, 1024), F32), shaped((16, 256), F32)),
-        in_specs=[vmem] * (1 + len(kept)) + [pl.BlockSpec(memory_space=pltpu.SMEM), anywhere],
-        out_specs=(vmem,) * 3,
+        layer_kernel,
+        out_shape=(
+            shaped((3 * 1024, 1024), BF16), shaped(narrow, BF16), shaped(narrow, F32),
+            shaped((PIECES, ROWS, 1024), F32), shaped((16, 256), F32),
+        ),
+        in_specs=[anywhere, vmem, vmem, pl.BlockSpec(memory_space=pltpu.SMEM)] + [anywhere] * 6,
+        out_specs=(anywhere,) + (vmem,) * 4,
         scratch_shapes=[
-            pair, pair, pair, wide_pair, pair, wide_pair, pair, pair, pair, pair, pltpu.VMEM((2, 16, 1024), F32),
-            pltpu.VMEM((4, 1024, 1024), BF16), pltpu.VMEM(narrow, BF16), half, half, full, full, half, half,
-            pltpu.VMEM(heads, jnp.int32), pltpu.VMEM(narrow, F32), dma((PIECES,)), dma((12,)), dma((22,)),
-        ] + reducer_bufs(PIECES, (ROWS, 1024), BF16) + reducer_sems(PIECES)
-        + reducer_bufs(1, (16, 128), F32) + reducer_sems(1),
-        compiler_params=pltpu.CompilerParams(collective_id=1, has_side_effects=True, vmem_limit_bytes=VMEM_LIMIT),
-    )(tokens, *kept, lens, weights)
+            pltpu.VMEM((PIECES * 1024, 1024), BF16), pltpu.VMEM((PIECES * ROWS, 1024), BF16), pltpu.VMEM((32, 16, 128), BF16),
+            pltpu.VMEM((3, 128, 1024), BF16), half, pltpu.VMEM(heads, jnp.int32), half, half, half, half,
+            pltpu.VMEM((2, 1024), F32), pltpu.VMEM((4, 128, 1024), F32), tokens_f32, pltpu.VMEM((128, 1), F32), tokens_f32,
+            full, full, pltpu.VMEM((16, 1024), F32), pltpu.VMEM((2, 16, 1024), F32),
+            pair, pair, pair, wide_pair, pair, wide_pair, pair, pair, pair, pair,
+            blocks(PIECES, 8), blocks(24), blocks(60), blocks(60),
+            tiles(16), tiles(1, 8), tiles(4), tiles(3), tiles(3), tiles(1),
+            dma((10,)), dma((3,)), dma((24,)), dma((2, 16)), dma((2,)),
+        ] + gather_sems(PIECES) + gather_sems(1) + reducer_sems(PIECES) + reducer_sems(1),
+        compiler_params=pltpu.CompilerParams(collective_id=0, has_side_effects=True, vmem_limit_bytes=VMEM_LIMIT),
+    )(tokens, cotangent, small, lens, *weights)
+
+
+def unpack_kernel(sums, small, hid, gin, *outs):
+    (o_hid, o_gin, o_q, o_k, o_v, o_bq, o_bv, o_o, o_bo, o_g1, o_s1, o_up, o_bup, o_down, o_bdown, o_g2, o_s2) = outs
+    o_hid[...] = hid[...]
+    o_gin[...] = gin[...]
+    for ref, c in ((o_q, 9), (o_k, 10), (o_v, 11), (o_o, 8)):
+        ref[...] = sums[c]
+    for i in range(4):
+        o_down[i * ROWS:(i + 1) * ROWS] = sums[i]
+        o_up[:, i * 1024:(i + 1) * 1024] = sums[4 + i]
+    for i, ref in enumerate((o_bq, o_bv, o_bo, o_g1, o_s1, o_bdown, o_g2, o_s2)):
+        ref[...] = small[i, 128:160]
+    o_bup[...] = small[8, 0:128]
+
+
+def unpack(sums, small, hid, gin):
+    vmem = pl.BlockSpec(memory_space=pltpu.VMEM)
+    block, vector = shaped((ROWS, 1024), F32), shaped((32,), F32)
+    return pl.pallas_call(
+        unpack_kernel,
+        out_shape=(
+            shaped(hid.shape, BF16), shaped(gin.shape, F32), block, block, block, vector, vector, block, vector, vector, vector,
+            shaped((ROWS, 4096), F32), shaped((128,), F32), shaped((128, 1024), F32), vector, vector, vector,
+        ),
+        in_specs=[vmem] * 4,
+        out_specs=(vmem,) * 17,
+        compiler_params=pltpu.CompilerParams(vmem_limit_bytes=VMEM_LIMIT),
+    )(sums, small, hid, gin)
 
 
 def fast_body(hidden_in, lengths, w_query, w_key, w_value, b_query, b_value, w_out, b_out, first_gain, first_shift,
@@ -880,20 +1072,11 @@
     rows = jnp.stack([b_query, b_value, b_out, first_gain, first_shift, b_down, second_gain, second_shift])
     spread = jnp.concatenate([jnp.where(me % 4 == q, rows, jnp.zeros_like(rows)) for q in range(4)], axis=1)
     small = jnp.concatenate([spread, b_up[None], jnp.zeros((7, 128), BF16)], axis=0)
-    lens = lengths.reshape(8)
-    (weights, att, qh, kh, vh, lse, hidden_out, act, pre, mid, nor1, inv1, gtwo, gffn, rows16, table) = forward(
-        tokens, cotangent.reshape(128, 1024), small, lens, (w_query, w_key, w_value, w_out, w_up, w_down)
-    )
-    grad_in, sums, small_sums = backward(
-        tokens, (att, qh, kh, vh, lse, act, pre, mid, nor1, inv1, gtwo, gffn, rows16, table), lens, weights
-    )
-    g_down = sums[:4].reshape(128, 1024)
-    g_up = jnp.concatenate([sums[4 + i] for i in range(4)], axis=1)
-    row = lambda r: small_sums[r, 128:160]
-    return (
-        hidden_out.reshape(hidden_in.shape), grad_in.reshape(hidden_in.shape), sums[9], sums[10], sums[11],
-        row(0), row(1), sums[8], row(2), row(3), row(4), g_up, small_sums[8, 0:128], g_down, row(5), row(6), row(7),
-    )
+    _, hidden_out, grad_in, sums, small_sums = layer(
+        tokens, cotangent.reshape(128, 1024), small, lengths.reshape(8), (w_query, w_key, w_value, w_out, w_up, w_down)
+    )
+    outs = unpack(sums, small_sums, hidden_out, grad_in)
+    return (outs[0].reshape(hidden_in.shape), outs[1].reshape(hidden_in.shape)) + tuple(outs[2:])
 
 
 def matmul(left, right):

time: 296 us -> 272 us (0.919)
  Pallas kernels: 283 us -> 269 us
  local copies, waits for them, and re-layouts: 9.2 us -> 0.87 us
    pallas_call x2, Pallas kernels: 283 us -> 269 us  [the longest x1 266 us: layer(): pl.pallas_call(layer_kernel, out_shape=(shaped((3 * 1024, 1024), BF16), s...]
    squeeze x3 -> x0, local copies, waits for them, and re-layouts: 4.89 us -> none  [the longest x1 2.19 us: fast_body(): g_up = jnp.concatenate([sums[4 + i] for i in range(4)], axis=1)]
where the time goes in v3:
time: 272 us
  Pallas kernels  269 us (99%)
    pallas_call x1, Pallas kernels, layer(): pl.pallas_call(layer_kernel, out_shape=(shaped((3 * 1024, 1024), BF16), s...  266 us

profile of v3, /device:TPU:0, one launch (start us, length us, event | category | flops | bytes accessed | tf_op | source)
XLA Modules:
  0.0 271.9 jit_solution(7189164085022393751)
XLA Ops:
  0.7 0.1 pad.5.clone
  0.8 0.8 stack.35
  1.6 1.3 maximum_maximum_fusion.v_ref
  2.9 265.7 %shard_map.305 = (bf16[3072,1024]{1,0:T(8,128)(2,1)}, bf16[128,1024]{1,0:T(8,128)(2,1)}, f32[128,1024]{1,0:T(8,128)}, f32[12,32,1024]{2,1,0:T(8,128)}, f32[16,256]{1,0:T(8,128)}) custom-call(bf16[128,1024]{1,0:T(8,128)(2,1)} %bitcast.14, bf16[128,1024]{1,0:T(8,128)(2,1)} %bitcast.15, bf16[16,128]{1,0:T(8,128)(2,1)} %maximum_maximum_fusion.v_ref, s32[8]{0:T(128)} %bitcast.16, ...), custom_call_target="tpu_custom_call" | custom-call | tf_op jit(solution)/shard_map/pallas_call | solution.py:1017
  268.6 3.1 %shard_map.306 = (bf16[128,1024]{1,0:T(8,128)(2,1)}, f32[128,1024]{1,0:T(8,128)}, f32[32,1024]{1,0:T(8,128)}, f32[32,1024]{1,0:T(8,128)}, f32[32,1024]{1,0:T(8,1...) custom-call(f32[12,32,1024]{2,1,0:T(8,128)} %get-tuple-element.38.su, ...), custom_call_target="tpu_custom_call" | custom-call | tf_op jit(solution)/shard_map/pallas_call | solution.py:1056
  (2 shorter events, 0.0 us)

commit v4 on v3

--- a/solution.py
+++ b/solution.py
@@ -94,6 +94,9 @@
     def turned(self, c):
         return self.member(c, self.which_turned)
 
+    def mixed_before(self, c):
+        return sum((c > item).astype(jnp.int32) for item in self.which_mixed)
+
     @staticmethod
     def member(c, items):
         hit = jnp.bool_(False)
@@ -112,6 +115,11 @@
     def spread(self, c, src, j, jz, ro, to_a, to_b, z_dirs):
         rt, dst = self.rt, self.block(c, j)
         which, directions = z_dirs
+        if "line" in directions:
+            for slot in range(3):
+                target = device(rt.x, rt.y, (rt.z + slot + 1) % 4, rt.core)
+                remote(src, dst, self.zs.at[0, c, which, slot], self.zr.at[c, which, jz], target).start()
+
         if "up" in directions:
 
             @when(rt.z < 3)
@@ -146,7 +154,16 @@
         rt, ro = self.rt, self.rt.roles(self.plan.turned(c))
         j = owner(rt.x, rt.y, rt.z, rt.core)
         pltpu.make_async_copy(self.own(c), self.block(c, j), self.ls.at[c]).start()
-        self.spread(c, self.own(c), j, rt.z, ro, jnp.bool_(True), 0, (0, ("up", "down")))
+        mixed = self.plan.mixed(c)
+
+        @when(mixed)
+        def _():
+            self.spread(c, self.own(c), j, rt.z, ro, jnp.bool_(True), 0, (0, ("up", "down")))
+
+        @when(~mixed)
+        def _():
+            self.spread(c, self.own(c), j, rt.z, ro, jnp.bool_(True), 0, (0, ("line",)))
+
 
     def z_stage(self, c, k):
         rt, ro = self.rt, self.rt.roles(self.plan.turned(c))
@@ -154,7 +171,15 @@
         def action(zz, direction):
             j = owner(rt.x, rt.y, zz, rt.core)
             bytes_of(self.block(c, j), self.zr.at[c, 0, zz]).wait()
-            self.spread(c, self.block(c, j), j, zz, ro, ~self.plan.mixed(c), 0, (0, (direction,)))
+
+            @when(self.plan.mixed(c))
+            def _():
+                self.spread(c, self.block(c, j), j, zz, ro, None, 0, (0, (direction,)))
+
+            @when(~self.plan.mixed(c))
+            def _():
+                self.spread(c, self.block(c, j), j, zz, ro, jnp.bool_(True), 0, (0, ()))
+
 
         self.near(k, action)
 
@@ -239,11 +264,15 @@
                 def _():
                     bytes_of(self.span(1), self.zs.at[1, c, which, zz]).wait()
 
-        sent(0)
-
         @when(self.plan.mixed(c))
         def _():
+            sent(0)
             sent(1)
+
+        @when(~self.plan.mixed(c))
+        def _():
+            for slot in range(3):
+                bytes_of(self.span(1), self.zs.at[0, c, 0, slot]).wait()
 
 
 def gather_sems(count):
@@ -396,8 +425,8 @@
 V_QUERY, V_VALUE, V_OUT, V_GAIN1, V_SHIFT1, V_DOWN, V_GAIN2, V_SHIFT2 = range(8)
 V_UP = 8
 W_DOWN, W_UP = 4096, 8192
-GATHER = Plan(PIECES, (1, 2, 4, 5, 7, 8, 10, 11), (2,))
-REDUCE = Plan(PIECES, (0, 1, 3, 4, 6, 7, 9, 10), (7,))
+GATHER = Plan(PIECES, (1, 3, 4, 6, 8, 10), (4,))
+REDUCE = Plan(PIECES, (1, 3, 6, 9), (6,))
 ONE_PIECE = Plan(1, (), ())
 
 
@@ -439,35 +468,50 @@
         return blocks
 
     def send_b(self, c, k, at):
-        remote(self.own(c, k), self.rb.at[c, at], self.sb_s.at[c], self.sb_r.at[c], self.roles(c).b).start()
+        remote(self.own(c, k), self.rb.at[c, at], self.sb_s.at[c], self.sb_r.at[c, at], self.roles(c).b).start()
 
     def to_b(self, c):
         for k, at in self.b_blocks(c):
             self.send_b(c, k, at)
 
-    def from_b(self, c):
-        bytes_of(self.rb.at[c], self.sb_r.at[c]).wait()
+    def add_b(self, c, k, at):
+        bytes_of(self.rb.at[c, at], self.sb_r.at[c, at]).wait()
+        self.add(c, k, self.rb[c, at])
 
     def to_a(self, c):
         rt, ro = self.rt, self.roles(c)
         for zz in range(4):
             k = self.slot(ro.ax, ro.ay, zz)
-            self.add(c, k, self.rb[c, zz])
-            remote(self.own(c, k), self.ra(c, zz), self.sa_s.at[c], self.sa_r.at[c], ro.a).start()
+            self.add_b(c, k, zz)
+            remote(self.own(c, k), self.ra(c, zz), self.sa_s.at[c], self.sa_r.at[c, zz], ro.a).start()
         for zz in range(4):
-            self.add(c, self.slot(rt.x, rt.y, zz), self.rb[c, 4 + zz])
+            self.add_b(c, self.slot(rt.x, rt.y, zz), 4 + zz)
 
     def keep_b(self, c):
         rt, ro = self.rt, self.roles(c)
         for zz in range(4):
-            self.add(c, self.slot(ro.ax, ro.ay, zz), self.rb[c, zz])
-            self.add(c, self.slot(rt.x, rt.y, zz), self.rb[c, 4 + zz])
+            self.add_b(c, self.slot(ro.ax, ro.ay, zz), zz)
+        for zz in range(4):
+            self.add_b(c, self.slot(rt.x, rt.y, zz), 4 + zz)
 
     def from_a(self, c):
         rt = self.rt
-        bytes_of(self.rb.at[c, pl.ds(0, 4)], self.sa_r.at[c]).wait()
-        for zz in range(4):
-            self.add(c, self.slot(rt.x, rt.y, zz), self.ra(c, zz)[...])
+        for step in range(4):
+            zz = (rt.z + 1 + step) % 4
+            k = self.slot(rt.x, rt.y, zz)
+            bytes_of(self.ra(c, zz), self.sa_r.at[c, zz]).wait()
+            self.add(c, k, self.ra(c, zz)[...])
+            if step < 3:
+                target = device(rt.x, rt.y, zz, rt.core)
+                remote(self.own(c, k), self.ru(c, 0, step), self.sz_s.at[c, 0, step], self.su_r.at[c, 0, step], target).start()
+
+    def total_line(self, c):
+        rt = self.rt
+        value = self.own(c, self.slot(rt.x, rt.y, rt.z))[...].astype(F32)
+        for step in range(3):
+            bytes_of(self.ru(c, 0, step), self.su_r.at[c, 0, step]).wait()
+            value = value + self.ru(c, 0, step)[...].astype(F32)
+        self.out[c] = value
 
     def along_z(self, c, hop, which):
         rt, ro = self.rt, self.roles(c)
@@ -526,75 +570,64 @@
 
         self.sum_z(c, 1, store)
         k = self.slot(ro.ax, ro.ay, self.rt.z)
-        remote(self.own(c, k), self.ra(c, 0), self.sa_s.at[c], self.sa_r.at[c], ro.a).start()
-
-    def total(self, c, from_a):
+        remote(self.own(c, k), self.ra(c, 0), self.sa_s.at[c], self.sa_r.at[c, 0], ro.a).start()
+
+    def total(self, c):
         def store(k, value):
-            if from_a:
-                bytes_of(self.ra(c, 0), self.sa_r.at[c]).wait()
-                value = value + self.ra(c, 0)[...].astype(F32)
-            self.out[c] = value
+            bytes_of(self.ra(c, 0), self.sa_r.at[c, 0]).wait()
+            self.out[c] = value + self.ra(c, 0)[...].astype(F32)
 
         self.sum_z(c, 0, store)
 
     def stage(self, s, c):
         mixed = self.plan.mixed(c)
-        if s == 0:
-            self.to_b(c)
-        if s == 2:
-            self.from_b(c)
-
-        if s >= 2:
-
-            @when(mixed)
-            def _():
-                if s == 2:
-                    self.keep_b(c)
-                if s <= 5:
-                    self.along_z(c, s - 2, 1)
-                    self.along_z(c, s - 2, 0)
-                if s == 5:
-                    self.close_a(c)
-                if s == 6:
-                    self.total(c, True)
-
-            @when(~mixed)
-            def _():
-                if s == 2:
-                    self.to_a(c)
-                if s == 3:
-                    self.from_a(c)
-                if s >= 3:
-                    self.along_z(c, s - 3, 0)
-                if s == 6:
-                    self.total(c, False)
+
+        @when(mixed)
+        def _():
+            if s == 2:
+                self.keep_b(c)
+            if 2 <= s <= 5:
+                self.along_z(c, s - 2, 1)
+                self.along_z(c, s - 2, 0)
+            if s == 5:
+                self.close_a(c)
+            if s == 6:
+                self.total(c)
+
+        @when(~mixed)
+        def _():
+            if s == 2:
+                self.to_a(c)
+            if s == 3:
+                self.from_a(c)
+            if s == 4:
+                self.total_line(c)
 
     def finish(self, c):
         rt = self.rt
         bytes_of(self.rb.at[c], self.sb_s.at[c]).wait()
 
-        def sent(which):
-            for d in range(4):
-
-                @when(rt.z != d)
-                def _():
-                    bytes_of(self.ra(c, 0), self.sz_s.at[c, which, d]).wait()
-
-        sent(0)
-
         @when(self.plan.mixed(c))
         def _():
-            sent(1)
+            for which in range(2):
+                for d in range(4):
+
+                    @when(rt.z != d)
+                    def _():
+                        bytes_of(self.ra(c, 0), self.sz_s.at[c, which, d]).wait()
+
             bytes_of(self.ra(c, 0), self.sa_s.at[c]).wait()
 
         @when(~self.plan.mixed(c))
         def _():
+            for step in range(3):
+                bytes_of(self.ra(c, 0), self.sz_s.at[c, 0, step]).wait()
             bytes_of(self.rb.at[c, pl.ds(0, 4)], self.sa_s.at[c]).wait()
 
 
 def reducer_sems(count):
     dma = pltpu.SemaphoreType.DMA
-    return [dma((count,))] * 4 + [dma((count, 2, 4)), dma((count, 2, 3)), dma((count, 2, 3))]
+    return [dma((count,)), dma((count, 8)), dma((count,)), dma((count, 4)), dma((count, 2, 4)), dma((count, 2, 3)), dma((count, 2, 3))]
 
 
 class Shared:
@@ -613,7 +646,8 @@
         bytes_of(self.mine, self.send).wait()
 
 
-OFFSETS = (0, 0, 2, 3, 4, 5, 6)
+SMALL_AT = 10
+OFFSETS = (0, 0, 3, 5, 7, 9, 11)
 
 
 def layer_kernel(x_ref, cot_ref, v_ref, len_ref, wq, wk, wv, wo, wu, wd,
@@ -645,21 +679,16 @@
         first = jnp.where(c < 6, c * 512, W_DOWN + (c - 6) * 512)
         return w.at[pl.ds(pl.multiple_of(first + k * ROWS, ROWS), ROWS)]
 
-    def third(c):
-        return c // 3, c % 3
-
     def ra_block(c, i):
-        n, m = third(c)
-        return ra.at[n * 6 + m + i]
-
-    def z_block(ref):
-        def place_of(c, which, d):
-            n, m = third(c)
-            return ref.at[n * 15 + m * 6 + which * 3 + d]
-
-        return place_of
-
-    reduce = Reducer(rt, REDUCE, own_block, rb, ra_block, z_block(ru), z_block(rn), sums, r_sems)
+        return ra.at[4 * c - 3 * REDUCE.mixed_before(c) + i]
+
+    def ru_block(c, which, d):
+        return ru.at[3 * (c + REDUCE.mixed_before(c) + which) + d]
+
+    def rn_block(c, which, d):
+        return rn.at[3 * (2 * REDUCE.mixed_before(c) + which) + d]
+
+    reduce = Reducer(rt, REDUCE, own_block, rb, ra_block, ru_block, rn_block, sums, r_sems)
     reduce_small = Reducer(
         rt, ONE_PIECE, lambda c, k: v_own.at[k], v_rb, lambda c, i: v_ra.at[i],
         lambda c, which, d: v_ru.at[d], lambda c, which, d: v_rn.at[d], v_out, rv_sems,
@@ -953,7 +982,7 @@
         def _():
             compute(t)
 
-        @when(t == PIECES)
+        @when(t == SMALL_AT)
         def _():
             compute_small()
             reduce_small.to_b(0)
@@ -965,9 +994,11 @@
             def _():
                 reduce.stage(s, c)
 
-            @when(c == PIECES)
-            def _():
-                reduce_small.stage(s, 0)
+            if s <= 4:
+
+                @when(c == SMALL_AT)
+                def _():
+                    reduce_small.stage(s, 0)
 
         for k, parts in back_items.items():
 
@@ -978,7 +1009,7 @@
 
         return 0
 
-    lax.fori_loop(0, PIECES + 1 + OFFSETS[-1], reduce_step, 0)
+    lax.fori_loop(0, PIECES + OFFSETS[-1], reduce_step, 0)
 
     def reduced(c, _):
         reduce.finish(c)
@@ -1007,6 +1038,8 @@
     narrow, heads = (128, 1024), (1024, 128)
     half, full = pltpu.VMEM(heads, BF16), pltpu.VMEM(heads, F32)
     pair, wide_pair, tokens_f32 = pltpu.VMEM((256, 1024), BF16), pltpu.VMEM((256, 4096), BF16), pltpu.VMEM(narrow, F32)
+
+    mixed = len(REDUCE.which_mixed)
 
     def blocks(*n):
         return pltpu.VMEM(n + (ROWS, 1024), BF16)
@@ -1028,7 +1061,7 @@
             pltpu.VMEM((2, 1024), F32), pltpu.VMEM((4, 128, 1024), F32), tokens_f32, pltpu.VMEM((128, 1), F32), tokens_f32,
             full, full, pltpu.VMEM((16, 1024), F32), pltpu.VMEM((2, 16, 1024), F32),
             pair, pair, pair, wide_pair, pair, wide_pair, pair, pair, pair, pair,
-            blocks(PIECES, 8), blocks(24), blocks(60), blocks(60),
+            blocks(PIECES, 8), blocks(4 * PIECES - 3 * mixed), blocks(3 * PIECES + 3 * mixed), blocks(6 * mixed),
             tiles(16), tiles(1, 8), tiles(4), tiles(3), tiles(3), tiles(1),
             dma((10,)), dma((3,)), dma((24,)), dma((2, 16)), dma((2,)),
         ] + gather_sems(PIECES) + gather_sems(1) + reducer_sems(PIECES) + reducer_sems(1),

time: 272 us -> 251 us (0.923)
  Pallas kernels: 269 us -> 248 us
    pallas_call x1, Pallas kernels: 266 us -> 244 us  [layer(): pl.pallas_call(layer_kernel, out_shape=(shaped((3 * 1024, 1024), BF16), s...]
where the time goes in v4:
time: 251 us
  Pallas kernels  248 us (99%)
    pallas_call x1, Pallas kernels, layer(): pl.pallas_call(layer_kernel, out_shape=(shaped((3 * 1024, 1024), BF16), s...  244 us

profile of v4, /device:TPU:0, one launch (start us, length us, event | category | flops | bytes accessed | tf_op | source)
XLA Modules:
  0.0 250.6 jit_solution(1935747556600910315)
XLA Ops:
  0.7 0.1 pad.5.clone
  0.8 0.8 stack.35
  1.6 1.3 maximum_maximum_fusion.v_ref
  2.9 244.5 %shard_map.305 = (bf16[3072,1024]{1,0:T(8,128)(2,1)}, bf16[128,1024]{1,0:T(8,128)(2,1)}, f32[128,1024]{1,0:T(8,128)}, f32[12,32,1024]{2,1,0:T(8,128)}, f32[16,256]{1,0:T(8,128)}) custom-call(bf16[128,1024]{1,0:T(8,128)(2,1)} %bitcast.14, bf16[128,1024]{1,0:T(8,128)(2,1)} %bitcast.15, bf16[16,128]{1,0:T(8,128)(2,1)} %maximum_maximum_fusion.v_ref, s32[8]{0:T(128)} %bitcast.16, ...), custom_call_target="tpu_custom_call" | custom-call | tf_op jit(solution)/shard_map/pallas_call | solution.py:1050
  247.4 3.1 %shard_map.306 = (bf16[128,1024]{1,0:T(8,128)(2,1)}, f32[128,1024]{1,0:T(8,128)}, f32[32,1024]{1,0:T(8,128)}, f32[32,1024]{1,0:T(8,128)}, f32[32,1024]{1,0:T(8,1...) custom-call(f32[12,32,1024]{2,1,0:T(8,128)} %get-tuple-element.38.su, ...), custom_call_target="tpu_custom_call" | custom-call | tf_op jit(solution)/shard_map/pallas_call | solution.py:1089
  (2 shorter events, 0.0 us)

commit v5 on v4

--- a/solution.py
+++ b/solution.py
@@ -85,8 +85,14 @@
 
 
 class Plan:
-    def __init__(self, count, mixed, turned):
-        self.count, self.which_mixed, self.which_turned = count, mixed, turned
+    def __init__(self, count, mixed, turned, direct):
+        self.count, self.which_mixed, self.which_turned, self.which_direct = count, mixed, turned, direct
+
+    def direct(self, c):
+        return self.member(c, self.which_direct)
+
+    def chained(self, c):
+        return ~(self.mixed(c) | self.direct(c))
 
     def mixed(self, c):
         return self.member(c, self.which_mixed)
@@ -154,16 +160,15 @@
         rt, ro = self.rt, self.rt.roles(self.plan.turned(c))
         j = owner(rt.x, rt.y, rt.z, rt.core)
         pltpu.make_async_copy(self.own(c), self.block(c, j), self.ls.at[c]).start()
-        mixed = self.plan.mixed(c)
-
-        @when(mixed)
+        direct = self.plan.direct(c)
+
+        @when(direct)
+        def _():
+            self.spread(c, self.own(c), j, rt.z, ro, jnp.bool_(True), 0, (0, ("line",)))
+
+        @when(~direct)
         def _():
             self.spread(c, self.own(c), j, rt.z, ro, jnp.bool_(True), 0, (0, ("up", "down")))
-
-        @when(~mixed)
-        def _():
-            self.spread(c, self.own(c), j, rt.z, ro, jnp.bool_(True), 0, (0, ("line",)))
-
 
     def z_stage(self, c, k):
         rt, ro = self.rt, self.rt.roles(self.plan.turned(c))
@@ -172,13 +177,13 @@
             j = owner(rt.x, rt.y, zz, rt.core)
             bytes_of(self.block(c, j), self.zr.at[c, 0, zz]).wait()
 
-            @when(self.plan.mixed(c))
-            def _():
-                self.spread(c, self.block(c, j), j, zz, ro, None, 0, (0, (direction,)))
-
-            @when(~self.plan.mixed(c))
+            @when(self.plan.direct(c))
             def _():
                 self.spread(c, self.block(c, j), j, zz, ro, jnp.bool_(True), 0, (0, ()))
+
+            @when(~self.plan.direct(c))
+            def _():
+                self.spread(c, self.block(c, j), j, zz, ro, ~self.plan.mixed(c), 0, (0, (direction,)))
 
 
         self.near(k, action)
@@ -215,33 +220,47 @@
         self.near(k, action)
 
     def stage(self, s, c):
-        mixed = self.plan.mixed(c)
+        mixed, direct = self.plan.mixed(c), self.plan.direct(c)
         if s == 0:
             self.own_stage(c)
-        if 1 <= s <= 3:
-            self.z_stage(c, s)
-        if s == 1:
-
-            @when(mixed)
-            def _():
-                self.a_stage(c, 0, ("up", "down"))
-
-            @when(~mixed)
-            def _():
-                self.a_stage(c, 0)
-
-        if 2 <= s <= 4:
-
-            @when(mixed)
-            def _():
-                self.z_stage_of_a(c, s - 1)
-
-            @when(~mixed)
-            def _():
-                self.a_stage(c, s - 1)
-
-        if 3 <= s <= 6:
-            self.b_stage(c, s - 3)
+
+        @when(direct)
+        def _():
+            for k in range(1, 4):
+                if s == 1:
+                    self.z_stage(c, k)
+            for k in range(4):
+                if s == 2:
+                    self.a_stage(c, k)
+                if s == 3:
+                    self.b_stage(c, k)
+
+        @when(~direct)
+        def _():
+            if 1 <= s <= 3:
+                self.z_stage(c, s)
+            if s == 1:
+
+                @when(mixed)
+                def _():
+                    self.a_stage(c, 0, ("up", "down"))
+
+                @when(~mixed)
+                def _():
+                    self.a_stage(c, 0)
+
+            if 2 <= s <= 4:
+
+                @when(mixed)
+                def _():
+                    self.z_stage_of_a(c, s - 1)
+
+                @when(~mixed)
+                def _():
+                    self.a_stage(c, s - 1)
+
+            if 3 <= s <= 6:
+                self.b_stage(c, s - 3)
 
     def arrived(self, c):
         bytes_of(self.span(16), self.dr.at[c]).wait()
@@ -264,15 +283,18 @@
                 def _():
                     bytes_of(self.span(1), self.zs.at[1, c, which, zz]).wait()
 
-        @when(self.plan.mixed(c))
-        def _():
-            sent(0)
-            sent(1)
-
-        @when(~self.plan.mixed(c))
+        @when(self.plan.direct(c))
         def _():
             for slot in range(3):
                 bytes_of(self.span(1), self.zs.at[0, c, 0, slot]).wait()
+
+        @when(~self.plan.direct(c))
+        def _():
+            sent(0)
+
+        @when(self.plan.mixed(c))
+        def _():
+            sent(1)
 
 
 def gather_sems(count):
@@ -425,9 +447,9 @@
 V_QUERY, V_VALUE, V_OUT, V_GAIN1, V_SHIFT1, V_DOWN, V_GAIN2, V_SHIFT2 = range(8)
 V_UP = 8
 W_DOWN, W_UP = 4096, 8192
-GATHER = Plan(PIECES, (1, 3, 4, 6, 8, 10), (4,))
-REDUCE = Plan(PIECES, (1, 3, 6, 9), (6,))
-ONE_PIECE = Plan(1, (), ())
+GATHER = Plan(PIECES, (1, 3, 4, 6, 8, 10), (4,), ())
+REDUCE = Plan(PIECES, (1, 3, 6, 9), (6,), (11,))
+ONE_PIECE = Plan(1, (), (), ())
 
 
 def piece_row(c, j):
@@ -495,6 +517,12 @@
             self.add_b(c, self.slot(rt.x, rt.y, zz), 4 + zz)
 
     def from_a(self, c):
+        rt = self.rt
+        for zz in range(4):
+            bytes_of(self.ra(c, zz), self.sa_r.at[c, zz]).wait()
+            self.add(c, self.slot(rt.x, rt.y, zz), self.ra(c, zz)[...])
+
+    def to_line(self, c):
         rt = self.rt
         for step in range(4):
             zz = (rt.z + 1 + step) % 4
@@ -572,10 +600,12 @@
         k = self.slot(ro.ax, ro.ay, self.rt.z)
         remote(self.own(c, k), self.ra(c, 0), self.sa_s.at[c], self.sa_r.at[c, 0], ro.a).start()
 
-    def total(self, c):
+    def total(self, c, from_a):
         def store(k, value):
-            bytes_of(self.ra(c, 0), self.sa_r.at[c, 0]).wait()
-            self.out[c] = value + self.ra(c, 0)[...].astype(F32)
+            if from_a:
+                bytes_of(self.ra(c, 0), self.sa_r.at[c, 0]).wait()
+                value = value + self.ra(c, 0)[...].astype(F32)
+            self.out[c] = value
 
         self.sum_z(c, 0, store)
 
@@ -592,36 +622,55 @@
             if s == 5:
                 self.close_a(c)
             if s == 6:
-                self.total(c)
-
-        @when(~mixed)
+                self.total(c, True)
+
+        @when(self.plan.direct(c))
+        def _():
+            if s == 2:
+                self.to_a(c)
+            if s == 3:
+                self.to_line(c)
+            if s == 4:
+                self.total_line(c)
+
+        @when(self.plan.chained(c))
         def _():
             if s == 2:
                 self.to_a(c)
             if s == 3:
                 self.from_a(c)
-            if s == 4:
-                self.total_line(c)
+            if s >= 3:
+                self.along_z(c, s - 3, 0)
+            if s == 6:
+                self.total(c, False)
 
     def finish(self, c):
         rt = self.rt
         bytes_of(self.rb.at[c], self.sb_s.at[c]).wait()
 
-        @when(self.plan.mixed(c))
-        def _():
-            for which in range(2):
-                for d in range(4):
-
-                    @when(rt.z != d)
-                    def _():
-                        bytes_of(self.ra(c, 0), self.sz_s.at[c, which, d]).wait()
-
-            bytes_of(self.ra(c, 0), self.sa_s.at[c]).wait()
-
-        @when(~self.plan.mixed(c))
+        def sent(which):
+            for d in range(4):
+
+                @when(rt.z != d)
+                def _():
+                    bytes_of(self.ra(c, 0), self.sz_s.at[c, which, d]).wait()
+
+        @when(self.plan.direct(c))
         def _():
             for step in range(3):
                 bytes_of(self.ra(c, 0), self.sz_s.at[c, 0, step]).wait()
+
+        @when(~self.plan.direct(c))
+        def _():
+            sent(0)
+
+        @when(self.plan.mixed(c))
+        def _():
+            sent(1)
+            bytes_of(self.ra(c, 0), self.sa_s.at[c]).wait()
+
+        @when(~self.plan.mixed(c))
+        def _():
             bytes_of(self.rb.at[c, pl.ds(0, 4)], self.sa_s.at[c]).wait()
 
 
@@ -647,6 +696,7 @@
 
 
 SMALL_AT = 10
+GATHER_OFFSETS = (0, 1, 2, 3, 4, 5, 6, 7)
 OFFSETS = (0, 0, 3, 5, 7, 9, 11)
 
 
@@ -686,7 +736,7 @@
         return ru.at[3 * (c + REDUCE.mixed_before(c) + which) + d]
 
     def rn_block(c, which, d):
-        return rn.at[3 * (2 * REDUCE.mixed_before(c) + which) + d]
+        return rn.at[3 * (c + REDUCE.mixed_before(c) + which) + d]
 
     reduce = Reducer(rt, REDUCE, own_block, rb, ra_block, ru_block, rn_block, sums, r_sems)
     reduce_small = Reducer(
@@ -756,8 +806,8 @@
         gtwo[...] += dense(now, w[W_DOWN + i * 1024:W_DOWN + (i + 1) * 1024])
 
     items = {
-        7: start, 8: lambda: project(1), 9: lambda: project(2), 10: lambda: score(0), 11: lambda: score(2), 13: first_norm,
-        15: lambda: up(0), 16: lambda: up(1), 17: lambda: up(2), 18: lambda: up(3),
+        0: start, 1: lambda: project(1), 2: lambda: project(2), 4: lambda: score(0), 5: lambda: score(2), 7: first_norm,
+        8: lambda: up(0), 9: lambda: up(1), 10: lambda: up(2), 11: lambda: up(3),
     }
 
     def save(i):
@@ -766,7 +816,7 @@
 
     def gather_step(t, _):
         for s in range(Gatherer.stages):
-            c = t - s
+            c = t - GATHER_OFFSETS[s]
 
             @when(c == 0)
             def _():
@@ -776,7 +826,7 @@
             def _():
                 gather.stage(s, c)
 
-        c = t - Gatherer.stages
+        c = t - GATHER_OFFSETS[-1]
 
         @when(c >= 0)
         def _():
@@ -788,13 +838,13 @@
 
         for k, item in items.items():
 
-            @when(t == k)
+            @when(c == k)
             def _():
                 item()
 
         return 0
 
-    lax.fori_loop(0, PIECES + Gatherer.stages, gather_step, 0)
+    lax.fori_loop(0, PIECES + GATHER_OFFSETS[-1], gather_step, 0)
     middle = nor1[...] * vec(V_GAIN1) + vec(V_SHIFT1)
     normed2, inv2 = norm_parts(middle + (gtwo[...] + vec(V_DOWN)))
     g = cot_ref[...].astype(F32)
@@ -838,8 +888,6 @@
 
         for k, at in order:
             block(k)
-            for q in range(4):
-                reduce.send_b(first + q, k, at)
         for k in kept_here:
             block(k)
 
@@ -880,9 +928,7 @@
                 rw.wait()
                 square(left, right[...], c)
 
-        @when(c >= 4)
-        def _():
-            reduce.to_b(c)
+        reduce.to_b(c)
 
     def share_rows():
         return remote(rows2.at[0], rows2.at[1], row_sems.at[0], row_sems.at[1], rt.sibling)
@@ -994,11 +1040,9 @@
             def _():
                 reduce.stage(s, c)
 
-            if s <= 4:
-
-                @when(c == SMALL_AT)
-                def _():
-                    reduce_small.stage(s, 0)
+            @when(c == SMALL_AT)
+            def _():
+                reduce_small.stage(s, 0)
 
         for k, parts in back_items.items():
 
@@ -1061,7 +1105,7 @@
             pltpu.VMEM((2, 1024), F32), pltpu.VMEM((4, 128, 1024), F32), tokens_f32, pltpu.VMEM((128, 1), F32), tokens_f32,
             full, full, pltpu.VMEM((16, 1024), F32), pltpu.VMEM((2, 16, 1024), F32),
             pair, pair, pair, wide_pair, pair, wide_pair, pair, pair, pair, pair,
-            blocks(PIECES, 8), blocks(4 * PIECES - 3 * mixed), blocks(3 * PIECES + 3 * mixed), blocks(6 * mixed),
+            blocks(PIECES, 8), blocks(4 * PIECES - 3 * mixed), blocks(3 * PIECES + 3 * mixed), blocks(3 * PIECES + 3 * mixed),
             tiles(16), tiles(1, 8), tiles(4), tiles(3), tiles(3), tiles(1),
             dma((10,)), dma((3,)), dma((24,)), dma((2, 16)), dma((2,)),
         ] + gather_sems(PIECES) + gather_sems(1) + reducer_sems(PIECES) + reducer_sems(1),

time: 251 us -> 246 us (0.980)
  Pallas kernels: 248 us -> 242 us
    pallas_call x1, Pallas kernels: 244 us -> 239 us  [layer(): pl.pallas_call(layer_kernel, out_shape=(shaped((3 * 1024, 1024), BF16), s...]
where the time goes in v5:
time: 246 us; the launch traced here: 245 us
  Pallas kernels  242 us (98%)
    pallas_call x1, Pallas kernels, layer(): pl.pallas_call(layer_kernel, out_shape=(shaped((3 * 1024, 1024), BF16), s...  239 us

profile of v5, /device:TPU:0, one launch (start us, length us, event | category | flops | bytes accessed | tf_op | source)
XLA Modules:
  0.0 245.5 jit_solution(18131136829414620105)
XLA Ops:
  0.7 0.1 pad.5.clone
  0.8 0.8 stack.35
  1.6 1.3 maximum_maximum_fusion.v_ref
  2.9 239.3 %shard_map.305 = (bf16[3072,1024]{1,0:T(8,128)(2,1)}, bf16[128,1024]{1,0:T(8,128)(2,1)}, f32[128,1024]{1,0:T(8,128)}, f32[12,32,1024]{2,1,0:T(8,128)}, f32[16,256]{1,0:T(8,128)}) custom-call(bf16[128,1024]{1,0:T(8,128)(2,1)} %bitcast.14, bf16[128,1024]{1,0:T(8,128)(2,1)} %bitcast.15, bf16[16,128]{1,0:T(8,128)(2,1)} %maximum_maximum_fusion.v_ref, s32[8]{0:T(128)} %bitcast.16, ...), custom_call_target="tpu_custom_call" | custom-call | tf_op jit(solution)/shard_map/pallas_call | solution.py:1094
  242.2 3.1 %shard_map.306 = (bf16[128,1024]{1,0:T(8,128)(2,1)}, f32[128,1024]{1,0:T(8,128)}, f32[32,1024]{1,0:T(8,128)}, f32[32,1024]{1,0:T(8,128)}, f32[32,1024]{1,0:T(8,1...) custom-call(f32[12,32,1024]{2,1,0:T(8,128)} %get-tuple-element.38.su, ...), custom_call_target="tpu_custom_call" | custom-call | tf_op jit(solution)/shard_map/pallas_call | solution.py:1133
  (2 shorter events, 0.0 us)

commit v6 on v5

--- a/solution.py
+++ b/solution.py
@@ -748,9 +748,9 @@
     )
     sact = [Shared(rt, act2, shared_sems, 8 + i, i * 1024) for i in range(4)]
     sgpre = [Shared(rt, gpre2, shared_sems, 12 + i, i * 1024) for i in range(4)]
+    rt.greet()
     for load in loads:
         load.wait()
-    rt.greet()
 
     def vec(row):
         return table[row:row + 1]

time: 246 us -> 245 us (level)
  no operation moved by 1% of the time
where the time goes in v6:
time: 245 us; the launch traced here: 244 us
  Pallas kernels  241 us (98%)
    pallas_call x1, Pallas kernels, layer(): pl.pallas_call(layer_kernel, out_shape=(shaped((3 * 1024, 1024), BF16), s...  238 us

profile of v6, /device:TPU:0, one launch (start us, length us, event | category | flops | bytes accessed | tf_op | source)
XLA Modules:
  0.0 244.4 jit_solution(1309553820246982987)
XLA Ops:
  0.7 0.1 pad.5.clone
  0.8 0.8 stack.35
  1.6 1.3 maximum_maximum_fusion.v_ref
  2.9 238.3 %shard_map.305 = (bf16[3072,1024]{1,0:T(8,128)(2,1)}, bf16[128,1024]{1,0:T(8,128)(2,1)}, f32[128,1024]{1,0:T(8,128)}, f32[12,32,1024]{2,1,0:T(8,128)}, f32[16,256]{1,0:T(8,128)}) custom-call(bf16[128,1024]{1,0:T(8,128)(2,1)} %bitcast.14, bf16[128,1024]{1,0:T(8,128)(2,1)} %bitcast.15, bf16[16,128]{1,0:T(8,128)(2,1)} %maximum_maximum_fusion.v_ref, s32[8]{0:T(128)} %bitcast.16, ...), custom_call_target="tpu_custom_call" | custom-call | tf_op jit(solution)/shard_map/pallas_call | solution.py:1094
  241.2 3.1 %shard_map.306 = (bf16[128,1024]{1,0:T(8,128)(2,1)}, f32[128,1024]{1,0:T(8,128)}, f32[32,1024]{1,0:T(8,128)}, f32[32,1024]{1,0:T(8,128)}, f32[32,1024]{1,0:T(8,1...) custom-call(f32[12,32,1024]{2,1,0:T(8,128)} %get-tuple-element.38.su, ...), custom_call_target="tpu_custom_call" | custom-call | tf_op jit(solution)/shard_map/pallas_call | solution.py:1133
  (2 shorter events, 0.0 us)
